TPU v7x, 32 devices: a whole 2x2x4 slice. The times are simulated.
32 devices in a mesh: group: 2 (over y), src: 4 (over z), tgt: 2 (over x), prompt: 2 (over core).
Axes of the slice: x: 2, y: 2, z: 4, core: 2. Of those that a mesh axis runs over, the one named last changes fastest.
Arguments:
- decoder: bfloat16 [4, 2, 448, 4608], P('src', 'prompt'), may hold values from -6 to 6
- encoder: bfloat16 [2, 4, 64, 4608], P('prompt', 'src', None, 'tgt'), may hold values from -0.09375 to 0.09375
- activations: bfloat16 [64, 4, 448], P(('group', 'prompt'), 'src'), parts along dimension 0, may hold values from 0.0049743652 to 0.03491211
- prompt_mask: int32 [64, 4, 7], P(('group', 'prompt'), 'src'), parts along dimension 0, may hold values 0 or 1
- counts: int32 [8], P('group'), parts along dimension 0, may hold values from 1 to 6, as said below
Outputs:
- virtual: bfloat16 [8, 2, 4, 64, 448], P(('group', 'src'), 'prompt', None, 'tgt'), parts along dimension 0
- edges: float32 [64, 2, 4, 64], P(('group', 'prompt'), None, 'src', 'tgt'), parts along dimension 0
There are 2 independent parts, one for each index of `group`. A program takes and returns all parts, laid end to end along the dimension named above; an argument that names none is the same for every part. Nothing has to cross between parts.
Inputs may be any that keep to these rules, and one draw needn't show every extreme that they name: counts[l] + counts[l + 2] == 7 for every l < 2.
All inputs are finite; a program needn't handle non-finite values. No bound on the sum of `prompt_mask` on one device may be relied on, other than what follows from the above.
Results may differ from a plain program's by a relative error of at most 0.0029.
Values may be sent and summed in bfloat16 or wider, within the bound.
No kernel may reach another device: no remote copies, remote signals or barrier semaphores. Data moves between devices by JAX's collectives and lax.ppermute only.
A program may use at most 64 MiB of HBM per device.

v0:
```python
import jax
import jax.numpy as jnp
from jax import lax
from jax.sharding import PartitionSpec as P


def per_device(decoder, encoder, activations, prompt_mask, counts):
    layer_index = lax.axis_index("src")
    count_here = counts[layer_index]
    slot_count = prompt_mask.shape[2]
    row_count = decoder.shape[2]
    block_rows = row_count // slot_count
    prompt_rows = activations.shape[0]
    block_ids = jnp.arange(slot_count, dtype=jnp.int32)
    blocks_live = block_ids < count_here
    live_mask = (prompt_mask[:, 0, :] * blocks_live.astype(jnp.int32)).astype(jnp.float32)
    own_weights = (
        activations[:, 0, :].reshape(prompt_rows, slot_count, block_rows).astype(jnp.float32)
        * live_mask[:, :, None]
    ).astype(jnp.bfloat16)
    row_slab = decoder[0, 0]
    weights_slot = own_weights.reshape(prompt_rows, row_count)
    columns = lax.all_gather(encoder, "src", axis=1, tiled=True)
    quarter = lax.all_to_all(columns, "tgt", split_axis=2, concat_axis=3, tiled=True)
    products = jnp.einsum("kwd,rd->kwr", quarter[0], row_slab, preferred_element_type=jnp.float32)
    rounded = products.astype(jnp.bfloat16)
    paired = lax.all_gather(rounded[None], "prompt", axis=0, tiled=True)
    partial_value = jnp.einsum(
        "pr,tkwr->ptkw", weights_slot, paired, preferred_element_type=jnp.float32
    )
    edges_out = lax.psum_scatter(partial_value, "src", scatter_dimension=2, tiled=True)
    live_rows = jnp.repeat(blocks_live, block_rows)
    virtual_out = jnp.where(live_rows[None, None, :], rounded, jnp.zeros_like(rounded))
    return (virtual_out[None, None], edges_out)


def solution(mesh):
    placed = (
        P("src", "prompt", None, None),
        P("prompt", "src", None, "tgt"),
        P(("group", "prompt"), "src", None),
        P(("group", "prompt"), "src", None),
        P("group"),
    )
    return jax.shard_map(
        per_device,
        mesh=mesh,
        in_specs=placed,
        out_specs=(
            P(("group", "src"), "prompt", None, "tgt", None),
            P(("group", "prompt"), None, "src", "tgt"),
        ),
        check_vma=False,
    )
```

profile of v0, /device:TPU:0, one launch (start us, length us, event | category | flops | bytes accessed | tf_op | source)
XLA Modules:
  0.0 99.3 jit_solution(7829507951229298264)
XLA Ops:
  7.2 0.0 all-gather.3.cloned.1.call-start
  7.2 0.7 all-gather.3.cloned.1.call-update
  7.9 34.8 %all-gather.3.cloned.1.call-done = bf16[1,4,64,2304]{3,2,0,1:T(8,128)(2,1)} async-done(((bf16[1,1,64,2304]{3,2,0,1:T(8,128)(2,1)}), bf16[1,4,64,2304]{3,2,0,1:T(8,128)(2,1)}) %all-gather.3.cloned.1.call-update) | async-done | bytes 1179664 | tf_op jit(solution)/shard_map/all_gather | solution.py:23
  42.7 3.2 %copy.14 = bf16[1,4,64,2304]{3,1,0,2:T(4,128)(2,1)} copy(bf16[1,4,64,2304]{3,2,0,1:T(8,128)(2,1)} %all-gather.3.cloned.1.call-done) | data formatting | bytes 2359296 | tf_op jit(solution)/shard_map/all_gather | solution.py:23
  46.0 0.0 copy-start.2
  46.0 0.0 copy-start.1
  46.0 0.0 copy-start.3
  46.0 3.7 %all-to-all-start = ((bf16[1,4,64,2304]{3,1,0,2:T(4,128)(2,1)}), bf16[1,4,64,2304]{3,1,0,2:T(4,128)(2,1)S(1)}, u32[]{:S(2)}, u32[]{:S(2)}) async-start(bf16[1,4,64,2304]{3,1,0,2:T(4,128)(2,1)} %copy.14), calls=%async_computation | async-start | bytes 2359296 | tf_op jit(solution)/shard_map/all_to_all | solution.py:24
  49.7 0.0 copy-done.2
  49.7 0.6 dynamic_slice.3
  50.3 0.6 iota_compare_fusion
  51.0 0.1 broadcast_in_dim.24
  51.0 0.1 broadcast_in_dim.25
  51.1 0.0 copy-done.1
  51.1 0.1 fusion.10
  51.2 0.1 copy.16
  51.3 0.1 mul.25
  51.4 0.1 mul.26
  51.4 0.0 copy-done.3
  51.4 0.6 dynamic-slice
  52.0 12.4 %all-to-all-done = bf16[1,4,64,2304]{3,1,0,2:T(4,128)(2,1)S(1)} async-done(((bf16[1,4,64,2304]{3,1,0,2:T(4,128)(2,1)}), bf16[1,4,64,2304]{3,1,0,2:T(4,128)(2,1)S(1)}, u32[]{:S(2)}, u32[]{:S(2)}) %all-to-all-start) | async-done | bytes 1179680 | tf_op jit(solution)/shard_map/all_to_all | solution.py:24
  64.4 1.2 %copy.24 = bf16[1,4,2,32,2304]{4,2,3,1,0:T(2,128)(2,1)S(1)} copy(bf16[1,4,2,32,2304]{4,1,3,2,0:T(4,128)(2,1)S(1)} %bitcast.38) | data formatting | bytes 2359296 | tf_op jit(solution)/shard_map/all_to_all | solution.py:24
  65.6 0.8 squeeze.13
  66.4 0.0 copy-start
  66.4 3.5 %fusion.2 = bf16[4,32,448]{2,1,0:T(8,128)(2,1)S(1)} fusion(bf16[4,32,4608]{2,1,0:T(8,128)(2,1)S(1)} %squeeze.13, bf16[1,1,448,4608]{3,2,1,0:T(8,128)(2,1)} %param.5), kind=kOutput, calls=%fused_computation.3 | convolution fusion | flops 528539648 | bytes 5423104 | tf_op jit(solution)/shard_map/kwd,rd->kwr/dot_general | solution.py:25
  69.9 2.0 %all-gather = bf16[8,32,448]{2,1,0:T(8,128)(2,1)S(1)} all-gather(bf16[4,32,448]{2,1,0:T(8,128)(2,1)S(1)} %fusion.2), channel_id=2, replica_groups=mesh['group'=2,'src'=4,'tgt'=2,'prompt'=2] {'prompt'}, dimensions={0}, use_global_device_ids=true | all-gather | bytes 344064 | tf_op jit(solution)/shard_map/all_gather | solution.py:27
  71.9 0.7 select_bitcast_fusion
  72.6 0.0 copy-done
  72.6 0.3 fusion.7
  72.9 18.3 %all-reduce = f32[16,2,4,32]{3,0,2,1:T(8,128)S(1)} all-reduce(f32[16,2,4,32]{3,0,2,1:T(8,128)S(1)} %fusion.7), channel_id=3, replica_groups=mesh['group'=2,'src'=4,'tgt'=2,'prompt'=2] {'src'}, use_global_device_ids=true, to_apply=%region_0.0.clone | all-reduce | flops 4096 | bytes 32768
  91.2 0.7 constant_dynamic-slice_fusion
  91.9 0.6 copy.17
Async XLA Ops:
  7.2 35.6 %all-gather.3.cloned.1.call-start = ((), (), s32[]{:S(2)}) async-start(), calls=%async_computation.1 | async-start | bytes 1474560 | tf_op jit(solution)/shard_map/all_gather | solution.py:23
  46.0 3.8 %copy-start.2 = (s32[4]{0:T(128)S(1)}, s32[4]{0:T(128)}, u32[]{:S(2)}) copy-start(s32[4]{0:T(128)} %param.9) | copy-start | bytes 52
  46.0 5.2 %copy-start.1 = (s32[16,1,7]{0,1,2:T(1,128)S(1)}, s32[16,1,7]{0,1,2:T(1,128)}, u32[]{:S(2)}) copy-start(s32[16,1,7]{0,1,2:T(1,128)} %param.8) | copy-start | bytes 1348
  46.0 5.5 %copy-start.3 = (u32[32]{0:T(128)S(1)}, u32[32]{0:T(128)}, u32[]{:S(2)}) copy-start(u32[32]{0:T(128)} %constant.17) | copy-start | bytes 388
  46.0 18.4 %all-to-all-start = ((bf16[1,4,64,2304]{3,1,0,2:T(4,128)(2,1)}), bf16[1,4,64,2304]{3,1,0,2:T(4,128)(2,1)S(1)}, u32[]{:S(2)}, u32[]{:S(2)}) async-start(bf16[1,4,64,2304]{3,1,0,2:T(4,128)(2,1)} %copy.14), calls=%async_computation | async-start | bytes 2359296 | tf_op jit(solution)/shard_map/all_to_all | solution.py:24
  66.4 6.2 %copy-start = (bf16[16,1,448]{2,0,1:T(8,128)(2,1)S(1)}, bf16[16,1,448]{2,0,1:T(8,128)(2,1)}, u32[]{:S(2)}) copy-start(bf16[16,1,448]{2,0,1:T(8,128)(2,1)} %param.7) | copy-start | bytes 43012
Sparse Core Ops, SparseCore 0:
  9.6 33.1 all-gather.2
where the time goes:
time: 99.7 us; the launch traced here: 99.3 us
  waiting for transfers between devices  47.9 us (48%)
  blocking collectives  20.3 us (20%)
  between operations  14.1 us (14%)
  local copies, waits for them, and re-layouts  8.09 us (8%)
  starting transfers between devices  3.77 us (4%)
  matrix products  3.77 us (4%)
  other arithmetic  1.39 us (1%)
    all_gather x1, waiting for transfers between devices, per_device(): columns = lax.all_gather(encoder, 'src', axis=1, tiled=True)  34.8 us
    unnamed x1, blocking collectives  18.3 us
    all_to_all x1, waiting for transfers between devices, per_device(): lax.all_to_all(columns, 'tgt', split_axis=2, concat_axis=3, tiled=True)  12.4 us
    all_to_all x1, starting transfers between devices, per_device(): lax.all_to_all(columns, 'tgt', split_axis=2, concat_axis=3, tiled=True)  3.73 us
    dot_general x1, matrix products, per_device(): jnp.einsum('kwd,rd->kwr', quarter[0], row_slab, preferred_element_type=jn...  3.49 us
    all_gather x1, local copies, waits for them, and re-layouts, per_device(): columns = lax.all_gather(encoder, 'src', axis=1, tiled=True)  3.21 us
    all_gather x1, blocking collectives, per_device(): paired = lax.all_gather(rounded[None], 'prompt', axis=0, tiled=True)  1.99 us
  transfers between devices with their start and end apart: 2, of which 2 were waited for; matrix products, arithmetic and copies ran while one was open for 2% of the time, Pallas kernels for 0%

commit v1 on v0

v1 whole, which is shorter than its diff:
```python
import jax
import jax.numpy as jnp
from jax import lax
from jax.sharding import PartitionSpec as P

AXES = ("group", "src", "tgt")


def own_weights(activations, prompt_mask, blocks_live, rows):
    slots = rows * prompt_mask.shape[2] // activations.shape[2]
    block = activations.shape[2] // prompt_mask.shape[2]
    mask = prompt_mask[:, 0, :slots] * blocks_live[None, :slots].astype(jnp.int32)
    return activations[:, 0, :rows] * jnp.repeat(mask, block, axis=1).astype(activations.dtype)


def any_mesh(decoder, encoder, activations, prompt_mask, counts):
    row_count, slot_count = decoder.shape[2], prompt_mask.shape[2]
    blocks_live = jnp.arange(slot_count, dtype=jnp.int32) < counts[lax.axis_index("src")]
    weights = own_weights(activations, prompt_mask, blocks_live, row_count)
    part = lax.all_to_all(encoder, "tgt", split_axis=2, concat_axis=3, tiled=True)
    blocks = lax.all_gather(part, "src", axis=1, tiled=True)[0]
    products = jnp.einsum("kwd,rd->kwr", blocks, decoder[0, 0], preferred_element_type=jnp.float32)
    virtual = jnp.where(jnp.repeat(blocks_live, row_count // slot_count), products, 0.0).astype(jnp.bfloat16)
    both = lax.all_gather(weights, "prompt", axis=0, tiled=True)
    terms = jnp.einsum("pr,kwr->pkw", both, virtual, preferred_element_type=jnp.float32)
    terms = lax.psum_scatter(terms, "src", scatter_dimension=1, tiled=True)
    edges = lax.all_to_all(terms[:, None], "prompt", split_axis=0, concat_axis=1, tiled=True)
    return virtual[None, None], edges


def square_mesh(decoder, encoder, activations, prompt_mask, counts):
    row_count, slot_count = decoder.shape[2], prompt_mask.shape[2]
    block_rows = row_count // slot_count
    rows = row_count - block_rows
    y, z, x, core = (lax.axis_index(a) for a in ("group", "src", "tgt", "prompt"))
    features, width = encoder.shape[2] // 2, encoder.shape[3]

    def place(y, z, x):
        return (y * 4 + z) * 2 + x

    def swapped(pairs):
        return [(place(y, a, x), place(x, b, y)) for y in range(2) for x in range(2) for a, b in pairs]

    def step(s):
        return [(i, i ^ s) for i in range(4)]

    piece = lax.dynamic_slice_in_dim(encoder[0, 0], y * features, features, axis=0)
    far = lax.ppermute(piece, AXES, swapped(step(2)))
    near = lax.ppermute(piece, AXES, swapped(step(1)))
    own = lax.ppermute(piece, AXES, swapped(step(0)))
    last = lax.ppermute(far, "src", step(1))

    blocks_live = jnp.arange(slot_count, dtype=jnp.int32) < counts[z]
    live = jnp.repeat(blocks_live, block_rows)[:rows]
    mine = own_weights(activations, prompt_mask, blocks_live, rows)
    other = lax.ppermute(mine, "prompt", [(0, 1), (1, 0)])
    weights = jnp.concatenate([mine, other])

    slab = lax.dynamic_slice(decoder[0, 0], (0, y * width), (rows, width))

    def products(blocks):
        return jnp.einsum("kwd,rd->kwr", blocks, slab, preferred_element_type=jnp.float32)

    def finish(part):
        total = part + lax.ppermute(part, "group", [(0, 1), (1, 0)])
        return jnp.where(live, total, 0.0).astype(jnp.bfloat16)

    def terms(virtual):
        return jnp.einsum("pr,kwr->kpw", weights, virtual, preferred_element_type=jnp.float32)

    first = finish(products(jnp.stack([own, near, far])))
    first_terms = terms(first)
    final = finish(products(last[None]))
    final_terms = terms(final)
    total = first_terms[0] + lax.ppermute(first_terms[1], "src", step(1)) + lax.ppermute(first_terms[2], "src", step(2))
    total = total + lax.ppermute(final_terms[0], "src", step(3))
    half = total.shape[0] // 2
    theirs = lax.ppermute(total[half:], "prompt", [(0, 1), (1, 0)])
    keep = total[:half]
    edges = jnp.where(core == 0, jnp.stack([keep, theirs], 1), jnp.stack([theirs, keep], 1))
    held = jnp.concatenate([first, final])
    virtual = jnp.stack([lax.dynamic_index_in_dim(held, jnp.bitwise_xor(z, k), 0, keepdims=False) for k in range(4)])
    virtual = jnp.pad(virtual, ((0, 0), (0, 0), (0, row_count - rows)))
    return virtual[None, None], edges[:, :, None]


def solution(mesh):
    placed = (
        P("src", "prompt", None, None),
        P("prompt", "src", None, "tgt"),
        P(("group", "prompt"), "src", None),
        P(("group", "prompt"), "src", None),
        P("group"),
    )
    square = mesh.shape["group"] == 2 and mesh.shape["tgt"] == 2 and mesh.shape["src"] == 4
    return jax.shard_map(
        square_mesh if square else any_mesh,
        mesh=mesh,
        in_specs=placed,
        out_specs=(
            P(("group", "src"), "prompt", None, "tgt", None),
            P(("group", "prompt"), None, "src", "tgt"),
        ),
        check_vma=False,
    )
```

time: 99.7 us -> 42.3 us (0.42)
  waiting for transfers between devices: 47.9 us -> 10 us
  blocking collectives: 20.3 us -> 0 us
  starting transfers between devices: 3.77 us -> 20.4 us
  between operations: 14.1 us -> 0.76 us
  local copies, waits for them, and re-layouts: 8.09 us -> 3.97 us
    all_gather x1 -> x0, waiting for transfers between devices: 34.8 us -> none  [per_device(): columns = lax.all_gather(encoder, 'src', axis=1, tiled=True)]
    ppermute x0 -> x11, starting transfers between devices: none -> 20.4 us  [the longest x2 7.89 us: finish(): total = part + lax.ppermute(part, 'group', [(0, 1), (1, 0)])]
    unnamed x1 -> x0, blocking collectives: 18.3 us -> none
    all_to_all x1 -> x0, waiting for transfers between devices: 12.4 us -> none  [per_device(): lax.all_to_all(columns, 'tgt', split_axis=2, concat_axis=3, tiled=True)]
    ppermute x0 -> x11, waiting for transfers between devices: none -> 10 us  [the longest x1 4.05 us: square_mesh(): last = lax.ppermute(far, 'src', step(1))]
    all_to_all x1 -> x0, starting transfers between devices: 3.73 us -> none  [per_device(): lax.all_to_all(columns, 'tgt', split_axis=2, concat_axis=3, tiled=True)]
    all_gather x1 -> x0, local copies, waits for them, and re-layouts: 3.21 us -> none  [per_device(): columns = lax.all_gather(encoder, 'src', axis=1, tiled=True)]
    all_gather x1 -> x0, blocking collectives: 1.99 us -> none  [per_device(): paired = lax.all_gather(rounded[None], 'prompt', axis=0, tiled=True)]
  transfers between devices with their start and end apart: 2 -> 11, of which waited for: 2 -> 6; matrix products, arithmetic and copies ran while one was open for 2% -> 17% of each run, Pallas kernels for 0% -> 0%
where the time goes in v1:
time: 42.3 us; the launch traced here: 41.9 us
  starting transfers between devices  20.4 us (48%)
  waiting for transfers between devices  10 us (24%)
  matrix products  4.52 us (11%)
  local copies, waits for them, and re-layouts  3.97 us (9%)
  other arithmetic  2.2 us (5%)
  between operations  0.76 us (2%)
    ppermute x2, starting transfers between devices, finish(): total = part + lax.ppermute(part, 'group', [(0, 1), (1, 0)])  7.89 us
    dot_general x2, matrix products, products(): jnp.einsum('kwd,rd->kwr', blocks, slab, preferred_element_type=jnp.float32)  4.23 us
    ppermute x1, starting transfers between devices, square_mesh(): far = lax.ppermute(piece, AXES, swapped(step(2)))  4.1 us
    ppermute x1, waiting for transfers between devices, square_mesh(): last = lax.ppermute(far, 'src', step(1))  4.05 us
    ppermute x1, waiting for transfers between devices, square_mesh(): total = total + lax.ppermute(final_terms[0], 'src', step(3))  3 us
    ppermute x1, starting transfers between devices, square_mesh(): total = total + lax.ppermute(final_terms[0], 'src', step(3))  2.47 us
    ppermute x1, waiting for transfers between devices, square_mesh(): far = lax.ppermute(piece, AXES, swapped(step(2)))  1.9 us
    ppermute x1, starting transfers between devices, square_mesh(): lax.ppermute(first_terms[2], 'src', step(2))  1.58 us
  transfers between devices with their start and end apart: 11, of which 6 were waited for; matrix products, arithmetic and copies ran while one was open for 17% of the time, Pallas kernels for 0%

profile of v1, /device:TPU:0, one launch (start us, length us, event | category | flops | bytes accessed | tf_op | source)
XLA Modules:
  0.0 41.9 jit_solution(10919718249096470859)
XLA Ops:
  0.6 0.0 copy-start
  0.7 0.9 %copy-done = bf16[1,1,64,2304]{3,2,1,0:T(8,128)(2,1)S(1)} copy-done((bf16[1,1,64,2304]{3,2,1,0:T(8,128)(2,1)S(1)}, bf16[1,1,64,2304]{3,2,1,0:T(8,128)(2,1)}, u32[]{:S(2)}) %copy-start) | copy-done | bytes 294936
  1.6 4.1 %collective-permute-start.2 = (bf16[32,2304]{1,0:T(8,128)(2,1)S(1)}, bf16[32,2304]{1,0:T(8,128)(2,1)S(1)}, u32[]{:S(2)}, u32[]{:S(2)}) collective-permute-start(bf16[32,2304]{1,0:T(8,128)(2,1)S(1)} %dynamic-slice_bitcast_fusion), channel_id=1, source_target_pairs={{0,8},{4,12},{8,0},{12,4},{2,24},{6,28},{10,16},{14,20},{16,10},{2... | collective-permute-start | bytes 442376 | tf_op jit(solution)/shard_map/ppermute | solution.py:48
  5.7 1.6 %collective-permute-start.1 = (bf16[32,2304]{1,0:T(8,128)(2,1)S(1)}, bf16[32,2304]{1,0:T(8,128)(2,1)S(1)}, u32[]{:S(2)}, u32[]{:S(2)}) collective-permute-start(bf16[32,2304]{1,0:T(8,128)(2,1)S(1)} %dynamic-slice_bitcast_fusion), channel_id=1, source_target_pairs={{0,4},{4,0},{8,12},{12,8},{2,20},{6,16},{10,28},{14,24},{16,6},{20... | collective-permute-start | bytes 442376 | tf_op jit(solution)/shard_map/ppermute | solution.py:49
  7.3 0.7 %collective-permute-start = (bf16[32,2304]{1,0:T(8,128)(2,1)S(1)}, bf16[32,2304]{1,0:T(8,128)(2,1)S(1)}, u32[]{:S(2)}, u32[]{:S(2)}) collective-permute-start(bf16[32,2304]{1,0:T(8,128)(2,1)S(1)} %dynamic-slice_bitcast_fusion), channel_id=1, source_target_pairs={{0,0},{4,4},{8,8},{12,12},{2,16},{6,20},{10,24},{14,28},{16,2},{20... | collective-permute-start | bytes 442376 | tf_op jit(solution)/shard_map/ppermute | solution.py:50
  8.0 1.2 %dynamic_slice.26 = s32[1]{0:T(128)} dynamic-slice(s32[4]{0:T(128)} %param.9, s32[]{:T(128)S(6)} %select_n.43), dynamic_slice_sizes={1} | dynamic-slice | bytes 12 | tf_op jit(solution)/shard_map/dynamic_slice | solution.py:53
  9.2 0.6 %iota_compare_fusion.1 = pred[7]{0:T(512)(128)(4,1)S(1)} fusion(s32[]{:T(128)} %bitcast), kind=kLoop, calls=%fused_computation.55 | loop fusion | flops 7 | bytes 11 | tf_op jit(solution)/shard_map/lt | solution.py:53
  9.9 0.7 %slice.32 = s32[16,1,6]{0,1,2:T(1,128)S(1)} slice(s32[16,1,7]{0,1,2:T(1,128)} %param.8), slice={[0:16], [0:1], [0:6]} | slice | bytes 768 | tf_op jit(solution)/shard_map/slice | solution.py:12
  10.6 0.1 fusion.32
  10.6 0.1 copy.12
  10.7 0.1 broadcast_in_dim.34
  10.8 0.1 convert_element_type.23
  10.9 1.9 %collective-permute-done.2 = bf16[32,2304]{1,0:T(8,128)(2,1)S(1)} collective-permute-done((bf16[32,2304]{1,0:T(8,128)(2,1)S(1)}, bf16[32,2304]{1,0:T(8,128)(2,1)S(1)}, u32[]{:S(2)}, u32[]{:S(2)}) %collective-permute-start.2) | collective-permute-done | bytes 147488 | tf_op jit(solution)/shard_map/ppermute | solution.py:48
  12.8 0.2 collective-permute-done.1
  13.0 0.0 collective-permute-done
  13.0 2.1 %fusion = f32[3,32,384]{2,1,0:T(8,128)S(1)} fusion(bf16[1,1,448,4608]{3,2,1,0:T(8,128)(2,1)} %param.5, s32[]{:T(128)S(6)} %select_n.45, bf16[1,32,2304]{2,1,0:T(8,128)(2,1)S(1)} %bitcast.59, bf16[1,32,2304]{2,1,0:T(8,128)(2,1)S(1)} %bitcast.60, bf16[1,32,2304]{2,1,0:T(8,128)(2,1)S(1)} %bitcast.61), kind=kOutput, calls=%fused_computation | convolution fusion | flops 170311680 | bytes 2359300 | tf_op jit(solution)/shard_map/kwd,rd->kwr/dot_general | solution.py:62
  15.2 7.5 %collective-permute-start.3 = (f32[3,32,384]{2,1,0:T(8,128)S(1)}, f32[3,32,384]{2,1,0:T(8,128)S(1)}, u32[]{:S(2)}, u32[]{:S(2)}) collective-permute-start(f32[3,32,384]{2,1,0:T(8,128)S(1)} %fusion), channel_id=1, source_target_pairs={{0,16},{16,0},{1,17},{17,1},{2,18},{18,2},{3,19},{19,3},{4,20},{20... | collective-permute-start | bytes 442376 | tf_op jit(solution)/shard_map/ppermute | solution.py:65
  22.6 0.6 %collective-permute-start.4 = (bf16[32,2304]{1,0:T(8,128)(2,1)S(1)}, bf16[32,2304]{1,0:T(8,128)(2,1)S(1)}, u32[]{:S(2)}, u32[]{:S(2)}) collective-permute-start(bf16[32,2304]{1,0:T(8,128)(2,1)S(1)} %collective-permute-done.2), channel_id=1, source_target_pairs={{0,4},{4,0},{8,12},{12,8},{1,5},{5,1},{9,13},{13,9},{2,6},{6,2},{1... | collective-permute-start | bytes 442376 | tf_op jit(solution)/shard_map/ppermute | solution.py:51
  23.2 0.7 %bitcast_multiply_fusion = bf16[16,384]{1,0:T(8,128)(2,1)S(1)} fusion(bf16[16,384]{1,0:T(8,128)(2,1)S(1)} %convert_element_type.23, bf16[16,1,448]{2,0,1:T(8,128)(2,1)} %param.7), kind=kLoop, calls=%fused_computation.48 | loop fusion | flops 6144 | bytes 36864 | tf_op jit(solution)/shard_map/mul | solution.py:13
  23.9 0.0 collective-permute-start.6
  23.9 0.1 broadcast_in_dim.28
  24.0 0.1 slice.30
  24.1 4.0 %collective-permute-done.4 = bf16[32,2304]{1,0:T(8,128)(2,1)S(1)} collective-permute-done((bf16[32,2304]{1,0:T(8,128)(2,1)S(1)}, bf16[32,2304]{1,0:T(8,128)(2,1)S(1)}, u32[]{:S(2)}, u32[]{:S(2)}) %collective-permute-start.4) | collective-permute-done | bytes 147488 | tf_op jit(solution)/shard_map/ppermute | solution.py:51
  28.1 2.1 %fusion.6 = f32[1,32,384]{2,1,0:T(8,128)S(1)} fusion(bf16[32,2304]{1,0:T(8,128)(2,1)S(1)} %collective-permute-done.4, bf16[1,1,448,4608]{3,2,1,0:T(8,128)(2,1)} %param.5, s32[]{:T(128)S(6)} %select_n.45), kind=kOutput, calls=%fused_computation.6 | convolution fusion | flops 56623104 | bytes 1966084 | tf_op jit(solution)/shard_map/kwd,rd->kwr/dot_general | solution.py:62
  30.2 0.4 %collective-permute-start.5 = (f32[1,32,384]{2,1,0:T(8,128)S(1)}, f32[1,32,384]{2,1,0:T(8,128)S(1)}, u32[]{:S(2)}, u32[]{:S(2)}) collective-permute-start(f32[1,32,384]{2,1,0:T(8,128)S(1)} %fusion.6), channel_id=1, source_target_pairs={{0,16},{16,0},{1,17},{17,1},{2,18},{18,2},{3,19},{19,3},{4,20},{20... | collective-permute-start | bytes 147464 | tf_op jit(solution)/shard_map/ppermute | solution.py:65
  30.6 0.0 collective-permute-done.3
  30.7 0.0 collective-permute-done.6
  30.7 0.2 convolution_bitcast_fusion
  30.9 1.6 %collective-permute-start.8 = (f32[32,32]{1,0:T(8,128)S(1)}, f32[32,32]{1,0:T(8,128)S(1)}, u32[]{:S(2)}, u32[]{:S(2)}) collective-permute-start(f32[32,32]{1,0:T(8,128)S(1)} %get-tuple-element.11), channel_id=1, source_target_pairs={{0,8},{4,12},{8,0},{12,4},{1,9},{5,13},{9,1},{13,5},{2,10},{6,14},... | collective-permute-start | bytes 12296 | tf_op jit(solution)/shard_map/ppermute | solution.py:75
  32.4 1.5 %collective-permute-start.7 = (f32[32,32]{1,0:T(8,128)S(1)}, f32[32,32]{1,0:T(8,128)S(1)}, u32[]{:S(2)}, u32[]{:S(2)}) collective-permute-start(f32[32,32]{1,0:T(8,128)S(1)} %get-tuple-element.10), channel_id=1, source_target_pairs={{0,4},{4,0},{8,12},{12,8},{1,5},{5,1},{9,13},{13,9},{2,6},{6,2},{1... | collective-permute-start | bytes 12296 | tf_op jit(solution)/shard_map/ppermute | solution.py:75
  34.0 0.4 collective-permute-done.5
  34.4 0.1 convolution_bitcast_fusion.1
  34.5 2.5 %collective-permute-start.9 = (f32[32,32]{1,0:T(8,128)S(1)}, f32[32,32]{1,0:T(8,128)S(1)}, u32[]{:S(2)}, u32[]{:S(2)}) collective-permute-start(f32[32,32]{1,0:T(8,128)S(1)} %convolution_bitcast_fusion.1), channel_id=1, source_target_pairs={{0,12},{4,8},{8,4},{12,0},{1,13},{5,9},{9,5},{13,1},{2,14},{6,10},... | collective-permute-start | bytes 12296 | tf_op jit(solution)/shard_map/ppermute | solution.py:76
  37.0 0.1 fusion.23
  37.0 0.0 collective-permute-done.8
  37.0 0.0 collective-permute-done.7
  37.1 3.0 %collective-permute-done.9 = f32[32,32]{1,0:T(8,128)S(1)} collective-permute-done((f32[32,32]{1,0:T(8,128)S(1)}, f32[32,32]{1,0:T(8,128)S(1)}, u32[]{:S(2)}, u32[]{:S(2)}) %collective-permute-start.9) | collective-permute-done | bytes 4128 | tf_op jit(solution)/shard_map/ppermute | solution.py:76
  40.1 0.1 collective-permute-start.10
  40.1 0.7 %fusion.21 = bf16[1,1,4,32,448]{4,3,2,1,0:T(8,128)(2,1)} fusion(bf16[1,32,384]{2,1,0:T(8,128)(2,1)S(1)} %get-tuple-element.9, bf16[1,32,384]{2,1,0:T(8,128)(2,1)S(1)} %get-tuple-element.8, bf16[1,32,384]{2,1,0:T(8,128)(2,1)S(1)} %get-tuple-element.7, bf16[1,32,384]{2,1,0:T(8,128)(2,1)S(1)} %get-tuple-element.6), kind=kLoop, calls=%fused_computation.28 | loop fusion | flops 745472 | bytes 212992 | tf_op jit(solution)/shard_map/broadcast_in_dim | solution.py:84
  40.8 0.5 %collective-permute-done.10 = f32[16,32]{1,0:T(8,128)S(1)} collective-permute-done((f32[16,32]{1,0:T(8,128)S(1)}, f32[16,32]{1,0:T(8,128)S(1)}, u32[]{:S(2)}, u32[]{:S(2)}) %collective-permute-start.10) | collective-permute-done | bytes 2080 | tf_op jit(solution)/shard_map/ppermute | solution.py:78
  41.3 0.6 %copy.14 = f32[16,2,1,32]{3,2,1,0:T(1,128)} copy(f32[16,2,1,32]{3,0,2,1:T(8,128)S(1)} %maximum_select_fusion) | data formatting | bytes 8192
  (8 shorter events, 0.1 us)
Async XLA Ops:
  0.6 1.0 %copy-start = (bf16[1,1,64,2304]{3,2,1,0:T(8,128)(2,1)S(1)}, bf16[1,1,64,2304]{3,2,1,0:T(8,128)(2,1)}, u32[]{:S(2)}) copy-start(bf16[1,1,64,2304]{3,2,1,0:T(8,128)(2,1)} %param.6) | copy-start | bytes 884740
  1.6 11.2 %collective-permute-start.2 = (bf16[32,2304]{1,0:T(8,128)(2,1)S(1)}, bf16[32,2304]{1,0:T(8,128)(2,1)S(1)}, u32[]{:S(2)}, u32[]{:S(2)}) collective-permute-start(bf16[32,2304]{1,0:T(8,128)(2,1)S(1)} %dynamic-slice_bitcast_fusion), channel_id=1, source_target_pairs={{0,8},{4,12},{8,0},{12,4},{2,24},{6,28},{10,16},{14,20},{16,10},{2... | collective-permute-start | bytes 442376 | tf_op jit(solution)/shard_map/ppermute | solution.py:48
  5.7 7.3 %collective-permute-start.1 = (bf16[32,2304]{1,0:T(8,128)(2,1)S(1)}, bf16[32,2304]{1,0:T(8,128)(2,1)S(1)}, u32[]{:S(2)}, u32[]{:S(2)}) collective-permute-start(bf16[32,2304]{1,0:T(8,128)(2,1)S(1)} %dynamic-slice_bitcast_fusion), channel_id=1, source_target_pairs={{0,4},{4,0},{8,12},{12,8},{2,20},{6,16},{10,28},{14,24},{16,6},{20... | collective-permute-start | bytes 442376 | tf_op jit(solution)/shard_map/ppermute | solution.py:49
  7.3 5.7 %collective-permute-start = (bf16[32,2304]{1,0:T(8,128)(2,1)S(1)}, bf16[32,2304]{1,0:T(8,128)(2,1)S(1)}, u32[]{:S(2)}, u32[]{:S(2)}) collective-permute-start(bf16[32,2304]{1,0:T(8,128)(2,1)S(1)} %dynamic-slice_bitcast_fusion), channel_id=1, source_target_pairs={{0,0},{4,4},{8,8},{12,12},{2,16},{6,20},{10,24},{14,28},{16,2},{20... | collective-permute-start | bytes 442376 | tf_op jit(solution)/shard_map/ppermute | solution.py:50
  15.2 15.5 %collective-permute-start.3 = (f32[3,32,384]{2,1,0:T(8,128)S(1)}, f32[3,32,384]{2,1,0:T(8,128)S(1)}, u32[]{:S(2)}, u32[]{:S(2)}) collective-permute-start(f32[3,32,384]{2,1,0:T(8,128)S(1)} %fusion), channel_id=1, source_target_pairs={{0,16},{16,0},{1,17},{17,1},{2,18},{18,2},{3,19},{19,3},{4,20},{20... | collective-permute-start | bytes 442376 | tf_op jit(solution)/shard_map/ppermute | solution.py:65
  22.6 5.5 %collective-permute-start.4 = (bf16[32,2304]{1,0:T(8,128)(2,1)S(1)}, bf16[32,2304]{1,0:T(8,128)(2,1)S(1)}, u32[]{:S(2)}, u32[]{:S(2)}) collective-permute-start(bf16[32,2304]{1,0:T(8,128)(2,1)S(1)} %collective-permute-done.2), channel_id=1, source_target_pairs={{0,4},{4,0},{8,12},{12,8},{1,5},{5,1},{9,13},{13,9},{2,6},{6,2},{1... | collective-permute-start | bytes 442376 | tf_op jit(solution)/shard_map/ppermute | solution.py:51
  23.9 6.8 %collective-permute-start.6 = (bf16[16,384]{1,0:T(8,128)(2,1)S(1)}, bf16[16,384]{1,0:T(8,128)(2,1)S(1)}, u32[]{:S(2)}, u32[]{:S(2)}) collective-permute-start(bf16[16,384]{1,0:T(8,128)(2,1)S(1)} %bitcast_multiply_fusion), channel_id=1, source_target_pairs={{0,1},{1,0},{2,3},{3,2},{4,5},{5,4},{6,7},{7,6},{8,9},{9,8},{10,11... | collective-permute-start | bytes 36872 | tf_op jit(solution)/shard_map/ppermute | solution.py:56
  30.2 4.2 %collective-permute-start.5 = (f32[1,32,384]{2,1,0:T(8,128)S(1)}, f32[1,32,384]{2,1,0:T(8,128)S(1)}, u32[]{:S(2)}, u32[]{:S(2)}) collective-permute-start(f32[1,32,384]{2,1,0:T(8,128)S(1)} %fusion.6), channel_id=1, source_target_pairs={{0,16},{16,0},{1,17},{17,1},{2,18},{18,2},{3,19},{19,3},{4,20},{20... | collective-permute-start | bytes 147464 | tf_op jit(solution)/shard_map/ppermute | solution.py:65
  30.9 6.2 %collective-permute-start.8 = (f32[32,32]{1,0:T(8,128)S(1)}, f32[32,32]{1,0:T(8,128)S(1)}, u32[]{:S(2)}, u32[]{:S(2)}) collective-permute-start(f32[32,32]{1,0:T(8,128)S(1)} %get-tuple-element.11), channel_id=1, source_target_pairs={{0,8},{4,12},{8,0},{12,4},{1,9},{5,13},{9,1},{13,5},{2,10},{6,14},... | collective-permute-start | bytes 12296 | tf_op jit(solution)/shard_map/ppermute | solution.py:75
  32.4 4.6 %collective-permute-start.7 = (f32[32,32]{1,0:T(8,128)S(1)}, f32[32,32]{1,0:T(8,128)S(1)}, u32[]{:S(2)}, u32[]{:S(2)}) collective-permute-start(f32[32,32]{1,0:T(8,128)S(1)} %get-tuple-element.10), channel_id=1, source_target_pairs={{0,4},{4,0},{8,12},{12,8},{1,5},{5,1},{9,13},{13,9},{2,6},{6,2},{1... | collective-permute-start | bytes 12296 | tf_op jit(solution)/shard_map/ppermute | solution.py:75
  34.5 5.5 %collective-permute-start.9 = (f32[32,32]{1,0:T(8,128)S(1)}, f32[32,32]{1,0:T(8,128)S(1)}, u32[]{:S(2)}, u32[]{:S(2)}) collective-permute-start(f32[32,32]{1,0:T(8,128)S(1)} %convolution_bitcast_fusion.1), channel_id=1, source_target_pairs={{0,12},{4,8},{8,4},{12,0},{1,13},{5,9},{9,5},{13,1},{2,14},{6,10},... | collective-permute-start | bytes 12296 | tf_op jit(solution)/shard_map/ppermute | solution.py:76
  40.1 1.2 %collective-permute-start.10 = (f32[16,32]{1,0:T(8,128)S(1)}, f32[16,32]{1,0:T(8,128)S(1)}, u32[]{:S(2)}, u32[]{:S(2)}) collective-permute-start(f32[16,32]{1,0:T(8,128)S(1)} %get-tuple-element.13), channel_id=1, source_target_pairs={{0,1},{1,0},{2,3},{3,2},{4,5},{5,4},{6,7},{7,6},{8,9},{9,8},{10,11... | collective-permute-start | bytes 6152 | tf_op jit(solution)/shard_map/ppermute | solution.py:78

commit v2 on v1

--- a/solution.py
+++ b/solution.py
@@ -1,6 +1,8 @@
 import jax
 import jax.numpy as jnp
 from jax import lax
+from jax.experimental import pallas as pl
+from jax.experimental.pallas import tpu as pltpu
 from jax.sharding import PartitionSpec as P
 
 AXES = ("group", "src", "tgt")
@@ -11,6 +13,31 @@
     block = activations.shape[2] // prompt_mask.shape[2]
     mask = prompt_mask[:, 0, :slots] * blocks_live[None, :slots].astype(jnp.int32)
     return activations[:, 0, :rows] * jnp.repeat(mask, block, axis=1).astype(activations.dtype)
+
+
+def mask_kernel(counts_ref, activations_ref, mask_ref, weights_ref, live_ref):
+    slots, rows = mask_ref.shape[0], weights_ref.shape[1]
+    block = activations_ref.shape[1] // slots
+    row_slot = lax.broadcasted_iota(jnp.int32, (slots, rows), 1) // block
+    in_slot = row_slot == lax.broadcasted_iota(jnp.int32, (slots, rows), 0)
+    spread = jnp.where(in_slot & (row_slot < counts_ref[lax.axis_index("src")]), 1.0, 0.0)
+    mask = mask_ref[...].reshape(slots, mask_ref.shape[2]).astype(jnp.float32)
+    spread_mask = lax.dot_general(mask, spread, (((0,), (0,)), ((), ())), preferred_element_type=jnp.float32)
+    weights_ref[...] = (activations_ref[:, :rows].astype(jnp.float32) * spread_mask).astype(weights_ref.dtype)
+    live_ref[...] = jnp.broadcast_to(jnp.sum(spread, axis=0, keepdims=True), live_ref.shape)
+
+
+def masked(counts, activations, prompt_mask, rows):
+    whole = pl.BlockSpec(memory_space=pltpu.VMEM)
+    return pl.pallas_call(
+        mask_kernel,
+        out_shape=(
+            jax.ShapeDtypeStruct((activations.shape[0], rows), activations.dtype),
+            jax.ShapeDtypeStruct((8, rows), jnp.float32),
+        ),
+        in_specs=[pl.BlockSpec(memory_space=pltpu.SMEM), whole, whole],
+        out_specs=(whole, whole),
+    )(counts, activations[:, 0], jnp.transpose(prompt_mask, (2, 1, 0)))
 
 
 def any_mesh(decoder, encoder, activations, prompt_mask, counts):
@@ -44,26 +71,24 @@
     def step(s):
         return [(i, i ^ s) for i in range(4)]
 
-    piece = lax.dynamic_slice_in_dim(encoder[0, 0], y * features, features, axis=0)
+    swap = [(0, 1), (1, 0)]
+    piece = lax.optimization_barrier(lax.dynamic_slice_in_dim(encoder[0, 0], y * features, features, axis=0))
+    beside = lax.dynamic_slice_in_dim(encoder[0, 0], (1 - y) * features, features, axis=0)
     far = lax.ppermute(piece, AXES, swapped(step(2)))
     near = lax.ppermute(piece, AXES, swapped(step(1)))
-    own = lax.ppermute(piece, AXES, swapped(step(0)))
+    given = lax.ppermute(beside, ("group", "tgt"), [(0, 1), (3, 2)])
     last = lax.ppermute(far, "src", step(1))
-
-    blocks_live = jnp.arange(slot_count, dtype=jnp.int32) < counts[z]
-    live = jnp.repeat(blocks_live, block_rows)[:rows]
-    mine = own_weights(activations, prompt_mask, blocks_live, rows)
-    other = lax.ppermute(mine, "prompt", [(0, 1), (1, 0)])
-    weights = jnp.concatenate([mine, other])
-
-    slab = lax.dynamic_slice(decoder[0, 0], (0, y * width), (rows, width))
+    own = jnp.where(x == y, piece, given)
+    slab = lax.optimization_barrier(lax.dynamic_slice(decoder[0, 0], (0, y * width), (rows, width)))
+    mine, live = masked(counts, activations, prompt_mask, rows)
+    weights = jnp.concatenate([mine, lax.ppermute(mine, "prompt", swap)])
 
     def products(blocks):
         return jnp.einsum("kwd,rd->kwr", blocks, slab, preferred_element_type=jnp.float32)
 
     def finish(part):
-        total = part + lax.ppermute(part, "group", [(0, 1), (1, 0)])
-        return jnp.where(live, total, 0.0).astype(jnp.bfloat16)
+        total = part + lax.ppermute(part, "group", swap)
+        return jnp.where(live[0] > 0, total, 0.0).astype(jnp.bfloat16)
 
     def terms(virtual):
         return jnp.einsum("pr,kwr->kpw", weights, virtual, preferred_element_type=jnp.float32)
@@ -75,7 +100,7 @@
     total = first_terms[0] + lax.ppermute(first_terms[1], "src", step(1)) + lax.ppermute(first_terms[2], "src", step(2))
     total = total + lax.ppermute(final_terms[0], "src", step(3))
     half = total.shape[0] // 2
-    theirs = lax.ppermute(total[half:], "prompt", [(0, 1), (1, 0)])
+    theirs = lax.ppermute(total[half:], "prompt", swap)
     keep = total[:half]
     edges = jnp.where(core == 0, jnp.stack([keep, theirs], 1), jnp.stack([theirs, keep], 1))
     held = jnp.concatenate([first, final])

time: 42.3 us -> 35.1 us (0.83)
  matrix products: 4.52 us -> 1.57 us
  starting transfers between devices: 20.4 us -> 18.2 us
  waiting for transfers between devices: 10 us -> 7.96 us
  Pallas kernels: 0 us -> 1.52 us
  local copies, waits for them, and re-layouts: 3.97 us -> 3.26 us
  other arithmetic: 2.2 us -> 1.51 us
    dot_general x2, matrix products: 4.23 us -> 1.28 us  [products(): jnp.einsum('kwd,rd->kwr', blocks, slab, preferred_element_type=jnp.float32)]
    ppermute x1, waiting for transfers between devices: 4.05 us -> 1.43 us  [square_mesh(): last = lax.ppermute(far, 'src', step(1))]
    ppermute x5, waiting for transfers between devices: 0.91 us -> 3.25 us  [the longest x2 1.94 us: finish(): total = part + lax.ppermute(part, 'group', swap)]
    ppermute x1, waiting for transfers between devices: 1.9 us -> 0.01 us  [square_mesh(): far = lax.ppermute(piece, AXES, swapped(step(2)))]
    pallas_call x0 -> x1, Pallas kernels: none -> 1.52 us  [masked(): pl.pallas_call(mask_kernel, out_shape=(jax.ShapeDtypeStruct((activations....]
    dynamic_slice x2, local copies, waits for them, and re-layouts: 1.25 us -> 2.61 us  [the longest x1 1.6 us: square_mesh(): lax.dynamic_slice(decoder[0, 0], (0, y * width), (rows, width))]
    ppermute x1, starting transfers between devices: 1.51 us -> 0.52 us  [square_mesh(): lax.ppermute(first_terms[1], 'src', step(1))]
    unnamed x3 -> x4, local copies, waits for them, and re-layouts: 1.58 us -> 0.63 us
  transfers between devices with their start and end apart: 11 -> 11, of which waited for: 6 -> 7; matrix products, arithmetic and copies ran while one was open for 17% -> 13% of each run, Pallas kernels for 0% -> 4%
where the time goes in v2:
time: 35.1 us; the launch traced here: 34.9 us
  starting transfers between devices  18.2 us (52%)
  waiting for transfers between devices  7.96 us (23%)
  local copies, waits for them, and re-layouts  3.26 us (9%)
  matrix products  1.57 us (4%)
  Pallas kernels  1.52 us (4%)
  other arithmetic  1.51 us (4%)
  between operations  0.8 us (2%)
    ppermute x1, starting transfers between devices, square_mesh(): given = lax.ppermute(beside, ('group', 'tgt'), [(0, 1), (3, 2)])  5.19 us
    ppermute x1, starting transfers between devices, square_mesh(): far = lax.ppermute(piece, AXES, swapped(step(2)))  4.1 us
    ppermute x1, waiting for transfers between devices, square_mesh(): total = total + lax.ppermute(final_terms[0], 'src', step(3))  2.77 us
    ppermute x2, starting transfers between devices, finish(): total = part + lax.ppermute(part, 'group', swap)  2.65 us
    ppermute x1, starting transfers between devices, square_mesh(): total = total + lax.ppermute(final_terms[0], 'src', step(3))  2.21 us
    ppermute x2, waiting for transfers between devices, finish(): total = part + lax.ppermute(part, 'group', swap)  1.94 us
    dynamic_slice x1, local copies, waits for them, and re-layouts, square_mesh(): lax.dynamic_slice(decoder[0, 0], (0, y * width), (rows, width))  1.6 us
    ppermute x1, starting transfers between devices, square_mesh(): near = lax.ppermute(piece, AXES, swapped(step(1)))  1.58 us
  transfers between devices with their start and end apart: 11, of which 7 were waited for; matrix products, arithmetic and copies ran while one was open for 13% of the time, Pallas kernels for 4%

profile of v2, /device:TPU:0, one launch (start us, length us, event | category | flops | bytes accessed | tf_op | source)
XLA Modules:
  0.0 34.9 jit_solution(250646986164372011)
XLA Ops:
  0.6 1.0 %dynamic-slice_bitcast_fusion.1 = (bf16[32,2304]{1,0:T(8,128)(2,1)S(1)}, bf16[32,2304]{1,0:T(8,128)(2,1)S(1)}) fusion(bf16[1,1,64,2304]{3,2,1,0:T(8,128)(2,1)} %param.6, s32[]{:T(128)S(6)} %select_n.55, s32[]{:T(128)S(6)} %select_n.54), kind=kLoop, calls=%fused_computation.22 | loop fusion | bytes 589832 | tf_op jit(solution)/shard_map/dynamic_slice | solution.py:76
  1.6 4.1 %collective-permute-start.2 = (bf16[32,2304]{1,0:T(8,128)(2,1)S(1)}, bf16[32,2304]{1,0:T(8,128)(2,1)S(1)}, u32[]{:S(2)}, u32[]{:S(2)}) collective-permute-start(bf16[32,2304]{1,0:T(8,128)(2,1)S(1)} %get-tuple-element.9), channel_id=1, source_target_pairs={{0,8},{4,12},{8,0},{12,4},{2,24},{6,28},{10,16},{14,20},{16,10},{2... | collective-permute-start | bytes 442376 | tf_op jit(solution)/shard_map/ppermute | solution.py:77
  5.7 1.6 %collective-permute-start.1 = (bf16[32,2304]{1,0:T(8,128)(2,1)S(1)}, bf16[32,2304]{1,0:T(8,128)(2,1)S(1)}, u32[]{:S(2)}, u32[]{:S(2)}) collective-permute-start(bf16[32,2304]{1,0:T(8,128)(2,1)S(1)} %get-tuple-element.9), channel_id=1, source_target_pairs={{0,4},{4,0},{8,12},{12,8},{2,20},{6,16},{10,28},{14,24},{16,6},{20... | collective-permute-start | bytes 442376 | tf_op jit(solution)/shard_map/ppermute | solution.py:78
  7.3 1.5 %shard_map.68 = (bf16[16,384]{1,0:T(8,128)(2,1)}, f32[8,384]{1,0:T(8,128)}) custom-call(s32[4]{0:T(128)} %counts_ref.1, bf16[16,448]{1,0:T(8,128)(2,1)} %bitcast.52, s32[7,1,16]{2,1,0:T(1,128)} %bitcast.54), custom_call_target="tpu_custom_call" | custom-call | tf_op jit(solution)/shard_map/pallas_call | solution.py:32
  8.8 0.0 collective-permute-start.6
  8.9 5.2 %collective-permute-start = (bf16[32,2304]{1,0:T(8,128)(2,1)S(1)}, bf16[32,2304]{1,0:T(8,128)(2,1)S(1)}, u32[]{:S(2)}, u32[]{:S(2)}) collective-permute-start(bf16[32,2304]{1,0:T(8,128)(2,1)S(1)} %get-tuple-element.8), channel_id=1, source_target_pairs={{0,2},{18,16},{1,3},{19,17},{4,6},{22,20},{5,7},{23,21},{8,10},{26... | collective-permute-start | bytes 442376 | tf_op jit(solution)/shard_map/ppermute | solution.py:79
  14.1 0.7 %compare_reduce_fusion = pred[384]{0:T(512)(128)(4,1)S(1)} fusion(f32[8,384]{1,0:T(8,128)} %get-tuple-element.4), kind=kLoop, calls=%fused_computation.49 | loop fusion | flops 384 | bytes 1920 | tf_op jit(solution)/shard_map/gt | solution.py:91
  14.8 0.0 copy-start
  14.8 1.6 %dynamic-slice_bitcast_fusion = bf16[384,2304]{1,0:T(8,128)(2,1)S(1)} fusion(bf16[1,1,448,4608]{3,2,1,0:T(8,128)(2,1)} %param.5, s32[]{:T(128)S(6)} %select_n.57), kind=kLoop, calls=%fused_computation.2 | loop fusion | bytes 3538948 | tf_op jit(solution)/shard_map/dynamic_slice | solution.py:82
  16.4 0.0 copy-done
  16.4 0.0 collective-permute-done.6
  16.5 0.0 collective-permute-done.2
  16.5 0.5 %collective-permute-start.4 = (bf16[32,2304]{1,0:T(8,128)(2,1)S(1)}, bf16[32,2304]{1,0:T(8,128)(2,1)S(1)}, u32[]{:S(2)}, u32[]{:S(2)}) collective-permute-start(bf16[32,2304]{1,0:T(8,128)(2,1)S(1)} %collective-permute-done.2), channel_id=1, source_target_pairs={{0,4},{4,0},{8,12},{12,8},{1,5},{5,1},{9,13},{13,9},{2,6},{6,2},{1... | collective-permute-start | bytes 442376 | tf_op jit(solution)/shard_map/ppermute | solution.py:80
  17.0 0.8 %collective-permute-done = bf16[32,2304]{1,0:T(8,128)(2,1)S(1)} collective-permute-done((bf16[32,2304]{1,0:T(8,128)(2,1)S(1)}, bf16[32,2304]{1,0:T(8,128)(2,1)S(1)}, u32[]{:S(2)}, u32[]{:S(2)}) %collective-permute-start) | collective-permute-done | bytes 147488 | tf_op jit(solution)/shard_map/ppermute | solution.py:79
  17.8 0.0 collective-permute-done.1
  17.8 0.7 %fusion = f32[3,32,384]{2,1,0:T(8,128)S(1)} fusion(bf16[384,2304]{1,0:T(8,128)(2,1)S(1)} %dynamic-slice_bitcast_fusion, bf16[1,32,2304]{2,1,0:T(8,128)(2,1)S(1)} %bitcast.55, bf16[1,32,2304]{2,1,0:T(8,128)(2,1)S(1)} %bitcast.56, bf16[1,32,2304]{2,1,0:T(8,128)(2,1)S(1)} %select_bitcast_fusion), kind=kOutput, calls=%fused_computation | convolution fusion | flops 170311680 | bytes 2359296 | tf_op jit(solution)/shard_map/kwd,rd->kwr/dot_general | solution.py:87
  18.5 2.6 %collective-permute-start.3 = (f32[3,32,384]{2,1,0:T(8,128)S(1)}, f32[3,32,384]{2,1,0:T(8,128)S(1)}, u32[]{:S(2)}, u32[]{:S(2)}) collective-permute-start(f32[3,32,384]{2,1,0:T(8,128)S(1)} %fusion), channel_id=1, source_target_pairs={{0,16},{16,0},{1,17},{17,1},{2,18},{18,2},{3,19},{19,3},{4,20},{20... | collective-permute-start | bytes 442376 | tf_op jit(solution)/shard_map/ppermute | solution.py:90
  21.1 1.4 %collective-permute-done.4 = bf16[32,2304]{1,0:T(8,128)(2,1)S(1)} collective-permute-done((bf16[32,2304]{1,0:T(8,128)(2,1)S(1)}, bf16[32,2304]{1,0:T(8,128)(2,1)S(1)}, u32[]{:S(2)}, u32[]{:S(2)}) %collective-permute-start.4) | collective-permute-done | bytes 147488 | tf_op jit(solution)/shard_map/ppermute | solution.py:80
  22.5 0.6 %convolution_bitcast_fusion.1 = f32[1,32,384]{2,1,0:T(8,128)S(1)} fusion(bf16[32,2304]{1,0:T(8,128)(2,1)S(1)} %collective-permute-done.4, bf16[384,2304]{1,0:T(8,128)(2,1)S(1)} %dynamic-slice_bitcast_fusion), kind=kOutput, calls=%fused_computation.4 | convolution fusion | flops 56623104 | bytes 1966080 | tf_op jit(solution)/shard_map/kwd,rd->kwr/dot_general | solution.py:87
  23.1 0.1 collective-permute-start.5
  23.2 1.6 %collective-permute-done.3 = f32[3,32,384]{2,1,0:T(8,128)S(1)} collective-permute-done((f32[3,32,384]{2,1,0:T(8,128)S(1)}, f32[3,32,384]{2,1,0:T(8,128)S(1)}, u32[]{:S(2)}, u32[]{:S(2)}) %collective-permute-start.3) | collective-permute-done | bytes 147488 | tf_op jit(solution)/shard_map/ppermute | solution.py:90
  24.8 0.2 convolution_bitcast_fusion
  25.0 0.5 %collective-permute-start.7 = (f32[32,32]{1,0:T(8,128)S(1)}, f32[32,32]{1,0:T(8,128)S(1)}, u32[]{:S(2)}, u32[]{:S(2)}) collective-permute-start(f32[32,32]{1,0:T(8,128)S(1)} %get-tuple-element.14), channel_id=1, source_target_pairs={{0,4},{4,0},{8,12},{12,8},{1,5},{5,1},{9,13},{13,9},{2,6},{6,2},{1... | collective-permute-start | bytes 12296 | tf_op jit(solution)/shard_map/ppermute | solution.py:100
  25.6 1.4 %collective-permute-start.8 = (f32[32,32]{1,0:T(8,128)S(1)}, f32[32,32]{1,0:T(8,128)S(1)}, u32[]{:S(2)}, u32[]{:S(2)}) collective-permute-start(f32[32,32]{1,0:T(8,128)S(1)} %get-tuple-element.15), channel_id=1, source_target_pairs={{0,8},{4,12},{8,0},{12,4},{1,9},{5,13},{9,1},{13,5},{2,10},{6,14},... | collective-permute-start | bytes 12296 | tf_op jit(solution)/shard_map/ppermute | solution.py:100
  27.0 0.3 collective-permute-done.5
  27.3 0.1 convolution_bitcast_fusion.2
  27.4 2.2 %collective-permute-start.9 = (f32[32,32]{1,0:T(8,128)S(1)}, f32[32,32]{1,0:T(8,128)S(1)}, u32[]{:S(2)}, u32[]{:S(2)}) collective-permute-start(f32[32,32]{1,0:T(8,128)S(1)} %convolution_bitcast_fusion.2), channel_id=1, source_target_pairs={{0,12},{4,8},{8,4},{12,0},{1,13},{5,9},{9,5},{13,1},{2,14},{6,10},... | collective-permute-start | bytes 12296 | tf_op jit(solution)/shard_map/ppermute | solution.py:101
  29.6 0.1 fusion.16
  29.7 0.0 collective-permute-done.7
  29.7 0.5 %collective-permute-done.8 = f32[32,32]{1,0:T(8,128)S(1)} collective-permute-done((f32[32,32]{1,0:T(8,128)S(1)}, f32[32,32]{1,0:T(8,128)S(1)}, u32[]{:S(2)}, u32[]{:S(2)}) %collective-permute-start.8) | collective-permute-done | bytes 4128 | tf_op jit(solution)/shard_map/ppermute | solution.py:100
  30.2 2.8 %collective-permute-done.9 = f32[32,32]{1,0:T(8,128)S(1)} collective-permute-done((f32[32,32]{1,0:T(8,128)S(1)}, f32[32,32]{1,0:T(8,128)S(1)}, u32[]{:S(2)}, u32[]{:S(2)}) %collective-permute-start.9) | collective-permute-done | bytes 4128 | tf_op jit(solution)/shard_map/ppermute | solution.py:101
  33.0 0.1 collective-permute-start.10
  33.1 0.7 %fusion.14 = bf16[1,1,4,32,448]{4,3,2,1,0:T(8,128)(2,1)} fusion(bf16[1,32,384]{2,1,0:T(8,128)(2,1)S(1)} %get-tuple-element.13, bf16[1,32,384]{2,1,0:T(8,128)(2,1)S(1)} %get-tuple-element.12, bf16[1,32,384]{2,1,0:T(8,128)(2,1)S(1)} %get-tuple-element.11, bf16[1,32,384]{2,1,0:T(8,128)(2,1)S(1)} %get-tuple-element.10), kind=kLoop, calls=%fused_computation.27 | loop fusion | flops 745472 | bytes 212992 | tf_op jit(solution)/shard_map/broadcast_in_dim | solution.py:109
  33.7 0.5 %collective-permute-done.10 = f32[16,32]{1,0:T(8,128)S(1)} collective-permute-done((f32[16,32]{1,0:T(8,128)S(1)}, f32[16,32]{1,0:T(8,128)S(1)}, u32[]{:S(2)}, u32[]{:S(2)}) %collective-permute-start.10) | collective-permute-done | bytes 2080 | tf_op jit(solution)/shard_map/ppermute | solution.py:103
  34.2 0.6 %copy.8 = f32[16,2,1,32]{3,2,1,0:T(1,128)} copy(f32[16,2,1,32]{3,0,2,1:T(8,128)S(1)} %maximum_select_fusion) | data formatting | bytes 8192
  (9 shorter events, 0.1 us)
Async XLA Ops:
  1.6 14.8 %collective-permute-start.2 = (bf16[32,2304]{1,0:T(8,128)(2,1)S(1)}, bf16[32,2304]{1,0:T(8,128)(2,1)S(1)}, u32[]{:S(2)}, u32[]{:S(2)}) collective-permute-start(bf16[32,2304]{1,0:T(8,128)(2,1)S(1)} %get-tuple-element.9), channel_id=1, source_target_pairs={{0,8},{4,12},{8,0},{12,4},{2,24},{6,28},{10,16},{14,20},{16,10},{2... | collective-permute-start | bytes 442376 | tf_op jit(solution)/shard_map/ppermute | solution.py:77
  5.7 12.1 %collective-permute-start.1 = (bf16[32,2304]{1,0:T(8,128)(2,1)S(1)}, bf16[32,2304]{1,0:T(8,128)(2,1)S(1)}, u32[]{:S(2)}, u32[]{:S(2)}) collective-permute-start(bf16[32,2304]{1,0:T(8,128)(2,1)S(1)} %get-tuple-element.9), channel_id=1, source_target_pairs={{0,4},{4,0},{8,12},{12,8},{2,20},{6,16},{10,28},{14,24},{16,6},{20... | collective-permute-start | bytes 442376 | tf_op jit(solution)/shard_map/ppermute | solution.py:78
  8.8 7.6 %collective-permute-start.6 = (bf16[16,384]{1,0:T(8,128)(2,1)}, bf16[16,384]{1,0:T(8,128)(2,1)S(1)}, u32[]{:S(2)}, u32[]{:S(2)}) collective-permute-start(bf16[16,384]{1,0:T(8,128)(2,1)} %get-tuple-element.5), channel_id=1, source_target_pairs={{0,1},{1,0},{2,3},{3,2},{4,5},{5,4},{6,7},{7,6},{8,9},{9,8},{10,11... | collective-permute-start | bytes 36872 | tf_op jit(solution)/shard_map/ppermute | solution.py:84
  8.9 8.9 %collective-permute-start = (bf16[32,2304]{1,0:T(8,128)(2,1)S(1)}, bf16[32,2304]{1,0:T(8,128)(2,1)S(1)}, u32[]{:S(2)}, u32[]{:S(2)}) collective-permute-start(bf16[32,2304]{1,0:T(8,128)(2,1)S(1)} %get-tuple-element.8), channel_id=1, source_target_pairs={{0,2},{18,16},{1,3},{19,17},{4,6},{22,20},{5,7},{23,21},{8,10},{26... | collective-permute-start | bytes 442376 | tf_op jit(solution)/shard_map/ppermute | solution.py:79
  14.8 1.6 %copy-start = (bf16[16,384]{1,0:T(8,128)(2,1)S(1)}, bf16[16,384]{1,0:T(8,128)(2,1)}, u32[]{:S(2)}) copy-start(bf16[16,384]{1,0:T(8,128)(2,1)} %get-tuple-element.5) | copy-start | bytes 36868
  16.5 6.0 %collective-permute-start.4 = (bf16[32,2304]{1,0:T(8,128)(2,1)S(1)}, bf16[32,2304]{1,0:T(8,128)(2,1)S(1)}, u32[]{:S(2)}, u32[]{:S(2)}) collective-permute-start(bf16[32,2304]{1,0:T(8,128)(2,1)S(1)} %collective-permute-done.2), channel_id=1, source_target_pairs={{0,4},{4,0},{8,12},{12,8},{1,5},{5,1},{9,13},{13,9},{2,6},{6,2},{1... | collective-permute-start | bytes 442376 | tf_op jit(solution)/shard_map/ppermute | solution.py:80
  18.5 6.3 %collective-permute-start.3 = (f32[3,32,384]{2,1,0:T(8,128)S(1)}, f32[3,32,384]{2,1,0:T(8,128)S(1)}, u32[]{:S(2)}, u32[]{:S(2)}) collective-permute-start(f32[3,32,384]{2,1,0:T(8,128)S(1)} %fusion), channel_id=1, source_target_pairs={{0,16},{16,0},{1,17},{17,1},{2,18},{18,2},{3,19},{19,3},{4,20},{20... | collective-permute-start | bytes 442376 | tf_op jit(solution)/shard_map/ppermute | solution.py:90
  23.1 4.2 %collective-permute-start.5 = (f32[1,32,384]{2,1,0:T(8,128)S(1)}, f32[1,32,384]{2,1,0:T(8,128)S(1)}, u32[]{:S(2)}, u32[]{:S(2)}) collective-permute-start(f32[1,32,384]{2,1,0:T(8,128)S(1)} %convolution_bitcast_fusion.1), channel_id=1, source_target_pairs={{0,16},{16,0},{1,17},{17,1},{2,18},{18,2},{3,19},{19,3},{4,20},{20... | collective-permute-start | bytes 147464 | tf_op jit(solution)/shard_map/ppermute | solution.py:90
  25.0 4.7 %collective-permute-start.7 = (f32[32,32]{1,0:T(8,128)S(1)}, f32[32,32]{1,0:T(8,128)S(1)}, u32[]{:S(2)}, u32[]{:S(2)}) collective-permute-start(f32[32,32]{1,0:T(8,128)S(1)} %get-tuple-element.14), channel_id=1, source_target_pairs={{0,4},{4,0},{8,12},{12,8},{1,5},{5,1},{9,13},{13,9},{2,6},{6,2},{1... | collective-permute-start | bytes 12296 | tf_op jit(solution)/shard_map/ppermute | solution.py:100
  25.6 4.6 %collective-permute-start.8 = (f32[32,32]{1,0:T(8,128)S(1)}, f32[32,32]{1,0:T(8,128)S(1)}, u32[]{:S(2)}, u32[]{:S(2)}) collective-permute-start(f32[32,32]{1,0:T(8,128)S(1)} %get-tuple-element.15), channel_id=1, source_target_pairs={{0,8},{4,12},{8,0},{12,4},{1,9},{5,13},{9,1},{13,5},{2,10},{6,14},... | collective-permute-start | bytes 12296 | tf_op jit(solution)/shard_map/ppermute | solution.py:100
  27.4 5.5 %collective-permute-start.9 = (f32[32,32]{1,0:T(8,128)S(1)}, f32[32,32]{1,0:T(8,128)S(1)}, u32[]{:S(2)}, u32[]{:S(2)}) collective-permute-start(f32[32,32]{1,0:T(8,128)S(1)} %convolution_bitcast_fusion.2), channel_id=1, source_target_pairs={{0,12},{4,8},{8,4},{12,0},{1,13},{5,9},{9,5},{13,1},{2,14},{6,10},... | collective-permute-start | bytes 12296 | tf_op jit(solution)/shard_map/ppermute | solution.py:101
  33.0 1.2 %collective-permute-start.10 = (f32[16,32]{1,0:T(8,128)S(1)}, f32[16,32]{1,0:T(8,128)S(1)}, u32[]{:S(2)}, u32[]{:S(2)}) collective-permute-start(f32[16,32]{1,0:T(8,128)S(1)} %get-tuple-element.17), channel_id=1, source_target_pairs={{0,1},{1,0},{2,3},{3,2},{4,5},{5,4},{6,7},{7,6},{8,9},{9,8},{10,11... | collective-permute-start | bytes 6152 | tf_op jit(solution)/shard_map/ppermute | solution.py:103

commit v3 on v2

--- a/solution.py
+++ b/solution.py
@@ -73,37 +73,49 @@
 
     swap = [(0, 1), (1, 0)]
     piece = lax.optimization_barrier(lax.dynamic_slice_in_dim(encoder[0, 0], y * features, features, axis=0))
-    beside = lax.dynamic_slice_in_dim(encoder[0, 0], (1 - y) * features, features, axis=0)
-    far = lax.ppermute(piece, AXES, swapped(step(2)))
+    far = lax.ppermute(piece, AXES, swapped(step(3)))
     near = lax.ppermute(piece, AXES, swapped(step(1)))
-    given = lax.ppermute(beside, ("group", "tgt"), [(0, 1), (3, 2)])
     last = lax.ppermute(far, "src", step(1))
-    own = jnp.where(x == y, piece, given)
     slab = lax.optimization_barrier(lax.dynamic_slice(decoder[0, 0], (0, y * width), (rows, width)))
-    mine, live = masked(counts, activations, prompt_mask, rows)
-    weights = jnp.concatenate([mine, lax.ppermute(mine, "prompt", swap)])
 
     def products(blocks):
         return jnp.einsum("kwd,rd->kwr", blocks, slab, preferred_element_type=jnp.float32)
 
-    def finish(part):
-        total = part + lax.ppermute(part, "group", swap)
+    def finish(part, narrow, after=None):
+        if narrow:
+            sent = lax.ppermute((part * 16).astype(jnp.float16), "group", swap)
+            if after is not None:
+                sent, _ = lax.optimization_barrier((sent, after))
+            total = part + sent.astype(jnp.float32) * 0.0625
+        else:
+            sent = lax.ppermute(part, "group", swap)
+            if after is not None:
+                sent, _ = lax.optimization_barrier((sent, after))
+            total = part + sent
         return jnp.where(live[0] > 0, total, 0.0).astype(jnp.bfloat16)
 
     def terms(virtual):
         return jnp.einsum("pr,kwr->kpw", weights, virtual, preferred_element_type=jnp.float32)
 
-    first = finish(products(jnp.stack([own, near, far])))
+    whole = encoder[0, 0].reshape(2, features, width)
+    halves = products(whole)
+    counts, _ = lax.optimization_barrier((counts, halves))
+    mine, live = masked(counts, activations, prompt_mask, rows)
+    weights = jnp.concatenate([mine, lax.ppermute(mine, "prompt", swap)])
+    across = lax.ppermute(jnp.where(x == 0, halves[1], halves[0]), "tgt", swap)
+    own = jnp.where(x == y, jnp.where(x == 0, halves[0], halves[1]), across)
+    early = jnp.concatenate([own[None], products(jnp.stack([near, far]))])
+    first = finish(early, False, last)
     first_terms = terms(first)
-    final = finish(products(last[None]))
+    final = finish(products(last[None]), False)
     final_terms = terms(final)
-    total = first_terms[0] + lax.ppermute(first_terms[1], "src", step(1)) + lax.ppermute(first_terms[2], "src", step(2))
-    total = total + lax.ppermute(final_terms[0], "src", step(3))
+    total = first_terms[0] + lax.ppermute(first_terms[1], "src", step(1)) + lax.ppermute(first_terms[2], "src", step(3))
+    total = total + lax.ppermute(final_terms[0], "src", step(2))
+    held = jnp.stack([first[0], first[1], final[0], first[2]])
     half = total.shape[0] // 2
     theirs = lax.ppermute(total[half:], "prompt", swap)
     keep = total[:half]
     edges = jnp.where(core == 0, jnp.stack([keep, theirs], 1), jnp.stack([theirs, keep], 1))
-    held = jnp.concatenate([first, final])
     virtual = jnp.stack([lax.dynamic_index_in_dim(held, jnp.bitwise_xor(z, k), 0, keepdims=False) for k in range(4)])
     virtual = jnp.pad(virtual, ((0, 0), (0, 0), (0, row_count - rows)))
     return virtual[None, None], edges[:, :, None]

time: 35.1 us -> 35 us (level)
  starting transfers between devices: 18.2 us -> 15.4 us
  waiting for transfers between devices: 7.96 us -> 9.28 us
  local copies, waits for them, and re-layouts: 3.26 us -> 3.94 us
  matrix products: 1.57 us -> 2.24 us
    ppermute x6, starting transfers between devices: 15.6 us -> 12.4 us  [the longest x1 5.11 us: square_mesh(): far = lax.ppermute(piece, AXES, swapped(step(3)))]
    ppermute x1, starting transfers between devices: 0.51 us -> 2.32 us  [square_mesh(): last = lax.ppermute(far, 'src', step(1))]
    unnamed x4, local copies, waits for them, and re-layouts: 0.63 us -> 2.29 us
    ppermute x1, starting transfers between devices: 1.58 us -> 0.01 us  [square_mesh(): near = lax.ppermute(piece, AXES, swapped(step(1)))]
    dynamic_slice x1 -> x2, local copies, waits for them, and re-layouts: 1.01 us -> 0.04 us  [the longest x1 0.02 us: square_mesh(): lax.dynamic_index_in_dim(held, jnp.bitwise_xor(z, k), 0, keepdims=False)]
    ppermute x1, waiting for transfers between devices: 1.43 us -> 2.34 us  [square_mesh(): last = lax.ppermute(far, 'src', step(1))]
    dot_general x2 -> x3, matrix products: 1.28 us -> 1.95 us  [products(): jnp.einsum('kwd,rd->kwr', blocks, slab, preferred_element_type=jnp.float32)]
    ppermute x6, waiting for transfers between devices: 6.03 us -> 6.38 us  [the longest x1 2.36 us: square_mesh(): lax.ppermute(first_terms[2], 'src', step(3))]
  transfers between devices with their start and end apart: 11 -> 11, of which waited for: 7 -> 8; matrix products, arithmetic and copies ran while one was open for 13% -> 17% of each run, Pallas kernels for 4% -> 4%
where the time goes in v3:
time: 35 us; the launch traced here: 34.7 us
  starting transfers between devices  15.4 us (44%)
  waiting for transfers between devices  9.28 us (27%)
  local copies, waits for them, and re-layouts  3.94 us (11%)
  matrix products  2.24 us (6%)
  Pallas kernels  1.53 us (4%)
  other arithmetic  1.49 us (4%)
  between operations  0.76 us (2%)
    ppermute x1, starting transfers between devices, square_mesh(): far = lax.ppermute(piece, AXES, swapped(step(3)))  5.11 us
    ppermute x1, starting transfers between devices, square_mesh(): across = lax.ppermute(jnp.where(x == 0, halves[1], halves[0]), 'tgt', swap)  2.9 us
    ppermute x1, waiting for transfers between devices, square_mesh(): lax.ppermute(first_terms[2], 'src', step(3))  2.36 us
    ppermute x1, waiting for transfers between devices, square_mesh(): last = lax.ppermute(far, 'src', step(1))  2.34 us
    ppermute x1, starting transfers between devices, square_mesh(): last = lax.ppermute(far, 'src', step(1))  2.32 us
    unnamed x4, local copies, waits for them, and re-layouts  2.29 us
    dot_general x3, matrix products, products(): jnp.einsum('kwd,rd->kwr', blocks, slab, preferred_element_type=jnp.float32)  1.95 us
    ppermute x1, waiting for transfers between devices, square_mesh(): across = lax.ppermute(jnp.where(x == 0, halves[1], halves[0]), 'tgt', swap)  1.88 us
  transfers between devices with their start and end apart: 11, of which 8 were waited for; matrix products, arithmetic and copies ran while one was open for 17% of the time, Pallas kernels for 4%

profile of v3, /device:TPU:0, one launch (start us, length us, event | category | flops | bytes accessed | tf_op | source)
XLA Modules:
  0.0 34.7 jit_solution(9611677573343003462)
XLA Ops:
  0.6 0.0 copy-start
  0.7 0.9 %copy-done = bf16[1,1,64,2304]{3,2,1,0:T(8,128)(2,1)S(1)} copy-done((bf16[1,1,64,2304]{3,2,1,0:T(8,128)(2,1)S(1)}, bf16[1,1,64,2304]{3,2,1,0:T(8,128)(2,1)}, u32[]{:S(2)}) %copy-start) | copy-done | bytes 294936
  1.6 5.1 %collective-permute-start.2 = (bf16[32,2304]{1,0:T(8,128)(2,1)S(1)}, bf16[32,2304]{1,0:T(8,128)(2,1)S(1)}, u32[]{:S(2)}, u32[]{:S(2)}) collective-permute-start(bf16[32,2304]{1,0:T(8,128)(2,1)S(1)} %dynamic-slice_bitcast_fusion.1), channel_id=1, source_target_pairs={{0,12},{4,8},{8,4},{12,0},{2,28},{6,24},{10,20},{14,16},{16,14},{2... | collective-permute-start | bytes 442376 | tf_op jit(solution)/shard_map/ppermute | solution.py:76
  6.7 0.0 collective-permute-start.1
  6.7 1.6 %dynamic-slice_bitcast_fusion = bf16[384,2304]{1,0:T(8,128)(2,1)S(1)} fusion(bf16[1,1,448,4608]{3,2,1,0:T(8,128)(2,1)} %param.5, s32[]{:T(128)S(6)} %select_n.66), kind=kLoop, calls=%fused_computation.4 | loop fusion | bytes 3538948 | tf_op jit(solution)/shard_map/dynamic_slice | solution.py:79
  8.3 0.7 %fusion.4 = f32[2,32,384]{2,1,0:T(8,128)S(1)} fusion(bf16[2,32,2304]{2,1,0:T(8,128)(2,1)S(1)} %bitcast.64, bf16[384,2304]{1,0:T(8,128)(2,1)S(1)} %dynamic-slice_bitcast_fusion), kind=kOutput, calls=%fused_computation.5 | convolution fusion | flops 113246208 | bytes 2162688 | tf_op jit(solution)/shard_map/kwd,rd->kwr/dot_general | solution.py:82
  9.0 1.5 %shard_map.68 = (bf16[16,384]{1,0:T(8,128)(2,1)}, f32[8,384]{1,0:T(8,128)}) custom-call(s32[4]{0:T(128)} %counts_ref, bf16[16,448]{1,0:T(8,128)(2,1)} %bitcast.67, s32[7,1,16]{2,1,0:T(1,128)} %bitcast.69), custom_call_target="tpu_custom_call" | custom-call | tf_op jit(solution)/shard_map/pallas_call | solution.py:32
  10.5 0.0 collective-permute-start.6
  10.5 2.9 %collective-permute-start = (f32[32,384]{1,0:T(8,128)S(1)}, f32[32,384]{1,0:T(8,128)S(1)}, u32[]{:S(2)}, u32[]{:S(2)}) collective-permute-start(f32[32,384]{1,0:T(8,128)S(1)} %select_bitcast_fusion), channel_id=1, source_target_pairs={{0,2},{2,0},{1,3},{3,1},{4,6},{6,4},{5,7},{7,5},{8,10},{10,8},{9,1... | collective-permute-start | bytes 147464 | tf_op jit(solution)/shard_map/ppermute | solution.py:105
  13.4 0.7 %compare_reduce_fusion = pred[384]{0:T(512)(128)(4,1)S(1)} fusion(f32[8,384]{1,0:T(8,128)} %get-tuple-element.7), kind=kLoop, calls=%fused_computation.41 | loop fusion | flops 384 | bytes 1920 | tf_op jit(solution)/shard_map/gt | solution.py:95
  14.2 0.7 %constant_dynamic-update-slice_fusion.1 = bf16[32,384]{1,0:T(8,128)(2,1)S(1)} fusion(bf16[16,384]{1,0:T(8,128)(2,1)} %get-tuple-element.9), kind=kLoop, calls=%fused_computation.40 | loop fusion | bytes 24576
  14.9 0.0 collective-permute-done.6
  14.9 1.9 %collective-permute-done = f32[32,384]{1,0:T(8,128)S(1)} collective-permute-done((f32[32,384]{1,0:T(8,128)S(1)}, f32[32,384]{1,0:T(8,128)S(1)}, u32[]{:S(2)}, u32[]{:S(2)}) %collective-permute-start) | collective-permute-done | bytes 49184 | tf_op jit(solution)/shard_map/ppermute | solution.py:105
  16.8 0.0 collective-permute-done.2
  16.8 2.3 %collective-permute-start.4 = (bf16[32,2304]{1,0:T(8,128)(2,1)S(1)}, bf16[32,2304]{1,0:T(8,128)(2,1)S(1)}, u32[]{:S(2)}, u32[]{:S(2)}) collective-permute-start(bf16[32,2304]{1,0:T(8,128)(2,1)S(1)} %collective-permute-done.2), channel_id=1, source_target_pairs={{0,4},{4,0},{8,12},{12,8},{1,5},{5,1},{9,13},{13,9},{2,6},{6,2},{1... | collective-permute-start | bytes 442376 | tf_op jit(solution)/shard_map/ppermute | solution.py:78
  19.1 0.0 collective-permute-done.1
  19.1 0.7 %fusion = f32[2,32,384]{2,1,0:T(8,128)S(1)} fusion(bf16[384,2304]{1,0:T(8,128)(2,1)S(1)} %dynamic-slice_bitcast_fusion, bf16[1,32,2304]{2,1,0:T(8,128)(2,1)S(1)} %bitcast.65, bf16[1,32,2304]{2,1,0:T(8,128)(2,1)S(1)} %bitcast.66), kind=kOutput, calls=%fused_computation | convolution fusion | flops 113393664 | bytes 2162688 | tf_op jit(solution)/shard_map/kwd,rd->kwr/dot_general | solution.py:82
  19.8 1.1 %collective-permute-start.3 = (f32[3,32,384]{2,1,0:T(8,128)S(1)}, f32[3,32,384]{2,1,0:T(8,128)S(1)}, u32[]{:S(2)}, u32[]{:S(2)}) collective-permute-start(f32[3,32,384]{2,1,0:T(8,128)S(1)} %pad_maximum_fusion), channel_id=1, source_target_pairs={{0,16},{16,0},{1,17},{17,1},{2,18},{18,2},{3,19},{19,3},{4,20},{20... | collective-permute-start | bytes 442376 | tf_op jit(solution)/shard_map/ppermute | solution.py:91
  20.9 2.3 %collective-permute-done.4 = bf16[32,2304]{1,0:T(8,128)(2,1)S(1)} collective-permute-done((bf16[32,2304]{1,0:T(8,128)(2,1)S(1)}, bf16[32,2304]{1,0:T(8,128)(2,1)S(1)}, u32[]{:S(2)}, u32[]{:S(2)}) %collective-permute-start.4) | collective-permute-done | bytes 147488 | tf_op jit(solution)/shard_map/ppermute | solution.py:78
  23.2 0.6 %convolution_bitcast_fusion.1 = f32[1,32,384]{2,1,0:T(8,128)S(1)} fusion(bf16[32,2304]{1,0:T(8,128)(2,1)S(1)} %collective-permute-done.4, bf16[384,2304]{1,0:T(8,128)(2,1)S(1)} %dynamic-slice_bitcast_fusion), kind=kOutput, calls=%fused_computation.7 | convolution fusion | flops 56623104 | bytes 1966080 | tf_op jit(solution)/shard_map/kwd,rd->kwr/dot_general | solution.py:82
  23.8 0.4 %collective-permute-start.5 = (f32[1,32,384]{2,1,0:T(8,128)S(1)}, f32[1,32,384]{2,1,0:T(8,128)S(1)}, u32[]{:S(2)}, u32[]{:S(2)}) collective-permute-start(f32[1,32,384]{2,1,0:T(8,128)S(1)} %convolution_bitcast_fusion.1), channel_id=1, source_target_pairs={{0,16},{16,0},{1,17},{17,1},{2,18},{18,2},{3,19},{19,3},{4,20},{20... | collective-permute-start | bytes 147464 | tf_op jit(solution)/shard_map/ppermute | solution.py:91
  24.3 1.2 %collective-permute-done.3 = f32[3,32,384]{2,1,0:T(8,128)S(1)} collective-permute-done((f32[3,32,384]{2,1,0:T(8,128)S(1)}, f32[3,32,384]{2,1,0:T(8,128)S(1)}, u32[]{:S(2)}, u32[]{:S(2)}) %collective-permute-start.3) | collective-permute-done | bytes 147488 | tf_op jit(solution)/shard_map/ppermute | solution.py:91
  25.5 0.2 convolution_bitcast_fusion
  25.7 0.6 %collective-permute-start.7 = (f32[32,32]{1,0:T(8,128)S(1)}, f32[32,32]{1,0:T(8,128)S(1)}, u32[]{:S(2)}, u32[]{:S(2)}) collective-permute-start(f32[32,32]{1,0:T(8,128)S(1)} %get-tuple-element.16), channel_id=1, source_target_pairs={{0,4},{4,0},{8,12},{12,8},{1,5},{5,1},{9,13},{13,9},{2,6},{6,2},{1... | collective-permute-start | bytes 12296 | tf_op jit(solution)/shard_map/ppermute | solution.py:112
  26.3 1.6 %collective-permute-start.8 = (f32[32,32]{1,0:T(8,128)S(1)}, f32[32,32]{1,0:T(8,128)S(1)}, u32[]{:S(2)}, u32[]{:S(2)}) collective-permute-start(f32[32,32]{1,0:T(8,128)S(1)} %get-tuple-element.17), channel_id=1, source_target_pairs={{0,12},{4,8},{8,4},{12,0},{1,13},{5,9},{9,5},{13,1},{2,14},{6,10},... | collective-permute-start | bytes 12296 | tf_op jit(solution)/shard_map/ppermute | solution.py:112
  27.9 0.1 collective-permute-done.5
  28.0 0.1 convolution_bitcast_fusion.2
  28.1 1.3 %collective-permute-start.9 = (f32[32,32]{1,0:T(8,128)S(1)}, f32[32,32]{1,0:T(8,128)S(1)}, u32[]{:S(2)}, u32[]{:S(2)}) collective-permute-start(f32[32,32]{1,0:T(8,128)S(1)} %convolution_bitcast_fusion.2), channel_id=1, source_target_pairs={{0,8},{4,12},{8,0},{12,4},{1,9},{5,13},{9,1},{13,5},{2,10},{6,14},... | collective-permute-start | bytes 12296 | tf_op jit(solution)/shard_map/ppermute | solution.py:113
  29.4 0.1 collective-permute-done.7
  29.5 2.4 %collective-permute-done.8 = f32[32,32]{1,0:T(8,128)S(1)} collective-permute-done((f32[32,32]{1,0:T(8,128)S(1)}, f32[32,32]{1,0:T(8,128)S(1)}, u32[]{:S(2)}, u32[]{:S(2)}) %collective-permute-start.8) | collective-permute-done | bytes 4128 | tf_op jit(solution)/shard_map/ppermute | solution.py:112
  31.9 0.9 %collective-permute-done.9 = f32[32,32]{1,0:T(8,128)S(1)} collective-permute-done((f32[32,32]{1,0:T(8,128)S(1)}, f32[32,32]{1,0:T(8,128)S(1)}, u32[]{:S(2)}, u32[]{:S(2)}) %collective-permute-start.9) | collective-permute-done | bytes 4128 | tf_op jit(solution)/shard_map/ppermute | solution.py:113
  32.8 0.1 collective-permute-start.10
  32.9 0.7 %fusion.17 = bf16[1,1,4,32,448]{4,3,2,1,0:T(8,128)(2,1)} fusion(bf16[1,32,384]{2,1,0:T(8,128)(2,1)S(1)} %get-tuple-element.13, bf16[1,32,384]{2,1,0:T(8,128)(2,1)S(1)} %get-tuple-element.14, bf16[1,32,384]{2,1,0:T(8,128)(2,1)S(1)} %get-tuple-element.15, bf16[1,32,384]{2,1,0:T(8,128)(2,1)S(1)} %get-tuple-element.12), kind=kLoop, calls=%fused_computation.23 | loop fusion | flops 745472 | bytes 212992 | tf_op jit(solution)/shard_map/broadcast_in_dim | solution.py:121
  33.5 0.5 %collective-permute-done.10 = f32[16,32]{1,0:T(8,128)S(1)} collective-permute-done((f32[16,32]{1,0:T(8,128)S(1)}, f32[16,32]{1,0:T(8,128)S(1)}, u32[]{:S(2)}, u32[]{:S(2)}) %collective-permute-start.10) | collective-permute-done | bytes 2080 | tf_op jit(solution)/shard_map/ppermute | solution.py:116
  34.0 0.6 %copy.8 = f32[16,2,1,32]{3,2,1,0:T(1,128)} copy(f32[16,2,1,32]{3,0,2,1:T(8,128)S(1)} %maximum_select_fusion) | data formatting | bytes 8192
  (15 shorter events, 0.2 us)
Async XLA Ops:
  0.6 1.0 %copy-start = (bf16[1,1,64,2304]{3,2,1,0:T(8,128)(2,1)S(1)}, bf16[1,1,64,2304]{3,2,1,0:T(8,128)(2,1)}, u32[]{:S(2)}) copy-start(bf16[1,1,64,2304]{3,2,1,0:T(8,128)(2,1)} %param.6) | copy-start | bytes 884740
  1.6 15.2 %collective-permute-start.2 = (bf16[32,2304]{1,0:T(8,128)(2,1)S(1)}, bf16[32,2304]{1,0:T(8,128)(2,1)S(1)}, u32[]{:S(2)}, u32[]{:S(2)}) collective-permute-start(bf16[32,2304]{1,0:T(8,128)(2,1)S(1)} %dynamic-slice_bitcast_fusion.1), channel_id=1, source_target_pairs={{0,12},{4,8},{8,4},{12,0},{2,28},{6,24},{10,20},{14,16},{16,14},{2... | collective-permute-start | bytes 442376 | tf_op jit(solution)/shard_map/ppermute | solution.py:76
  6.7 12.4 %collective-permute-start.1 = (bf16[32,2304]{1,0:T(8,128)(2,1)S(1)}, bf16[32,2304]{1,0:T(8,128)(2,1)S(1)}, u32[]{:S(2)}, u32[]{:S(2)}) collective-permute-start(bf16[32,2304]{1,0:T(8,128)(2,1)S(1)} %dynamic-slice_bitcast_fusion.1), channel_id=1, source_target_pairs={{0,4},{4,0},{8,12},{12,8},{2,20},{6,16},{10,28},{14,24},{16,6},{20... | collective-permute-start | bytes 442376 | tf_op jit(solution)/shard_map/ppermute | solution.py:77
  10.5 4.4 %collective-permute-start.6 = (bf16[16,384]{1,0:T(8,128)(2,1)}, bf16[16,384]{1,0:T(8,128)(2,1)S(1)}, u32[]{:S(2)}, u32[]{:S(2)}) collective-permute-start(bf16[16,384]{1,0:T(8,128)(2,1)} %get-tuple-element.9), channel_id=1, source_target_pairs={{0,1},{1,0},{2,3},{3,2},{4,5},{5,4},{6,7},{7,6},{8,9},{9,8},{10,11... | collective-permute-start | bytes 36872 | tf_op jit(solution)/shard_map/ppermute | solution.py:104
  10.5 6.2 %collective-permute-start = (f32[32,384]{1,0:T(8,128)S(1)}, f32[32,384]{1,0:T(8,128)S(1)}, u32[]{:S(2)}, u32[]{:S(2)}) collective-permute-start(f32[32,384]{1,0:T(8,128)S(1)} %select_bitcast_fusion), channel_id=1, source_target_pairs={{0,2},{2,0},{1,3},{3,1},{4,6},{6,4},{5,7},{7,5},{8,10},{10,8},{9,1... | collective-permute-start | bytes 147464 | tf_op jit(solution)/shard_map/ppermute | solution.py:105
  16.8 6.4 %collective-permute-start.4 = (bf16[32,2304]{1,0:T(8,128)(2,1)S(1)}, bf16[32,2304]{1,0:T(8,128)(2,1)S(1)}, u32[]{:S(2)}, u32[]{:S(2)}) collective-permute-start(bf16[32,2304]{1,0:T(8,128)(2,1)S(1)} %collective-permute-done.2), channel_id=1, source_target_pairs={{0,4},{4,0},{8,12},{12,8},{1,5},{5,1},{9,13},{13,9},{2,6},{6,2},{1... | collective-permute-start | bytes 442376 | tf_op jit(solution)/shard_map/ppermute | solution.py:78
  19.8 5.6 %collective-permute-start.3 = (f32[3,32,384]{2,1,0:T(8,128)S(1)}, f32[3,32,384]{2,1,0:T(8,128)S(1)}, u32[]{:S(2)}, u32[]{:S(2)}) collective-permute-start(f32[3,32,384]{2,1,0:T(8,128)S(1)} %pad_maximum_fusion), channel_id=1, source_target_pairs={{0,16},{16,0},{1,17},{17,1},{2,18},{18,2},{3,19},{19,3},{4,20},{20... | collective-permute-start | bytes 442376 | tf_op jit(solution)/shard_map/ppermute | solution.py:91
  23.8 4.2 %collective-permute-start.5 = (f32[1,32,384]{2,1,0:T(8,128)S(1)}, f32[1,32,384]{2,1,0:T(8,128)S(1)}, u32[]{:S(2)}, u32[]{:S(2)}) collective-permute-start(f32[1,32,384]{2,1,0:T(8,128)S(1)} %convolution_bitcast_fusion.1), channel_id=1, source_target_pairs={{0,16},{16,0},{1,17},{17,1},{2,18},{18,2},{3,19},{19,3},{4,20},{20... | collective-permute-start | bytes 147464 | tf_op jit(solution)/shard_map/ppermute | solution.py:91
  25.7 3.8 %collective-permute-start.7 = (f32[32,32]{1,0:T(8,128)S(1)}, f32[32,32]{1,0:T(8,128)S(1)}, u32[]{:S(2)}, u32[]{:S(2)}) collective-permute-start(f32[32,32]{1,0:T(8,128)S(1)} %get-tuple-element.16), channel_id=1, source_target_pairs={{0,4},{4,0},{8,12},{12,8},{1,5},{5,1},{9,13},{13,9},{2,6},{6,2},{1... | collective-permute-start | bytes 12296 | tf_op jit(solution)/shard_map/ppermute | solution.py:112
  26.3 5.5 %collective-permute-start.8 = (f32[32,32]{1,0:T(8,128)S(1)}, f32[32,32]{1,0:T(8,128)S(1)}, u32[]{:S(2)}, u32[]{:S(2)}) collective-permute-start(f32[32,32]{1,0:T(8,128)S(1)} %get-tuple-element.17), channel_id=1, source_target_pairs={{0,12},{4,8},{8,4},{12,0},{1,13},{5,9},{9,5},{13,1},{2,14},{6,10},... | collective-permute-start | bytes 12296 | tf_op jit(solution)/shard_map/ppermute | solution.py:112
  28.1 4.6 %collective-permute-start.9 = (f32[32,32]{1,0:T(8,128)S(1)}, f32[32,32]{1,0:T(8,128)S(1)}, u32[]{:S(2)}, u32[]{:S(2)}) collective-permute-start(f32[32,32]{1,0:T(8,128)S(1)} %convolution_bitcast_fusion.2), channel_id=1, source_target_pairs={{0,8},{4,12},{8,0},{12,4},{1,9},{5,13},{9,1},{13,5},{2,10},{6,14},... | collective-permute-start | bytes 12296 | tf_op jit(solution)/shard_map/ppermute | solution.py:113
  32.8 1.2 %collective-permute-start.10 = (f32[16,32]{1,0:T(8,128)S(1)}, f32[16,32]{1,0:T(8,128)S(1)}, u32[]{:S(2)}, u32[]{:S(2)}) collective-permute-start(f32[16,32]{1,0:T(8,128)S(1)} %get-tuple-element.19), channel_id=1, source_target_pairs={{0,1},{1,0},{2,3},{3,2},{4,5},{5,4},{6,7},{7,6},{8,9},{9,8},{10,11... | collective-permute-start | bytes 6152 | tf_op jit(solution)/shard_map/ppermute | solution.py:116

commit v4 on v2

--- a/solution.py
+++ b/solution.py
@@ -73,37 +73,48 @@
 
     swap = [(0, 1), (1, 0)]
     piece = lax.optimization_barrier(lax.dynamic_slice_in_dim(encoder[0, 0], y * features, features, axis=0))
-    beside = lax.dynamic_slice_in_dim(encoder[0, 0], (1 - y) * features, features, axis=0)
-    far = lax.ppermute(piece, AXES, swapped(step(2)))
+    far = lax.ppermute(piece, AXES, swapped(step(3)))
     near = lax.ppermute(piece, AXES, swapped(step(1)))
-    given = lax.ppermute(beside, ("group", "tgt"), [(0, 1), (3, 2)])
     last = lax.ppermute(far, "src", step(1))
-    own = jnp.where(x == y, piece, given)
     slab = lax.optimization_barrier(lax.dynamic_slice(decoder[0, 0], (0, y * width), (rows, width)))
     mine, live = masked(counts, activations, prompt_mask, rows)
     weights = jnp.concatenate([mine, lax.ppermute(mine, "prompt", swap)])
 
-    def products(blocks):
+    def products(blocks, slab):
         return jnp.einsum("kwd,rd->kwr", blocks, slab, preferred_element_type=jnp.float32)
 
-    def finish(part):
-        total = part + lax.ppermute(part, "group", swap)
-        return jnp.where(live[0] > 0, total, 0.0).astype(jnp.bfloat16)
+    def swapped_sum(part, sent, axis, narrow, after=None):
+        if narrow:
+            sent = (sent * 16).astype(jnp.float16)
+        sent = lax.ppermute(sent, axis, swap)
+        if after is not None:
+            sent, _ = lax.optimization_barrier((sent, after))
+        if narrow:
+            sent = sent.astype(jnp.float32) * 0.0625
+        return jnp.where(live[0] > 0, part + sent, 0.0).astype(jnp.bfloat16)
 
     def terms(virtual):
         return jnp.einsum("pr,kwr->kpw", weights, virtual, preferred_element_type=jnp.float32)
 
-    first = finish(products(jnp.stack([own, near, far])))
-    first_terms = terms(first)
-    final = finish(products(last[None]))
-    final_terms = terms(final)
-    total = first_terms[0] + lax.ppermute(first_terms[1], "src", step(1)) + lax.ppermute(first_terms[2], "src", step(2))
-    total = total + lax.ppermute(final_terms[0], "src", step(3))
+    whole = encoder[0, 0].reshape(2, features, width)
+    own_slab = lax.optimization_barrier(lax.dynamic_slice(decoder[0, 0], (0, x * width), (rows, width)))
+    halves = products(whole, own_slab)
+    ours, theirs = jnp.where(x == 0, halves, halves[::-1])
+    early = products(jnp.stack([near, far]), slab)
+    ours, theirs, _ = lax.optimization_barrier((ours, theirs, early))
+    own = swapped_sum(ours[None], theirs[None], "tgt", False)
+    early = swapped_sum(early, early, "group", False, last)
+    near_terms, far_terms = terms(early)
+    late = products(last[None], slab)
+    late = swapped_sum(late, late, "group", False)
+    last_terms = terms(late)[0]
+    total = terms(own)[0] + lax.ppermute(near_terms, "src", step(1)) + lax.ppermute(far_terms, "src", step(3))
+    total = total + lax.ppermute(last_terms, "src", step(2))
     half = total.shape[0] // 2
     theirs = lax.ppermute(total[half:], "prompt", swap)
     keep = total[:half]
     edges = jnp.where(core == 0, jnp.stack([keep, theirs], 1), jnp.stack([theirs, keep], 1))
-    held = jnp.concatenate([first, final])
+    held = jnp.stack([own[0], early[0], late[0], early[1]])
     virtual = jnp.stack([lax.dynamic_index_in_dim(held, jnp.bitwise_xor(z, k), 0, keepdims=False) for k in range(4)])
     virtual = jnp.pad(virtual, ((0, 0), (0, 0), (0, row_count - rows)))
     return virtual[None, None], edges[:, :, None]

time: 35.1 us -> 33.2 us (0.946)
  waiting for transfers between devices: 7.96 us -> 5.14 us
  matrix products: 1.57 us -> 2.34 us
  local copies, waits for them, and re-layouts: 3.26 us -> 3.91 us
  starting transfers between devices: 18.2 us -> 17.7 us
    ppermute x7, waiting for transfers between devices: 6.03 us -> 4.26 us  [the longest x1 3.52 us: square_mesh(): lax.ppermute(far_terms, 'src', step(3))]
    ppermute x1, starting transfers between devices: 1.58 us -> 0.01 us  [square_mesh(): near = lax.ppermute(piece, AXES, swapped(step(1)))]
    ppermute x1, starting transfers between devices: 0.51 us -> 2.08 us  [square_mesh(): last = lax.ppermute(far, 'src', step(1))]
    ppermute x1, waiting for transfers between devices: 1.43 us -> 0.38 us  [square_mesh(): last = lax.ppermute(far, 'src', step(1))]
    unnamed x4 -> x6, local copies, waits for them, and re-layouts: 0.63 us -> 1.59 us
    dot_general x2 -> x3, matrix products: 1.28 us -> 1.95 us  [products(): jnp.einsum('kwd,rd->kwr', blocks, slab, preferred_element_type=jnp.float32)]
    ppermute x7, starting transfers between devices: 16.1 us -> 15.6 us  [the longest x3 6.84 us: swapped_sum(): sent = lax.ppermute(sent, axis, swap)]
    dynamic_slice x2 -> x3, local copies, waits for them, and re-layouts: 2.61 us -> 2.27 us  [the longest x1 2.24 us: square_mesh(): lax.dynamic_slice(decoder[0, 0], (0, x * width), (rows, width))]
  transfers between devices with their start and end apart: 11 -> 11, of which waited for: 7 -> 4; matrix products, arithmetic and copies ran while one was open for 13% -> 18% of each run, Pallas kernels for 4% -> 5%
where the time goes in v4:
time: 33.2 us; the launch traced here: 32.9 us
  starting transfers between devices  17.7 us (53%)
  waiting for transfers between devices  5.14 us (15%)
  local copies, waits for them, and re-layouts  3.91 us (12%)
  matrix products  2.34 us (7%)
  Pallas kernels  1.52 us (5%)
  other arithmetic  1.46 us (4%)
  between operations  0.81 us (2%)
    ppermute x3, starting transfers between devices, swapped_sum(): sent = lax.ppermute(sent, axis, swap)  6.84 us
    ppermute x1, starting transfers between devices, square_mesh(): far = lax.ppermute(piece, AXES, swapped(step(3)))  5.11 us
    ppermute x1, waiting for transfers between devices, square_mesh(): lax.ppermute(far_terms, 'src', step(3))  3.52 us
    dynamic_slice x1, local copies, waits for them, and re-layouts, square_mesh(): lax.dynamic_slice(decoder[0, 0], (0, x * width), (rows, width))  2.24 us
    ppermute x1, starting transfers between devices, square_mesh(): last = lax.ppermute(far, 'src', step(1))  2.08 us
    dot_general x3, matrix products, products(): jnp.einsum('kwd,rd->kwr', blocks, slab, preferred_element_type=jnp.float32)  1.95 us
    ppermute x1, starting transfers between devices, square_mesh(): lax.ppermute(near_terms, 'src', step(1))  1.8 us
    unnamed x6, local copies, waits for them, and re-layouts  1.59 us
  transfers between devices with their start and end apart: 11, of which 4 were waited for; matrix products, arithmetic and copies ran while one was open for 18% of the time, Pallas kernels for 5%

profile of v4, /device:TPU:0, one launch (start us, length us, event | category | flops | bytes accessed | tf_op | source)
XLA Modules:
  0.0 32.9 jit_solution(14095761071356668980)
XLA Ops:
  0.6 0.0 copy-start
  0.7 0.9 %copy-done = bf16[1,1,64,2304]{3,2,1,0:T(8,128)(2,1)S(1)} copy-done((bf16[1,1,64,2304]{3,2,1,0:T(8,128)(2,1)S(1)}, bf16[1,1,64,2304]{3,2,1,0:T(8,128)(2,1)}, u32[]{:S(2)}) %copy-start) | copy-done | bytes 294936
  1.6 5.1 %collective-permute-start.1 = (bf16[32,2304]{1,0:T(8,128)(2,1)S(1)}, bf16[32,2304]{1,0:T(8,128)(2,1)S(1)}, u32[]{:S(2)}, u32[]{:S(2)}) collective-permute-start(bf16[32,2304]{1,0:T(8,128)(2,1)S(1)} %dynamic-slice_bitcast_fusion.2), channel_id=1, source_target_pairs={{0,12},{4,8},{8,4},{12,0},{2,28},{6,24},{10,20},{14,16},{16,14},{2... | collective-permute-start | bytes 442376 | tf_op jit(solution)/shard_map/ppermute | solution.py:76
  6.7 0.0 collective-permute-start
  6.7 1.5 %shard_map.68 = (bf16[16,384]{1,0:T(8,128)(2,1)}, f32[8,384]{1,0:T(8,128)}) custom-call(s32[4]{0:T(128)} %counts_ref.1, bf16[16,448]{1,0:T(8,128)(2,1)} %bitcast.82, s32[7,1,16]{2,1,0:T(1,128)} %bitcast.84), custom_call_target="tpu_custom_call" | custom-call | tf_op jit(solution)/shard_map/pallas_call | solution.py:32
  8.3 0.0 collective-permute-start.6
  8.3 2.2 %dynamic-slice_bitcast_fusion.1 = (bf16[384,2304]{1,0:T(8,128)(2,1)S(1)}, bf16[384,2304]{1,0:T(8,128)(2,1)S(1)}) fusion(bf16[1,1,448,4608]{3,2,1,0:T(8,128)(2,1)} %param.5, s32[]{:T(128)S(6)} %select_n.57, s32[]{:T(128)S(6)} %select_n.60), kind=kLoop, calls=%fused_computation.5 | loop fusion | bytes 7077896 | tf_op jit(solution)/shard_map/dynamic_slice | solution.py:100
  10.5 0.0 copy-start.1
  10.5 0.7 %fusion.4 = f32[2,32,384]{2,1,0:T(8,128)S(1)} fusion(bf16[2,32,2304]{2,1,0:T(8,128)(2,1)S(1)} %bitcast.78, bf16[384,2304]{1,0:T(8,128)(2,1)S(1)} %get-tuple-element.14), kind=kOutput, calls=%fused_computation.6 | convolution fusion | flops 113246208 | bytes 2162688 | tf_op jit(solution)/shard_map/kwd,rd->kwr/dot_general | solution.py:84
  11.2 0.7 %compare_reduce_fusion = pred[384]{0:T(512)(128)(4,1)S(1)} fusion(f32[8,384]{1,0:T(8,128)} %get-tuple-element.7), kind=kLoop, calls=%fused_computation.45 | loop fusion | flops 384 | bytes 1920 | tf_op jit(solution)/shard_map/gt | solution.py:94
  12.0 0.0 copy-done.1
  12.0 0.0 collective-permute-done.6
  12.0 0.0 collective-permute-done.1
  12.0 2.1 %collective-permute-start.4 = (bf16[32,2304]{1,0:T(8,128)(2,1)S(1)}, bf16[32,2304]{1,0:T(8,128)(2,1)S(1)}, u32[]{:S(2)}, u32[]{:S(2)}) collective-permute-start(bf16[32,2304]{1,0:T(8,128)(2,1)S(1)} %collective-permute-done.1), channel_id=1, source_target_pairs={{0,4},{4,0},{8,12},{12,8},{1,5},{5,1},{9,13},{13,9},{2,6},{6,2},{1... | collective-permute-start | bytes 442376 | tf_op jit(solution)/shard_map/ppermute | solution.py:78
  14.1 0.0 collective-permute-done
  14.1 0.7 %fusion = f32[2,32,384]{2,1,0:T(8,128)S(1)} fusion(bf16[384,2304]{1,0:T(8,128)(2,1)S(1)} %get-tuple-element.15, bf16[1,32,2304]{2,1,0:T(8,128)(2,1)S(1)} %bitcast.79, bf16[1,32,2304]{2,1,0:T(8,128)(2,1)S(1)} %bitcast.80), kind=kOutput, calls=%fused_computation | convolution fusion | flops 113393664 | bytes 2162688 | tf_op jit(solution)/shard_map/kwd,rd->kwr/dot_general | solution.py:84
  14.8 3.4 %collective-permute-start.3 = (f32[2,32,384]{2,1,0:T(8,128)S(1)}, f32[2,32,384]{2,1,0:T(8,128)S(1)}, u32[]{:S(2)}, u32[]{:S(2)}) collective-permute-start(f32[2,32,384]{2,1,0:T(8,128)S(1)} %fusion), channel_id=1, source_target_pairs={{0,16},{16,0},{1,17},{17,1},{2,18},{18,2},{3,19},{19,3},{4,20},{20... | collective-permute-start | bytes 294920 | tf_op jit(solution)/shard_map/ppermute | solution.py:89
  18.2 0.1 collective-permute-start.2
  18.2 0.4 %collective-permute-done.4 = bf16[32,2304]{1,0:T(8,128)(2,1)S(1)} collective-permute-done((bf16[32,2304]{1,0:T(8,128)(2,1)S(1)}, bf16[32,2304]{1,0:T(8,128)(2,1)S(1)}, u32[]{:S(2)}, u32[]{:S(2)}) %collective-permute-start.4) | collective-permute-done | bytes 147488 | tf_op jit(solution)/shard_map/ppermute | solution.py:78
  18.6 0.6 %convolution_bitcast_fusion = f32[1,32,384]{2,1,0:T(8,128)S(1)} fusion(bf16[32,2304]{1,0:T(8,128)(2,1)S(1)} %collective-permute-done.4, bf16[384,2304]{1,0:T(8,128)(2,1)S(1)} %get-tuple-element.15), kind=kOutput, calls=%fused_computation.7 | convolution fusion | flops 56623104 | bytes 1966080 | tf_op jit(solution)/shard_map/kwd,rd->kwr/dot_general | solution.py:84
  19.2 3.4 %collective-permute-start.5 = (f32[1,32,384]{2,1,0:T(8,128)S(1)}, f32[1,32,384]{2,1,0:T(8,128)S(1)}, u32[]{:S(2)}, u32[]{:S(2)}) collective-permute-start(f32[1,32,384]{2,1,0:T(8,128)S(1)} %convolution_bitcast_fusion), channel_id=1, source_target_pairs={{0,16},{16,0},{1,17},{17,1},{2,18},{18,2},{3,19},{19,3},{4,20},{20... | collective-permute-start | bytes 147464 | tf_op jit(solution)/shard_map/ppermute | solution.py:89
  22.6 0.0 collective-permute-done.3
  22.7 0.1 convolution_bitcast_fusion.1
  22.8 1.8 %collective-permute-start.7 = (f32[32,32]{1,0:T(8,128)S(1)}, f32[32,32]{1,0:T(8,128)S(1)}, u32[]{:S(2)}, u32[]{:S(2)}) collective-permute-start(f32[32,32]{1,0:T(8,128)S(1)} %get-tuple-element.24), channel_id=1, source_target_pairs={{0,4},{4,0},{8,12},{12,8},{1,5},{5,1},{9,13},{13,9},{2,6},{6,2},{1... | collective-permute-start | bytes 12296 | tf_op jit(solution)/shard_map/ppermute | solution.py:111
  24.6 1.5 %collective-permute-start.8 = (f32[32,32]{1,0:T(8,128)S(1)}, f32[32,32]{1,0:T(8,128)S(1)}, u32[]{:S(2)}, u32[]{:S(2)}) collective-permute-start(f32[32,32]{1,0:T(8,128)S(1)} %get-tuple-element.25), channel_id=1, source_target_pairs={{0,12},{4,8},{8,4},{12,0},{1,13},{5,9},{9,5},{13,1},{2,14},{6,10},... | collective-permute-start | bytes 12296 | tf_op jit(solution)/shard_map/ppermute | solution.py:111
  26.1 0.0 collective-permute-done.2
  26.1 0.0 collective-permute-done.5
  26.1 0.1 convolution_bitcast_fusion.2
  26.2 0.3 %collective-permute-start.9 = (f32[32,32]{1,0:T(8,128)S(1)}, f32[32,32]{1,0:T(8,128)S(1)}, u32[]{:S(2)}, u32[]{:S(2)}) collective-permute-start(f32[32,32]{1,0:T(8,128)S(1)} %convolution_bitcast_fusion.2), channel_id=1, source_target_pairs={{0,8},{4,12},{8,0},{12,4},{1,9},{5,13},{9,1},{13,5},{2,10},{6,14},... | collective-permute-start | bytes 12296 | tf_op jit(solution)/shard_map/ppermute | solution.py:112
  26.6 0.0 collective-permute-done.7
  26.6 3.5 %collective-permute-done.8 = f32[32,32]{1,0:T(8,128)S(1)} collective-permute-done((f32[32,32]{1,0:T(8,128)S(1)}, f32[32,32]{1,0:T(8,128)S(1)}, u32[]{:S(2)}, u32[]{:S(2)}) %collective-permute-start.8) | collective-permute-done | bytes 4128 | tf_op jit(solution)/shard_map/ppermute | solution.py:111
  30.2 0.7 %collective-permute-done.9 = f32[32,32]{1,0:T(8,128)S(1)} collective-permute-done((f32[32,32]{1,0:T(8,128)S(1)}, f32[32,32]{1,0:T(8,128)S(1)}, u32[]{:S(2)}, u32[]{:S(2)}) %collective-permute-start.9) | collective-permute-done | bytes 4128 | tf_op jit(solution)/shard_map/ppermute | solution.py:112
  30.9 0.1 fusion.9
  31.0 0.1 collective-permute-start.10
  31.1 0.7 %fusion.20 = bf16[1,1,4,32,448]{4,3,2,1,0:T(8,128)(2,1)} fusion(bf16[1,32,384]{2,1,0:T(8,128)(2,1)S(1)} %get-tuple-element.17, bf16[1,32,384]{2,1,0:T(8,128)(2,1)S(1)} %get-tuple-element.18, bf16[1,32,384]{2,1,0:T(8,128)(2,1)S(1)} %get-tuple-element.19, bf16[1,32,384]{2,1,0:T(8,128)(2,1)S(1)} %get-tuple-element.16), kind=kLoop, calls=%fused_computation.27 | loop fusion | flops 745472 | bytes 212992 | tf_op jit(solution)/shard_map/broadcast_in_dim | solution.py:120
  31.8 0.5 %collective-permute-done.10 = f32[16,32]{1,0:T(8,128)S(1)} collective-permute-done((f32[16,32]{1,0:T(8,128)S(1)}, f32[16,32]{1,0:T(8,128)S(1)}, u32[]{:S(2)}, u32[]{:S(2)}) %collective-permute-start.10) | collective-permute-done | bytes 2080 | tf_op jit(solution)/shard_map/ppermute | solution.py:114
  32.3 0.6 %copy.9 = f32[16,2,1,32]{3,2,1,0:T(1,128)} copy(f32[16,2,1,32]{3,0,2,1:T(8,128)S(1)} %maximum_select_fusion) | data formatting | bytes 8192
  (13 shorter events, 0.2 us)
Async XLA Ops:
  0.6 1.0 %copy-start = (bf16[1,1,64,2304]{3,2,1,0:T(8,128)(2,1)S(1)}, bf16[1,1,64,2304]{3,2,1,0:T(8,128)(2,1)}, u32[]{:S(2)}) copy-start(bf16[1,1,64,2304]{3,2,1,0:T(8,128)(2,1)} %param.6) | copy-start | bytes 884740
  1.6 10.4 %collective-permute-start.1 = (bf16[32,2304]{1,0:T(8,128)(2,1)S(1)}, bf16[32,2304]{1,0:T(8,128)(2,1)S(1)}, u32[]{:S(2)}, u32[]{:S(2)}) collective-permute-start(bf16[32,2304]{1,0:T(8,128)(2,1)S(1)} %dynamic-slice_bitcast_fusion.2), channel_id=1, source_target_pairs={{0,12},{4,8},{8,4},{12,0},{2,28},{6,24},{10,20},{14,16},{16,14},{2... | collective-permute-start | bytes 442376 | tf_op jit(solution)/shard_map/ppermute | solution.py:76
  6.7 7.4 %collective-permute-start = (bf16[32,2304]{1,0:T(8,128)(2,1)S(1)}, bf16[32,2304]{1,0:T(8,128)(2,1)S(1)}, u32[]{:S(2)}, u32[]{:S(2)}) collective-permute-start(bf16[32,2304]{1,0:T(8,128)(2,1)S(1)} %dynamic-slice_bitcast_fusion.2), channel_id=1, source_target_pairs={{0,4},{4,0},{8,12},{12,8},{2,20},{6,16},{10,28},{14,24},{16,6},{20... | collective-permute-start | bytes 442376 | tf_op jit(solution)/shard_map/ppermute | solution.py:77
  8.3 3.7 %collective-permute-start.6 = (bf16[16,384]{1,0:T(8,128)(2,1)}, bf16[16,384]{1,0:T(8,128)(2,1)S(1)}, u32[]{:S(2)}, u32[]{:S(2)}) collective-permute-start(bf16[16,384]{1,0:T(8,128)(2,1)} %get-tuple-element.11), channel_id=1, source_target_pairs={{0,1},{1,0},{2,3},{3,2},{4,5},{5,4},{6,7},{7,6},{8,9},{9,8},{10,11... | collective-permute-start | bytes 36872 | tf_op jit(solution)/shard_map/ppermute | solution.py:81
  10.5 1.5 %copy-start.1 = (bf16[16,384]{1,0:T(8,128)(2,1)S(1)}, bf16[16,384]{1,0:T(8,128)(2,1)}, u32[]{:S(2)}) copy-start(bf16[16,384]{1,0:T(8,128)(2,1)} %get-tuple-element.11) | copy-start | bytes 36868
  12.0 6.6 %collective-permute-start.4 = (bf16[32,2304]{1,0:T(8,128)(2,1)S(1)}, bf16[32,2304]{1,0:T(8,128)(2,1)S(1)}, u32[]{:S(2)}, u32[]{:S(2)}) collective-permute-start(bf16[32,2304]{1,0:T(8,128)(2,1)S(1)} %collective-permute-done.1), channel_id=1, source_target_pairs={{0,4},{4,0},{8,12},{12,8},{1,5},{5,1},{9,13},{13,9},{2,6},{6,2},{1... | collective-permute-start | bytes 442376 | tf_op jit(solution)/shard_map/ppermute | solution.py:78
  14.8 7.8 %collective-permute-start.3 = (f32[2,32,384]{2,1,0:T(8,128)S(1)}, f32[2,32,384]{2,1,0:T(8,128)S(1)}, u32[]{:S(2)}, u32[]{:S(2)}) collective-permute-start(f32[2,32,384]{2,1,0:T(8,128)S(1)} %fusion), channel_id=1, source_target_pairs={{0,16},{16,0},{1,17},{17,1},{2,18},{18,2},{3,19},{19,3},{4,20},{20... | collective-permute-start | bytes 294920 | tf_op jit(solution)/shard_map/ppermute | solution.py:89
  18.2 7.9 %collective-permute-start.2 = (f32[1,32,384]{2,1,0:T(8,128)S(1)}, f32[1,32,384]{2,1,0:T(8,128)S(1)}, u32[]{:S(2)}, u32[]{:S(2)}) collective-permute-start(f32[1,32,384]{2,1,0:T(8,128)S(1)} %bitcast.81), channel_id=1, source_target_pairs={{0,2},{2,0},{1,3},{3,1},{4,6},{6,4},{5,7},{7,5},{8,10},{10,8},{9,1... | collective-permute-start | bytes 147464 | tf_op jit(solution)/shard_map/ppermute | solution.py:89
  19.2 6.9 %collective-permute-start.5 = (f32[1,32,384]{2,1,0:T(8,128)S(1)}, f32[1,32,384]{2,1,0:T(8,128)S(1)}, u32[]{:S(2)}, u32[]{:S(2)}) collective-permute-start(f32[1,32,384]{2,1,0:T(8,128)S(1)} %convolution_bitcast_fusion), channel_id=1, source_target_pairs={{0,16},{16,0},{1,17},{17,1},{2,18},{18,2},{3,19},{19,3},{4,20},{20... | collective-permute-start | bytes 147464 | tf_op jit(solution)/shard_map/ppermute | solution.py:89
  22.8 3.8 %collective-permute-start.7 = (f32[32,32]{1,0:T(8,128)S(1)}, f32[32,32]{1,0:T(8,128)S(1)}, u32[]{:S(2)}, u32[]{:S(2)}) collective-permute-start(f32[32,32]{1,0:T(8,128)S(1)} %get-tuple-element.24), channel_id=1, source_target_pairs={{0,4},{4,0},{8,12},{12,8},{1,5},{5,1},{9,13},{13,9},{2,6},{6,2},{1... | collective-permute-start | bytes 12296 | tf_op jit(solution)/shard_map/ppermute | solution.py:111
  24.6 5.5 %collective-permute-start.8 = (f32[32,32]{1,0:T(8,128)S(1)}, f32[32,32]{1,0:T(8,128)S(1)}, u32[]{:S(2)}, u32[]{:S(2)}) collective-permute-start(f32[32,32]{1,0:T(8,128)S(1)} %get-tuple-element.25), channel_id=1, source_target_pairs={{0,12},{4,8},{8,4},{12,0},{1,13},{5,9},{9,5},{13,1},{2,14},{6,10},... | collective-permute-start | bytes 12296 | tf_op jit(solution)/shard_map/ppermute | solution.py:111
  26.2 4.6 %collective-permute-start.9 = (f32[32,32]{1,0:T(8,128)S(1)}, f32[32,32]{1,0:T(8,128)S(1)}, u32[]{:S(2)}, u32[]{:S(2)}) collective-permute-start(f32[32,32]{1,0:T(8,128)S(1)} %convolution_bitcast_fusion.2), channel_id=1, source_target_pairs={{0,8},{4,12},{8,0},{12,4},{1,9},{5,13},{9,1},{13,5},{2,10},{6,14},... | collective-permute-start | bytes 12296 | tf_op jit(solution)/shard_map/ppermute | solution.py:112
  31.0 1.2 %collective-permute-start.10 = (f32[16,32]{1,0:T(8,128)S(1)}, f32[16,32]{1,0:T(8,128)S(1)}, u32[]{:S(2)}, u32[]{:S(2)}) collective-permute-start(f32[16,32]{1,0:T(8,128)S(1)} %get-tuple-element.27), channel_id=1, source_target_pairs={{0,1},{1,0},{2,3},{3,2},{4,5},{5,4},{6,7},{7,6},{8,9},{9,8},{10,11... | collective-permute-start | bytes 6152 | tf_op jit(solution)/shard_map/ppermute | solution.py:114

commit v5 on v4

--- a/solution.py
+++ b/solution.py
@@ -108,7 +108,7 @@
     late = products(last[None], slab)
     late = swapped_sum(late, late, "group", False)
     last_terms = terms(late)[0]
-    total = terms(own)[0] + lax.ppermute(near_terms, "src", step(1)) + lax.ppermute(far_terms, "src", step(3))
+    total = terms(own)[0] + lax.ppermute(far_terms, "src", step(3)) + lax.ppermute(near_terms, "src", step(1))
     total = total + lax.ppermute(last_terms, "src", step(2))
     half = total.shape[0] // 2
     theirs = lax.ppermute(total[half:], "prompt", swap)

time: 33.2 us -> 32.3 us (0.973)
  waiting for transfers between devices: 5.14 us -> 3.39 us
  starting transfers between devices: 17.7 us -> 18.6 us
    ppermute x1, waiting for transfers between devices: 3.52 us -> 1.05 us  [square_mesh(): lax.ppermute(far_terms, 'src', step(3))]
    ppermute x1, starting transfers between devices: 0.34 us -> 2.09 us  [square_mesh(): total = total + lax.ppermute(last_terms, 'src', step(2))]
    ppermute x1, starting transfers between devices: 1.8 us -> 0.52 us  [square_mesh(): lax.ppermute(near_terms, 'src', step(1))]
    ppermute x1, waiting for transfers between devices: 0.72 us -> 1.4 us  [square_mesh(): total = total + lax.ppermute(last_terms, 'src', step(2))]
    ppermute x1, starting transfers between devices: 1.47 us -> 1.85 us  [square_mesh(): lax.ppermute(far_terms, 'src', step(3))]
  transfers between devices with their start and end apart: 11 -> 11, of which waited for: 4 -> 5; matrix products, arithmetic and copies ran while one was open for 18% -> 19% of each run, Pallas kernels for 5% -> 5%
where the time goes in v5:
time: 32.3 us; the launch traced here: 32 us
  starting transfers between devices  18.6 us (58%)
  local copies, waits for them, and re-layouts  3.91 us (12%)
  waiting for transfers between devices  3.39 us (10%)
  matrix products  2.34 us (7%)
  Pallas kernels  1.52 us (5%)
  other arithmetic  1.46 us (5%)
  between operations  0.8 us (2%)
    ppermute x3, starting transfers between devices, swapped_sum(): sent = lax.ppermute(sent, axis, swap)  6.84 us
    ppermute x1, starting transfers between devices, square_mesh(): far = lax.ppermute(piece, AXES, swapped(step(3)))  5.11 us
    dynamic_slice x1, local copies, waits for them, and re-layouts, square_mesh(): lax.dynamic_slice(decoder[0, 0], (0, x * width), (rows, width))  2.24 us
    ppermute x1, starting transfers between devices, square_mesh(): total = total + lax.ppermute(last_terms, 'src', step(2))  2.09 us
    ppermute x1, starting transfers between devices, square_mesh(): last = lax.ppermute(far, 'src', step(1))  2.08 us
    dot_general x3, matrix products, products(): jnp.einsum('kwd,rd->kwr', blocks, slab, preferred_element_type=jnp.float32)  1.95 us
    ppermute x1, starting transfers between devices, square_mesh(): lax.ppermute(far_terms, 'src', step(3))  1.85 us
    unnamed x6, local copies, waits for them, and re-layouts  1.59 us
  transfers between devices with their start and end apart: 11, of which 5 were waited for; matrix products, arithmetic and copies ran while one was open for 19% of the time, Pallas kernels for 5%

profile of v5, /device:TPU:0, one launch (start us, length us, event | category | flops | bytes accessed | tf_op | source)
XLA Modules:
  0.0 32.0 jit_solution(9949242927217720197)
XLA Ops:
  0.6 0.0 copy-start
  0.7 0.9 %copy-done = bf16[1,1,64,2304]{3,2,1,0:T(8,128)(2,1)S(1)} copy-done((bf16[1,1,64,2304]{3,2,1,0:T(8,128)(2,1)S(1)}, bf16[1,1,64,2304]{3,2,1,0:T(8,128)(2,1)}, u32[]{:S(2)}) %copy-start) | copy-done | bytes 294936
  1.6 5.1 %collective-permute-start.1 = (bf16[32,2304]{1,0:T(8,128)(2,1)S(1)}, bf16[32,2304]{1,0:T(8,128)(2,1)S(1)}, u32[]{:S(2)}, u32[]{:S(2)}) collective-permute-start(bf16[32,2304]{1,0:T(8,128)(2,1)S(1)} %dynamic-slice_bitcast_fusion.2), channel_id=1, source_target_pairs={{0,12},{4,8},{8,4},{12,0},{2,28},{6,24},{10,20},{14,16},{16,14},{2... | collective-permute-start | bytes 442376 | tf_op jit(solution)/shard_map/ppermute | solution.py:76
  6.7 0.0 collective-permute-start
  6.7 1.5 %shard_map.68 = (bf16[16,384]{1,0:T(8,128)(2,1)}, f32[8,384]{1,0:T(8,128)}) custom-call(s32[4]{0:T(128)} %counts_ref.1, bf16[16,448]{1,0:T(8,128)(2,1)} %bitcast.82, s32[7,1,16]{2,1,0:T(1,128)} %bitcast.84), custom_call_target="tpu_custom_call" | custom-call | tf_op jit(solution)/shard_map/pallas_call | solution.py:32
  8.3 0.0 collective-permute-start.6
  8.3 2.2 %dynamic-slice_bitcast_fusion.1 = (bf16[384,2304]{1,0:T(8,128)(2,1)S(1)}, bf16[384,2304]{1,0:T(8,128)(2,1)S(1)}) fusion(bf16[1,1,448,4608]{3,2,1,0:T(8,128)(2,1)} %param.5, s32[]{:T(128)S(6)} %select_n.57, s32[]{:T(128)S(6)} %select_n.60), kind=kLoop, calls=%fused_computation.5 | loop fusion | bytes 7077896 | tf_op jit(solution)/shard_map/dynamic_slice | solution.py:100
  10.5 0.0 copy-start.1
  10.5 0.7 %fusion.4 = f32[2,32,384]{2,1,0:T(8,128)S(1)} fusion(bf16[2,32,2304]{2,1,0:T(8,128)(2,1)S(1)} %bitcast.78, bf16[384,2304]{1,0:T(8,128)(2,1)S(1)} %get-tuple-element.14), kind=kOutput, calls=%fused_computation.6 | convolution fusion | flops 113246208 | bytes 2162688 | tf_op jit(solution)/shard_map/kwd,rd->kwr/dot_general | solution.py:84
  11.2 0.7 %compare_reduce_fusion = pred[384]{0:T(512)(128)(4,1)S(1)} fusion(f32[8,384]{1,0:T(8,128)} %get-tuple-element.7), kind=kLoop, calls=%fused_computation.45 | loop fusion | flops 384 | bytes 1920 | tf_op jit(solution)/shard_map/gt | solution.py:94
  12.0 0.0 copy-done.1
  12.0 0.0 collective-permute-done.6
  12.0 0.0 collective-permute-done.1
  12.0 2.1 %collective-permute-start.4 = (bf16[32,2304]{1,0:T(8,128)(2,1)S(1)}, bf16[32,2304]{1,0:T(8,128)(2,1)S(1)}, u32[]{:S(2)}, u32[]{:S(2)}) collective-permute-start(bf16[32,2304]{1,0:T(8,128)(2,1)S(1)} %collective-permute-done.1), channel_id=1, source_target_pairs={{0,4},{4,0},{8,12},{12,8},{1,5},{5,1},{9,13},{13,9},{2,6},{6,2},{1... | collective-permute-start | bytes 442376 | tf_op jit(solution)/shard_map/ppermute | solution.py:78
  14.1 0.0 collective-permute-done
  14.1 0.7 %fusion = f32[2,32,384]{2,1,0:T(8,128)S(1)} fusion(bf16[384,2304]{1,0:T(8,128)(2,1)S(1)} %get-tuple-element.15, bf16[1,32,2304]{2,1,0:T(8,128)(2,1)S(1)} %bitcast.79, bf16[1,32,2304]{2,1,0:T(8,128)(2,1)S(1)} %bitcast.80), kind=kOutput, calls=%fused_computation | convolution fusion | flops 113393664 | bytes 2162688 | tf_op jit(solution)/shard_map/kwd,rd->kwr/dot_general | solution.py:84
  14.8 3.4 %collective-permute-start.3 = (f32[2,32,384]{2,1,0:T(8,128)S(1)}, f32[2,32,384]{2,1,0:T(8,128)S(1)}, u32[]{:S(2)}, u32[]{:S(2)}) collective-permute-start(f32[2,32,384]{2,1,0:T(8,128)S(1)} %fusion), channel_id=1, source_target_pairs={{0,16},{16,0},{1,17},{17,1},{2,18},{18,2},{3,19},{19,3},{4,20},{20... | collective-permute-start | bytes 294920 | tf_op jit(solution)/shard_map/ppermute | solution.py:89
  18.2 0.1 collective-permute-start.2
  18.2 0.4 %collective-permute-done.4 = bf16[32,2304]{1,0:T(8,128)(2,1)S(1)} collective-permute-done((bf16[32,2304]{1,0:T(8,128)(2,1)S(1)}, bf16[32,2304]{1,0:T(8,128)(2,1)S(1)}, u32[]{:S(2)}, u32[]{:S(2)}) %collective-permute-start.4) | collective-permute-done | bytes 147488 | tf_op jit(solution)/shard_map/ppermute | solution.py:78
  18.6 0.6 %convolution_bitcast_fusion = f32[1,32,384]{2,1,0:T(8,128)S(1)} fusion(bf16[32,2304]{1,0:T(8,128)(2,1)S(1)} %collective-permute-done.4, bf16[384,2304]{1,0:T(8,128)(2,1)S(1)} %get-tuple-element.15), kind=kOutput, calls=%fused_computation.7 | convolution fusion | flops 56623104 | bytes 1966080 | tf_op jit(solution)/shard_map/kwd,rd->kwr/dot_general | solution.py:84
  19.2 3.4 %collective-permute-start.5 = (f32[1,32,384]{2,1,0:T(8,128)S(1)}, f32[1,32,384]{2,1,0:T(8,128)S(1)}, u32[]{:S(2)}, u32[]{:S(2)}) collective-permute-start(f32[1,32,384]{2,1,0:T(8,128)S(1)} %convolution_bitcast_fusion), channel_id=1, source_target_pairs={{0,16},{16,0},{1,17},{17,1},{2,18},{18,2},{3,19},{19,3},{4,20},{20... | collective-permute-start | bytes 147464 | tf_op jit(solution)/shard_map/ppermute | solution.py:89
  22.6 0.0 collective-permute-done.3
  22.7 0.1 convolution_bitcast_fusion.1
  22.8 1.9 %collective-permute-start.7 = (f32[32,32]{1,0:T(8,128)S(1)}, f32[32,32]{1,0:T(8,128)S(1)}, u32[]{:S(2)}, u32[]{:S(2)}) collective-permute-start(f32[32,32]{1,0:T(8,128)S(1)} %get-tuple-element.24), channel_id=1, source_target_pairs={{0,12},{4,8},{8,4},{12,0},{1,13},{5,9},{9,5},{13,1},{2,14},{6,10},... | collective-permute-start | bytes 12296 | tf_op jit(solution)/shard_map/ppermute | solution.py:111
  24.7 0.5 %collective-permute-start.8 = (f32[32,32]{1,0:T(8,128)S(1)}, f32[32,32]{1,0:T(8,128)S(1)}, u32[]{:S(2)}, u32[]{:S(2)}) collective-permute-start(f32[32,32]{1,0:T(8,128)S(1)} %get-tuple-element.25), channel_id=1, source_target_pairs={{0,4},{4,0},{8,12},{12,8},{1,5},{5,1},{9,13},{13,9},{2,6},{6,2},{1... | collective-permute-start | bytes 12296 | tf_op jit(solution)/shard_map/ppermute | solution.py:111
  25.2 0.0 collective-permute-done.2
  25.2 0.0 collective-permute-done.5
  25.2 0.1 convolution_bitcast_fusion.2
  25.4 2.1 %collective-permute-start.9 = (f32[32,32]{1,0:T(8,128)S(1)}, f32[32,32]{1,0:T(8,128)S(1)}, u32[]{:S(2)}, u32[]{:S(2)}) collective-permute-start(f32[32,32]{1,0:T(8,128)S(1)} %convolution_bitcast_fusion.2), channel_id=1, source_target_pairs={{0,8},{4,12},{8,0},{12,4},{1,9},{5,13},{9,1},{13,5},{2,10},{6,14},... | collective-permute-start | bytes 12296 | tf_op jit(solution)/shard_map/ppermute | solution.py:112
  27.5 1.0 %collective-permute-done.7 = f32[32,32]{1,0:T(8,128)S(1)} collective-permute-done((f32[32,32]{1,0:T(8,128)S(1)}, f32[32,32]{1,0:T(8,128)S(1)}, u32[]{:S(2)}, u32[]{:S(2)}) %collective-permute-start.7) | collective-permute-done | bytes 4128 | tf_op jit(solution)/shard_map/ppermute | solution.py:111
  28.5 0.1 collective-permute-done.8
  28.6 1.4 %collective-permute-done.9 = f32[32,32]{1,0:T(8,128)S(1)} collective-permute-done((f32[32,32]{1,0:T(8,128)S(1)}, f32[32,32]{1,0:T(8,128)S(1)}, u32[]{:S(2)}, u32[]{:S(2)}) %collective-permute-start.9) | collective-permute-done | bytes 4128 | tf_op jit(solution)/shard_map/ppermute | solution.py:112
  30.0 0.1 fusion.9
  30.1 0.1 collective-permute-start.10
  30.2 0.7 %fusion.20 = bf16[1,1,4,32,448]{4,3,2,1,0:T(8,128)(2,1)} fusion(bf16[1,32,384]{2,1,0:T(8,128)(2,1)S(1)} %get-tuple-element.17, bf16[1,32,384]{2,1,0:T(8,128)(2,1)S(1)} %get-tuple-element.18, bf16[1,32,384]{2,1,0:T(8,128)(2,1)S(1)} %get-tuple-element.19, bf16[1,32,384]{2,1,0:T(8,128)(2,1)S(1)} %get-tuple-element.16), kind=kLoop, calls=%fused_computation.27 | loop fusion | flops 745472 | bytes 212992 | tf_op jit(solution)/shard_map/broadcast_in_dim | solution.py:120
  30.9 0.5 %collective-permute-done.10 = f32[16,32]{1,0:T(8,128)S(1)} collective-permute-done((f32[16,32]{1,0:T(8,128)S(1)}, f32[16,32]{1,0:T(8,128)S(1)}, u32[]{:S(2)}, u32[]{:S(2)}) %collective-permute-start.10) | collective-permute-done | bytes 2080 | tf_op jit(solution)/shard_map/ppermute | solution.py:114
  31.4 0.6 %copy.9 = f32[16,2,1,32]{3,2,1,0:T(1,128)} copy(f32[16,2,1,32]{3,0,2,1:T(8,128)S(1)} %maximum_select_fusion) | data formatting | bytes 8192
  (13 shorter events, 0.2 us)
Async XLA Ops:
  0.6 1.0 %copy-start = (bf16[1,1,64,2304]{3,2,1,0:T(8,128)(2,1)S(1)}, bf16[1,1,64,2304]{3,2,1,0:T(8,128)(2,1)}, u32[]{:S(2)}) copy-start(bf16[1,1,64,2304]{3,2,1,0:T(8,128)(2,1)} %param.6) | copy-start | bytes 884740
  1.6 10.4 %collective-permute-start.1 = (bf16[32,2304]{1,0:T(8,128)(2,1)S(1)}, bf16[32,2304]{1,0:T(8,128)(2,1)S(1)}, u32[]{:S(2)}, u32[]{:S(2)}) collective-permute-start(bf16[32,2304]{1,0:T(8,128)(2,1)S(1)} %dynamic-slice_bitcast_fusion.2), channel_id=1, source_target_pairs={{0,12},{4,8},{8,4},{12,0},{2,28},{6,24},{10,20},{14,16},{16,14},{2... | collective-permute-start | bytes 442376 | tf_op jit(solution)/shard_map/ppermute | solution.py:76
  6.7 7.4 %collective-permute-start = (bf16[32,2304]{1,0:T(8,128)(2,1)S(1)}, bf16[32,2304]{1,0:T(8,128)(2,1)S(1)}, u32[]{:S(2)}, u32[]{:S(2)}) collective-permute-start(bf16[32,2304]{1,0:T(8,128)(2,1)S(1)} %dynamic-slice_bitcast_fusion.2), channel_id=1, source_target_pairs={{0,4},{4,0},{8,12},{12,8},{2,20},{6,16},{10,28},{14,24},{16,6},{20... | collective-permute-start | bytes 442376 | tf_op jit(solution)/shard_map/ppermute | solution.py:77
  8.3 3.7 %collective-permute-start.6 = (bf16[16,384]{1,0:T(8,128)(2,1)}, bf16[16,384]{1,0:T(8,128)(2,1)S(1)}, u32[]{:S(2)}, u32[]{:S(2)}) collective-permute-start(bf16[16,384]{1,0:T(8,128)(2,1)} %get-tuple-element.11), channel_id=1, source_target_pairs={{0,1},{1,0},{2,3},{3,2},{4,5},{5,4},{6,7},{7,6},{8,9},{9,8},{10,11... | collective-permute-start | bytes 36872 | tf_op jit(solution)/shard_map/ppermute | solution.py:81
  10.5 1.5 %copy-start.1 = (bf16[16,384]{1,0:T(8,128)(2,1)S(1)}, bf16[16,384]{1,0:T(8,128)(2,1)}, u32[]{:S(2)}) copy-start(bf16[16,384]{1,0:T(8,128)(2,1)} %get-tuple-element.11) | copy-start | bytes 36868
  12.0 6.6 %collective-permute-start.4 = (bf16[32,2304]{1,0:T(8,128)(2,1)S(1)}, bf16[32,2304]{1,0:T(8,128)(2,1)S(1)}, u32[]{:S(2)}, u32[]{:S(2)}) collective-permute-start(bf16[32,2304]{1,0:T(8,128)(2,1)S(1)} %collective-permute-done.1), channel_id=1, source_target_pairs={{0,4},{4,0},{8,12},{12,8},{1,5},{5,1},{9,13},{13,9},{2,6},{6,2},{1... | collective-permute-start | bytes 442376 | tf_op jit(solution)/shard_map/ppermute | solution.py:78
  14.8 7.8 %collective-permute-start.3 = (f32[2,32,384]{2,1,0:T(8,128)S(1)}, f32[2,32,384]{2,1,0:T(8,128)S(1)}, u32[]{:S(2)}, u32[]{:S(2)}) collective-permute-start(f32[2,32,384]{2,1,0:T(8,128)S(1)} %fusion), channel_id=1, source_target_pairs={{0,16},{16,0},{1,17},{17,1},{2,18},{18,2},{3,19},{19,3},{4,20},{20... | collective-permute-start | bytes 294920 | tf_op jit(solution)/shard_map/ppermute | solution.py:89
  18.2 7.0 %collective-permute-start.2 = (f32[1,32,384]{2,1,0:T(8,128)S(1)}, f32[1,32,384]{2,1,0:T(8,128)S(1)}, u32[]{:S(2)}, u32[]{:S(2)}) collective-permute-start(f32[1,32,384]{2,1,0:T(8,128)S(1)} %bitcast.81), channel_id=1, source_target_pairs={{0,2},{2,0},{1,3},{3,1},{4,6},{6,4},{5,7},{7,5},{8,10},{10,8},{9,1... | collective-permute-start | bytes 147464 | tf_op jit(solution)/shard_map/ppermute | solution.py:89
  19.2 6.0 %collective-permute-start.5 = (f32[1,32,384]{2,1,0:T(8,128)S(1)}, f32[1,32,384]{2,1,0:T(8,128)S(1)}, u32[]{:S(2)}, u32[]{:S(2)}) collective-permute-start(f32[1,32,384]{2,1,0:T(8,128)S(1)} %convolution_bitcast_fusion), channel_id=1, source_target_pairs={{0,16},{16,0},{1,17},{17,1},{2,18},{18,2},{3,19},{19,3},{4,20},{20... | collective-permute-start | bytes 147464 | tf_op jit(solution)/shard_map/ppermute | solution.py:89
  22.8 5.7 %collective-permute-start.7 = (f32[32,32]{1,0:T(8,128)S(1)}, f32[32,32]{1,0:T(8,128)S(1)}, u32[]{:S(2)}, u32[]{:S(2)}) collective-permute-start(f32[32,32]{1,0:T(8,128)S(1)} %get-tuple-element.24), channel_id=1, source_target_pairs={{0,12},{4,8},{8,4},{12,0},{1,13},{5,9},{9,5},{13,1},{2,14},{6,10},... | collective-permute-start | bytes 12296 | tf_op jit(solution)/shard_map/ppermute | solution.py:111
  24.7 3.9 %collective-permute-start.8 = (f32[32,32]{1,0:T(8,128)S(1)}, f32[32,32]{1,0:T(8,128)S(1)}, u32[]{:S(2)}, u32[]{:S(2)}) collective-permute-start(f32[32,32]{1,0:T(8,128)S(1)} %get-tuple-element.25), channel_id=1, source_target_pairs={{0,4},{4,0},{8,12},{12,8},{1,5},{5,1},{9,13},{13,9},{2,6},{6,2},{1... | collective-permute-start | bytes 12296 | tf_op jit(solution)/shard_map/ppermute | solution.py:111
  25.4 4.6 %collective-permute-start.9 = (f32[32,32]{1,0:T(8,128)S(1)}, f32[32,32]{1,0:T(8,128)S(1)}, u32[]{:S(2)}, u32[]{:S(2)}) collective-permute-start(f32[32,32]{1,0:T(8,128)S(1)} %convolution_bitcast_fusion.2), channel_id=1, source_target_pairs={{0,8},{4,12},{8,0},{12,4},{1,9},{5,13},{9,1},{13,5},{2,10},{6,14},... | collective-permute-start | bytes 12296 | tf_op jit(solution)/shard_map/ppermute | solution.py:112
  30.1 1.2 %collective-permute-start.10 = (f32[16,32]{1,0:T(8,128)S(1)}, f32[16,32]{1,0:T(8,128)S(1)}, u32[]{:S(2)}, u32[]{:S(2)}) collective-permute-start(f32[16,32]{1,0:T(8,128)S(1)} %get-tuple-element.27), channel_id=1, source_target_pairs={{0,1},{1,0},{2,3},{3,2},{4,5},{5,4},{6,7},{7,6},{8,9},{9,8},{10,11... | collective-permute-start | bytes 6152 | tf_op jit(solution)/shard_map/ppermute | solution.py:114

commit v6 on v5

--- a/solution.py
+++ b/solution.py
@@ -83,14 +83,10 @@
     def products(blocks, slab):
         return jnp.einsum("kwd,rd->kwr", blocks, slab, preferred_element_type=jnp.float32)
 
-    def swapped_sum(part, sent, axis, narrow, after=None):
-        if narrow:
-            sent = (sent * 16).astype(jnp.float16)
+    def swapped_sum(part, sent, axis, after=None):
         sent = lax.ppermute(sent, axis, swap)
         if after is not None:
             sent, _ = lax.optimization_barrier((sent, after))
-        if narrow:
-            sent = sent.astype(jnp.float32) * 0.0625
         return jnp.where(live[0] > 0, part + sent, 0.0).astype(jnp.bfloat16)
 
     def terms(virtual):
@@ -102,11 +98,11 @@
     ours, theirs = jnp.where(x == 0, halves, halves[::-1])
     early = products(jnp.stack([near, far]), slab)
     ours, theirs, _ = lax.optimization_barrier((ours, theirs, early))
-    own = swapped_sum(ours[None], theirs[None], "tgt", False)
-    early = swapped_sum(early, early, "group", False, last)
+    own = swapped_sum(ours[None], theirs[None], "tgt")
+    early = swapped_sum(early, early, "group", after=last)
     near_terms, far_terms = terms(early)
     late = products(last[None], slab)
-    late = swapped_sum(late, late, "group", False)
+    late = swapped_sum(late, late, "group")
     last_terms = terms(late)[0]
     total = terms(own)[0] + lax.ppermute(far_terms, "src", step(3)) + lax.ppermute(near_terms, "src", step(1))
     total = total + lax.ppermute(last_terms, "src", step(2))

time: 32.3 us -> 32.3 us (level)
  no operation moved by 1% of the time
where the time goes in v6:
time: 32.3 us; the launch traced here: 32 us
  starting transfers between devices  18.6 us (58%)
  local copies, waits for them, and re-layouts  3.91 us (12%)
  waiting for transfers between devices  3.39 us (10%)
  matrix products  2.34 us (7%)
  Pallas kernels  1.52 us (5%)
  other arithmetic  1.46 us (5%)
  between operations  0.8 us (2%)
    ppermute x3, starting transfers between devices, swapped_sum(): sent = lax.ppermute(sent, axis, swap)  6.84 us
    ppermute x1, starting transfers between devices, square_mesh(): far = lax.ppermute(piece, AXES, swapped(step(3)))  5.11 us
    dynamic_slice x1, local copies, waits for them, and re-layouts, square_mesh(): lax.dynamic_slice(decoder[0, 0], (0, x * width), (rows, width))  2.24 us
    ppermute x1, starting transfers between devices, square_mesh(): total = total + lax.ppermute(last_terms, 'src', step(2))  2.09 us
    ppermute x1, starting transfers between devices, square_mesh(): last = lax.ppermute(far, 'src', step(1))  2.08 us
    dot_general x3, matrix products, products(): jnp.einsum('kwd,rd->kwr', blocks, slab, preferred_element_type=jnp.float32)  1.95 us
    ppermute x1, starting transfers between devices, square_mesh(): lax.ppermute(far_terms, 'src', step(3))  1.85 us
    unnamed x6, local copies, waits for them, and re-layouts  1.59 us
  transfers between devices with their start and end apart: 11, of which 5 were waited for; matrix products, arithmetic and copies ran while one was open for 19% of the time, Pallas kernels for 5%

profile of v6, /device:TPU:0, one launch (start us, length us, event | category | flops | bytes accessed | tf_op | source)
XLA Modules:
  0.0 32.0 jit_solution(9949242927217720197)
XLA Ops:
  0.6 0.0 copy-start
  0.7 0.9 %copy-done = bf16[1,1,64,2304]{3,2,1,0:T(8,128)(2,1)S(1)} copy-done((bf16[1,1,64,2304]{3,2,1,0:T(8,128)(2,1)S(1)}, bf16[1,1,64,2304]{3,2,1,0:T(8,128)(2,1)}, u32[]{:S(2)}) %copy-start) | copy-done | bytes 294936
  1.6 5.1 %collective-permute-start.1 = (bf16[32,2304]{1,0:T(8,128)(2,1)S(1)}, bf16[32,2304]{1,0:T(8,128)(2,1)S(1)}, u32[]{:S(2)}, u32[]{:S(2)}) collective-permute-start(bf16[32,2304]{1,0:T(8,128)(2,1)S(1)} %dynamic-slice_bitcast_fusion.2), channel_id=1, source_target_pairs={{0,12},{4,8},{8,4},{12,0},{2,28},{6,24},{10,20},{14,16},{16,14},{2... | collective-permute-start | bytes 442376 | tf_op jit(solution)/shard_map/ppermute | solution.py:76
  6.7 0.0 collective-permute-start
  6.7 1.5 %shard_map.68 = (bf16[16,384]{1,0:T(8,128)(2,1)}, f32[8,384]{1,0:T(8,128)}) custom-call(s32[4]{0:T(128)} %counts_ref.1, bf16[16,448]{1,0:T(8,128)(2,1)} %bitcast.82, s32[7,1,16]{2,1,0:T(1,128)} %bitcast.84), custom_call_target="tpu_custom_call" | custom-call | tf_op jit(solution)/shard_map/pallas_call | solution.py:32
  8.3 0.0 collective-permute-start.6
  8.3 2.2 %dynamic-slice_bitcast_fusion.1 = (bf16[384,2304]{1,0:T(8,128)(2,1)S(1)}, bf16[384,2304]{1,0:T(8,128)(2,1)S(1)}) fusion(bf16[1,1,448,4608]{3,2,1,0:T(8,128)(2,1)} %param.5, s32[]{:T(128)S(6)} %select_n.57, s32[]{:T(128)S(6)} %select_n.60), kind=kLoop, calls=%fused_computation.5 | loop fusion | bytes 7077896 | tf_op jit(solution)/shard_map/dynamic_slice | solution.py:96
  10.5 0.0 copy-start.1
  10.5 0.7 %fusion.4 = f32[2,32,384]{2,1,0:T(8,128)S(1)} fusion(bf16[2,32,2304]{2,1,0:T(8,128)(2,1)S(1)} %bitcast.78, bf16[384,2304]{1,0:T(8,128)(2,1)S(1)} %get-tuple-element.14), kind=kOutput, calls=%fused_computation.6 | convolution fusion | flops 113246208 | bytes 2162688 | tf_op jit(solution)/shard_map/kwd,rd->kwr/dot_general | solution.py:84
  11.2 0.7 %compare_reduce_fusion = pred[384]{0:T(512)(128)(4,1)S(1)} fusion(f32[8,384]{1,0:T(8,128)} %get-tuple-element.7), kind=kLoop, calls=%fused_computation.45 | loop fusion | flops 384 | bytes 1920 | tf_op jit(solution)/shard_map/gt | solution.py:90
  12.0 0.0 copy-done.1
  12.0 0.0 collective-permute-done.6
  12.0 0.0 collective-permute-done.1
  12.0 2.1 %collective-permute-start.4 = (bf16[32,2304]{1,0:T(8,128)(2,1)S(1)}, bf16[32,2304]{1,0:T(8,128)(2,1)S(1)}, u32[]{:S(2)}, u32[]{:S(2)}) collective-permute-start(bf16[32,2304]{1,0:T(8,128)(2,1)S(1)} %collective-permute-done.1), channel_id=1, source_target_pairs={{0,4},{4,0},{8,12},{12,8},{1,5},{5,1},{9,13},{13,9},{2,6},{6,2},{1... | collective-permute-start | bytes 442376 | tf_op jit(solution)/shard_map/ppermute | solution.py:78
  14.1 0.0 collective-permute-done
  14.1 0.7 %fusion = f32[2,32,384]{2,1,0:T(8,128)S(1)} fusion(bf16[384,2304]{1,0:T(8,128)(2,1)S(1)} %get-tuple-element.15, bf16[1,32,2304]{2,1,0:T(8,128)(2,1)S(1)} %bitcast.79, bf16[1,32,2304]{2,1,0:T(8,128)(2,1)S(1)} %bitcast.80), kind=kOutput, calls=%fused_computation | convolution fusion | flops 113393664 | bytes 2162688 | tf_op jit(solution)/shard_map/kwd,rd->kwr/dot_general | solution.py:84
  14.8 3.4 %collective-permute-start.3 = (f32[2,32,384]{2,1,0:T(8,128)S(1)}, f32[2,32,384]{2,1,0:T(8,128)S(1)}, u32[]{:S(2)}, u32[]{:S(2)}) collective-permute-start(f32[2,32,384]{2,1,0:T(8,128)S(1)} %fusion), channel_id=1, source_target_pairs={{0,16},{16,0},{1,17},{17,1},{2,18},{18,2},{3,19},{19,3},{4,20},{20... | collective-permute-start | bytes 294920 | tf_op jit(solution)/shard_map/ppermute | solution.py:87
  18.2 0.1 collective-permute-start.2
  18.2 0.4 %collective-permute-done.4 = bf16[32,2304]{1,0:T(8,128)(2,1)S(1)} collective-permute-done((bf16[32,2304]{1,0:T(8,128)(2,1)S(1)}, bf16[32,2304]{1,0:T(8,128)(2,1)S(1)}, u32[]{:S(2)}, u32[]{:S(2)}) %collective-permute-start.4) | collective-permute-done | bytes 147488 | tf_op jit(solution)/shard_map/ppermute | solution.py:78
  18.6 0.6 %convolution_bitcast_fusion = f32[1,32,384]{2,1,0:T(8,128)S(1)} fusion(bf16[32,2304]{1,0:T(8,128)(2,1)S(1)} %collective-permute-done.4, bf16[384,2304]{1,0:T(8,128)(2,1)S(1)} %get-tuple-element.15), kind=kOutput, calls=%fused_computation.7 | convolution fusion | flops 56623104 | bytes 1966080 | tf_op jit(solution)/shard_map/kwd,rd->kwr/dot_general | solution.py:84
  19.2 3.4 %collective-permute-start.5 = (f32[1,32,384]{2,1,0:T(8,128)S(1)}, f32[1,32,384]{2,1,0:T(8,128)S(1)}, u32[]{:S(2)}, u32[]{:S(2)}) collective-permute-start(f32[1,32,384]{2,1,0:T(8,128)S(1)} %convolution_bitcast_fusion), channel_id=1, source_target_pairs={{0,16},{16,0},{1,17},{17,1},{2,18},{18,2},{3,19},{19,3},{4,20},{20... | collective-permute-start | bytes 147464 | tf_op jit(solution)/shard_map/ppermute | solution.py:87
  22.6 0.0 collective-permute-done.3
  22.7 0.1 convolution_bitcast_fusion.1
  22.8 1.9 %collective-permute-start.7 = (f32[32,32]{1,0:T(8,128)S(1)}, f32[32,32]{1,0:T(8,128)S(1)}, u32[]{:S(2)}, u32[]{:S(2)}) collective-permute-start(f32[32,32]{1,0:T(8,128)S(1)} %get-tuple-element.24), channel_id=1, source_target_pairs={{0,12},{4,8},{8,4},{12,0},{1,13},{5,9},{9,5},{13,1},{2,14},{6,10},... | collective-permute-start | bytes 12296 | tf_op jit(solution)/shard_map/ppermute | solution.py:107
  24.7 0.5 %collective-permute-start.8 = (f32[32,32]{1,0:T(8,128)S(1)}, f32[32,32]{1,0:T(8,128)S(1)}, u32[]{:S(2)}, u32[]{:S(2)}) collective-permute-start(f32[32,32]{1,0:T(8,128)S(1)} %get-tuple-element.25), channel_id=1, source_target_pairs={{0,4},{4,0},{8,12},{12,8},{1,5},{5,1},{9,13},{13,9},{2,6},{6,2},{1... | collective-permute-start | bytes 12296 | tf_op jit(solution)/shard_map/ppermute | solution.py:107
  25.2 0.0 collective-permute-done.2
  25.2 0.0 collective-permute-done.5
  25.2 0.1 convolution_bitcast_fusion.2
  25.4 2.1 %collective-permute-start.9 = (f32[32,32]{1,0:T(8,128)S(1)}, f32[32,32]{1,0:T(8,128)S(1)}, u32[]{:S(2)}, u32[]{:S(2)}) collective-permute-start(f32[32,32]{1,0:T(8,128)S(1)} %convolution_bitcast_fusion.2), channel_id=1, source_target_pairs={{0,8},{4,12},{8,0},{12,4},{1,9},{5,13},{9,1},{13,5},{2,10},{6,14},... | collective-permute-start | bytes 12296 | tf_op jit(solution)/shard_map/ppermute | solution.py:108
  27.5 1.0 %collective-permute-done.7 = f32[32,32]{1,0:T(8,128)S(1)} collective-permute-done((f32[32,32]{1,0:T(8,128)S(1)}, f32[32,32]{1,0:T(8,128)S(1)}, u32[]{:S(2)}, u32[]{:S(2)}) %collective-permute-start.7) | collective-permute-done | bytes 4128 | tf_op jit(solution)/shard_map/ppermute | solution.py:107
  28.5 0.1 collective-permute-done.8
  28.6 1.4 %collective-permute-done.9 = f32[32,32]{1,0:T(8,128)S(1)} collective-permute-done((f32[32,32]{1,0:T(8,128)S(1)}, f32[32,32]{1,0:T(8,128)S(1)}, u32[]{:S(2)}, u32[]{:S(2)}) %collective-permute-start.9) | collective-permute-done | bytes 4128 | tf_op jit(solution)/shard_map/ppermute | solution.py:108
  30.0 0.1 fusion.9
  30.1 0.1 collective-permute-start.10
  30.2 0.7 %fusion.20 = bf16[1,1,4,32,448]{4,3,2,1,0:T(8,128)(2,1)} fusion(bf16[1,32,384]{2,1,0:T(8,128)(2,1)S(1)} %get-tuple-element.17, bf16[1,32,384]{2,1,0:T(8,128)(2,1)S(1)} %get-tuple-element.18, bf16[1,32,384]{2,1,0:T(8,128)(2,1)S(1)} %get-tuple-element.19, bf16[1,32,384]{2,1,0:T(8,128)(2,1)S(1)} %get-tuple-element.16), kind=kLoop, calls=%fused_computation.27 | loop fusion | flops 745472 | bytes 212992 | tf_op jit(solution)/shard_map/broadcast_in_dim | solution.py:116
  30.9 0.5 %collective-permute-done.10 = f32[16,32]{1,0:T(8,128)S(1)} collective-permute-done((f32[16,32]{1,0:T(8,128)S(1)}, f32[16,32]{1,0:T(8,128)S(1)}, u32[]{:S(2)}, u32[]{:S(2)}) %collective-permute-start.10) | collective-permute-done | bytes 2080 | tf_op jit(solution)/shard_map/ppermute | solution.py:110
  31.4 0.6 %copy.9 = f32[16,2,1,32]{3,2,1,0:T(1,128)} copy(f32[16,2,1,32]{3,0,2,1:T(8,128)S(1)} %maximum_select_fusion) | data formatting | bytes 8192
  (13 shorter events, 0.2 us)
Async XLA Ops:
  0.6 1.0 %copy-start = (bf16[1,1,64,2304]{3,2,1,0:T(8,128)(2,1)S(1)}, bf16[1,1,64,2304]{3,2,1,0:T(8,128)(2,1)}, u32[]{:S(2)}) copy-start(bf16[1,1,64,2304]{3,2,1,0:T(8,128)(2,1)} %param.6) | copy-start | bytes 884740
  1.6 10.4 %collective-permute-start.1 = (bf16[32,2304]{1,0:T(8,128)(2,1)S(1)}, bf16[32,2304]{1,0:T(8,128)(2,1)S(1)}, u32[]{:S(2)}, u32[]{:S(2)}) collective-permute-start(bf16[32,2304]{1,0:T(8,128)(2,1)S(1)} %dynamic-slice_bitcast_fusion.2), channel_id=1, source_target_pairs={{0,12},{4,8},{8,4},{12,0},{2,28},{6,24},{10,20},{14,16},{16,14},{2... | collective-permute-start | bytes 442376 | tf_op jit(solution)/shard_map/ppermute | solution.py:76
  6.7 7.4 %collective-permute-start = (bf16[32,2304]{1,0:T(8,128)(2,1)S(1)}, bf16[32,2304]{1,0:T(8,128)(2,1)S(1)}, u32[]{:S(2)}, u32[]{:S(2)}) collective-permute-start(bf16[32,2304]{1,0:T(8,128)(2,1)S(1)} %dynamic-slice_bitcast_fusion.2), channel_id=1, source_target_pairs={{0,4},{4,0},{8,12},{12,8},{2,20},{6,16},{10,28},{14,24},{16,6},{20... | collective-permute-start | bytes 442376 | tf_op jit(solution)/shard_map/ppermute | solution.py:77
  8.3 3.7 %collective-permute-start.6 = (bf16[16,384]{1,0:T(8,128)(2,1)}, bf16[16,384]{1,0:T(8,128)(2,1)S(1)}, u32[]{:S(2)}, u32[]{:S(2)}) collective-permute-start(bf16[16,384]{1,0:T(8,128)(2,1)} %get-tuple-element.11), channel_id=1, source_target_pairs={{0,1},{1,0},{2,3},{3,2},{4,5},{5,4},{6,7},{7,6},{8,9},{9,8},{10,11... | collective-permute-start | bytes 36872 | tf_op jit(solution)/shard_map/ppermute | solution.py:81
  10.5 1.5 %copy-start.1 = (bf16[16,384]{1,0:T(8,128)(2,1)S(1)}, bf16[16,384]{1,0:T(8,128)(2,1)}, u32[]{:S(2)}) copy-start(bf16[16,384]{1,0:T(8,128)(2,1)} %get-tuple-element.11) | copy-start | bytes 36868
  12.0 6.6 %collective-permute-start.4 = (bf16[32,2304]{1,0:T(8,128)(2,1)S(1)}, bf16[32,2304]{1,0:T(8,128)(2,1)S(1)}, u32[]{:S(2)}, u32[]{:S(2)}) collective-permute-start(bf16[32,2304]{1,0:T(8,128)(2,1)S(1)} %collective-permute-done.1), channel_id=1, source_target_pairs={{0,4},{4,0},{8,12},{12,8},{1,5},{5,1},{9,13},{13,9},{2,6},{6,2},{1... | collective-permute-start | bytes 442376 | tf_op jit(solution)/shard_map/ppermute | solution.py:78
  14.8 7.8 %collective-permute-start.3 = (f32[2,32,384]{2,1,0:T(8,128)S(1)}, f32[2,32,384]{2,1,0:T(8,128)S(1)}, u32[]{:S(2)}, u32[]{:S(2)}) collective-permute-start(f32[2,32,384]{2,1,0:T(8,128)S(1)} %fusion), channel_id=1, source_target_pairs={{0,16},{16,0},{1,17},{17,1},{2,18},{18,2},{3,19},{19,3},{4,20},{20... | collective-permute-start | bytes 294920 | tf_op jit(solution)/shard_map/ppermute | solution.py:87
  18.2 7.0 %collective-permute-start.2 = (f32[1,32,384]{2,1,0:T(8,128)S(1)}, f32[1,32,384]{2,1,0:T(8,128)S(1)}, u32[]{:S(2)}, u32[]{:S(2)}) collective-permute-start(f32[1,32,384]{2,1,0:T(8,128)S(1)} %bitcast.81), channel_id=1, source_target_pairs={{0,2},{2,0},{1,3},{3,1},{4,6},{6,4},{5,7},{7,5},{8,10},{10,8},{9,1... | collective-permute-start | bytes 147464 | tf_op jit(solution)/shard_map/ppermute | solution.py:87
  19.2 6.0 %collective-permute-start.5 = (f32[1,32,384]{2,1,0:T(8,128)S(1)}, f32[1,32,384]{2,1,0:T(8,128)S(1)}, u32[]{:S(2)}, u32[]{:S(2)}) collective-permute-start(f32[1,32,384]{2,1,0:T(8,128)S(1)} %convolution_bitcast_fusion), channel_id=1, source_target_pairs={{0,16},{16,0},{1,17},{17,1},{2,18},{18,2},{3,19},{19,3},{4,20},{20... | collective-permute-start | bytes 147464 | tf_op jit(solution)/shard_map/ppermute | solution.py:87
  22.8 5.7 %collective-permute-start.7 = (f32[32,32]{1,0:T(8,128)S(1)}, f32[32,32]{1,0:T(8,128)S(1)}, u32[]{:S(2)}, u32[]{:S(2)}) collective-permute-start(f32[32,32]{1,0:T(8,128)S(1)} %get-tuple-element.24), channel_id=1, source_target_pairs={{0,12},{4,8},{8,4},{12,0},{1,13},{5,9},{9,5},{13,1},{2,14},{6,10},... | collective-permute-start | bytes 12296 | tf_op jit(solution)/shard_map/ppermute | solution.py:107
  24.7 3.9 %collective-permute-start.8 = (f32[32,32]{1,0:T(8,128)S(1)}, f32[32,32]{1,0:T(8,128)S(1)}, u32[]{:S(2)}, u32[]{:S(2)}) collective-permute-start(f32[32,32]{1,0:T(8,128)S(1)} %get-tuple-element.25), channel_id=1, source_target_pairs={{0,4},{4,0},{8,12},{12,8},{1,5},{5,1},{9,13},{13,9},{2,6},{6,2},{1... | collective-permute-start | bytes 12296 | tf_op jit(solution)/shard_map/ppermute | solution.py:107
  25.4 4.6 %collective-permute-start.9 = (f32[32,32]{1,0:T(8,128)S(1)}, f32[32,32]{1,0:T(8,128)S(1)}, u32[]{:S(2)}, u32[]{:S(2)}) collective-permute-start(f32[32,32]{1,0:T(8,128)S(1)} %convolution_bitcast_fusion.2), channel_id=1, source_target_pairs={{0,8},{4,12},{8,0},{12,4},{1,9},{5,13},{9,1},{13,5},{2,10},{6,14},... | collective-permute-start | bytes 12296 | tf_op jit(solution)/shard_map/ppermute | solution.py:108
  30.1 1.2 %collective-permute-start.10 = (f32[16,32]{1,0:T(8,128)S(1)}, f32[16,32]{1,0:T(8,128)S(1)}, u32[]{:S(2)}, u32[]{:S(2)}) collective-permute-start(f32[16,32]{1,0:T(8,128)S(1)} %get-tuple-element.27), channel_id=1, source_target_pairs={{0,1},{1,0},{2,3},{3,2},{4,5},{5,4},{6,7},{7,6},{8,9},{9,8},{10,11... | collective-permute-start | bytes 6152 | tf_op jit(solution)/shard_map/ppermute | solution.py:110

commit v7 on v6

--- a/solution.py
+++ b/solution.py
@@ -78,7 +78,7 @@
     last = lax.ppermute(far, "src", step(1))
     slab = lax.optimization_barrier(lax.dynamic_slice(decoder[0, 0], (0, y * width), (rows, width)))
     mine, live = masked(counts, activations, prompt_mask, rows)
-    weights = jnp.concatenate([mine, lax.ppermute(mine, "prompt", swap)])
+    weights = jnp.stack([mine, lax.ppermute(mine, "prompt", swap)])
 
     def products(blocks, slab):
         return jnp.einsum("kwd,rd->kwr", blocks, slab, preferred_element_type=jnp.float32)
@@ -90,13 +90,14 @@
         return jnp.where(live[0] > 0, part + sent, 0.0).astype(jnp.bfloat16)
 
     def terms(virtual):
-        return jnp.einsum("pr,kwr->kpw", weights, virtual, preferred_element_type=jnp.float32)
+        out = jnp.einsum("spr,kwr->kspw", weights, virtual, preferred_element_type=jnp.float32)
+        return out.reshape(out.shape[0], -1, features)
 
     whole = encoder[0, 0].reshape(2, features, width)
     own_slab = lax.optimization_barrier(lax.dynamic_slice(decoder[0, 0], (0, x * width), (rows, width)))
     halves = products(whole, own_slab)
     ours, theirs = jnp.where(x == 0, halves, halves[::-1])
-    early = products(jnp.stack([near, far]), slab)
+    early = jnp.concatenate([products(near[None], slab), products(far[None], slab)])
     ours, theirs, _ = lax.optimization_barrier((ours, theirs, early))
     own = swapped_sum(ours[None], theirs[None], "tgt")
     early = swapped_sum(early, early, "group", after=last)

time: 32.3 us -> 32.2 us (level)
  other arithmetic: 1.46 us -> 2.13 us
  local copies, waits for them, and re-layouts: 3.91 us -> 3.27 us
  matrix products: 2.34 us -> 2.88 us
  waiting for transfers between devices: 3.39 us -> 2.93 us
    unnamed x6 -> x4, local copies, waits for them, and re-layouts: 1.59 us -> 0.96 us
    select_n x1, other arithmetic: 0.01 us -> 0.63 us  [square_mesh(): jnp.where(core == 0, jnp.stack([keep, theirs], 1), jnp.stack([theirs, kee...]
    dot_general x3 -> x4, matrix products: 1.95 us -> 2.5 us  [products(): jnp.einsum('kwd,rd->kwr', blocks, slab, preferred_element_type=jnp.float32)]
    ppermute x1, waiting for transfers between devices: 0.38 us -> 0.01 us  [square_mesh(): last = lax.ppermute(far, 'src', step(1))]
  transfers between devices with their start and end apart: 11 -> 11, of which waited for: 5 -> 3; matrix products, arithmetic and copies ran while one was open for 19% -> 21% of each run, Pallas kernels for 5% -> 5%
where the time goes in v7:
time: 32.2 us; the launch traced here: 31.9 us
  starting transfers between devices  18.3 us (57%)
  local copies, waits for them, and re-layouts  3.27 us (10%)
  waiting for transfers between devices  2.93 us (9%)
  matrix products  2.88 us (9%)
  other arithmetic  2.13 us (7%)
  Pallas kernels  1.52 us (5%)
  between operations  0.83 us (3%)
    ppermute x3, starting transfers between devices, swapped_sum(): sent = lax.ppermute(sent, axis, swap)  6.59 us
    ppermute x1, starting transfers between devices, square_mesh(): far = lax.ppermute(piece, AXES, swapped(step(3)))  5.11 us
    dot_general x4, matrix products, products(): jnp.einsum('kwd,rd->kwr', blocks, slab, preferred_element_type=jnp.float32)  2.5 us
    dynamic_slice x1, local copies, waits for them, and re-layouts, square_mesh(): lax.dynamic_slice(decoder[0, 0], (0, x * width), (rows, width))  2.24 us
    ppermute x1, starting transfers between devices, square_mesh(): last = lax.ppermute(far, 'src', step(1))  2.09 us
    ppermute x1, starting transfers between devices, square_mesh(): total = total + lax.ppermute(last_terms, 'src', step(2))  2.04 us
    ppermute x1, starting transfers between devices, square_mesh(): lax.ppermute(far_terms, 'src', step(3))  1.91 us
    pallas_call x1, Pallas kernels, masked(): pl.pallas_call(mask_kernel, out_shape=(jax.ShapeDtypeStruct((activations....  1.52 us
  transfers between devices with their start and end apart: 11, of which 3 were waited for; matrix products, arithmetic and copies ran while one was open for 21% of the time, Pallas kernels for 5%

profile of v7, /device:TPU:0, one launch (start us, length us, event | category | flops | bytes accessed | tf_op | source)
XLA Modules:
  0.0 31.9 jit_solution(16450938701892181101)
XLA Ops:
  0.6 0.0 copy-start
  0.7 0.9 %copy-done = bf16[1,1,64,2304]{3,2,1,0:T(8,128)(2,1)S(1)} copy-done((bf16[1,1,64,2304]{3,2,1,0:T(8,128)(2,1)S(1)}, bf16[1,1,64,2304]{3,2,1,0:T(8,128)(2,1)}, u32[]{:S(2)}) %copy-start) | copy-done | bytes 294936
  1.6 5.1 %collective-permute-start.1 = (bf16[32,2304]{1,0:T(8,128)(2,1)S(1)}, bf16[32,2304]{1,0:T(8,128)(2,1)S(1)}, u32[]{:S(2)}, u32[]{:S(2)}) collective-permute-start(bf16[32,2304]{1,0:T(8,128)(2,1)S(1)} %dynamic-slice_bitcast_fusion.2), channel_id=1, source_target_pairs={{0,12},{4,8},{8,4},{12,0},{2,28},{6,24},{10,20},{14,16},{16,14},{2... | collective-permute-start | bytes 442376 | tf_op jit(solution)/shard_map/ppermute | solution.py:76
  6.7 0.0 collective-permute-start
  6.7 1.5 %shard_map.68 = (bf16[16,384]{1,0:T(8,128)(2,1)}, f32[8,384]{1,0:T(8,128)}) custom-call(s32[4]{0:T(128)} %counts_ref.1, bf16[16,448]{1,0:T(8,128)(2,1)} %bitcast.90, s32[7,1,16]{2,1,0:T(1,128)} %bitcast.95), custom_call_target="tpu_custom_call" | custom-call | tf_op jit(solution)/shard_map/pallas_call | solution.py:32
  8.3 0.0 collective-permute-start.6
  8.3 2.2 %dynamic-slice_bitcast_fusion.1 = (bf16[384,2304]{1,0:T(8,128)(2,1)S(1)}, bf16[384,2304]{1,0:T(8,128)(2,1)S(1)}) fusion(bf16[1,1,448,4608]{3,2,1,0:T(8,128)(2,1)} %param.5, s32[]{:T(128)S(6)} %select_n.57, s32[]{:T(128)S(6)} %select_n.60), kind=kLoop, calls=%fused_computation.3 | loop fusion | bytes 7077896 | tf_op jit(solution)/shard_map/dynamic_slice | solution.py:97
  10.5 0.7 %fusion.2 = f32[2,32,384]{2,1,0:T(8,128)S(1)} fusion(bf16[2,32,2304]{2,1,0:T(8,128)(2,1)S(1)} %bitcast.81, bf16[384,2304]{1,0:T(8,128)(2,1)S(1)} %get-tuple-element.12), kind=kOutput, calls=%fused_computation.4 | convolution fusion | flops 113246208 | bytes 2162688 | tf_op jit(solution)/shard_map/kwd,rd->kwr/dot_general | solution.py:84
  11.2 0.7 %compare_reduce_fusion = pred[384]{0:T(512)(128)(4,1)S(1)} fusion(f32[8,384]{1,0:T(8,128)} %get-tuple-element.7), kind=kLoop, calls=%fused_computation.40 | loop fusion | flops 384 | bytes 1920 | tf_op jit(solution)/shard_map/gt | solution.py:90
  12.0 0.0 collective-permute-done.1
  12.0 2.1 %collective-permute-start.4 = (bf16[32,2304]{1,0:T(8,128)(2,1)S(1)}, bf16[32,2304]{1,0:T(8,128)(2,1)S(1)}, u32[]{:S(2)}, u32[]{:S(2)}) collective-permute-start(bf16[32,2304]{1,0:T(8,128)(2,1)S(1)} %collective-permute-done.1), channel_id=1, source_target_pairs={{0,4},{4,0},{8,12},{12,8},{1,5},{5,1},{9,13},{13,9},{2,6},{6,2},{1... | collective-permute-start | bytes 442376 | tf_op jit(solution)/shard_map/ppermute | solution.py:78
  14.1 0.6 %convolution_bitcast_fusion.1 = f32[1,32,384]{2,1,0:T(8,128)S(1)} fusion(bf16[32,2304]{1,0:T(8,128)(2,1)S(1)} %collective-permute-done.1, bf16[384,2304]{1,0:T(8,128)(2,1)S(1)} %get-tuple-element.13), kind=kOutput, calls=%fused_computation.6 | convolution fusion | flops 56623104 | bytes 1966080 | tf_op jit(solution)/shard_map/kwd,rd->kwr/dot_general | solution.py:84
  14.7 0.0 copy-start.1
  14.7 0.0 collective-permute-done
  14.7 0.6 %convolution_bitcast_fusion.2 = f32[1,32,384]{2,1,0:T(8,128)S(1)} fusion(bf16[32,2304]{1,0:T(8,128)(2,1)S(1)} %collective-permute-done, bf16[384,2304]{1,0:T(8,128)(2,1)S(1)} %get-tuple-element.13), kind=kOutput, calls=%fused_computation.7 | convolution fusion | flops 56623104 | bytes 1966080 | tf_op jit(solution)/shard_map/kwd,rd->kwr/dot_general | solution.py:84
  15.4 3.5 %collective-permute-start.3 = (f32[2,32,384]{2,1,0:T(8,128)S(1)}, f32[2,32,384]{2,1,0:T(8,128)S(1)}, u32[]{:S(2)}, u32[]{:S(2)}) collective-permute-start(f32[2,32,384]{2,1,0:T(8,128)S(1)} %pad_maximum_fusion), channel_id=1, source_target_pairs={{0,16},{16,0},{1,17},{17,1},{2,18},{18,2},{3,19},{19,3},{4,20},{20... | collective-permute-start | bytes 294920 | tf_op jit(solution)/shard_map/ppermute | solution.py:87
  18.8 0.1 collective-permute-start.2
  18.9 0.0 collective-permute-done.4
  18.9 0.6 %convolution_bitcast_fusion = f32[1,32,384]{2,1,0:T(8,128)S(1)} fusion(bf16[32,2304]{1,0:T(8,128)(2,1)S(1)} %collective-permute-done.4, bf16[384,2304]{1,0:T(8,128)(2,1)S(1)} %get-tuple-element.13), kind=kOutput, calls=%fused_computation.5 | convolution fusion | flops 56623104 | bytes 1966080 | tf_op jit(solution)/shard_map/kwd,rd->kwr/dot_general | solution.py:84
  19.5 3.1 %collective-permute-start.5 = (f32[1,32,384]{2,1,0:T(8,128)S(1)}, f32[1,32,384]{2,1,0:T(8,128)S(1)}, u32[]{:S(2)}, u32[]{:S(2)}) collective-permute-start(f32[1,32,384]{2,1,0:T(8,128)S(1)} %convolution_bitcast_fusion), channel_id=1, source_target_pairs={{0,16},{16,0},{1,17},{17,1},{2,18},{18,2},{3,19},{19,3},{4,20},{20... | collective-permute-start | bytes 147464 | tf_op jit(solution)/shard_map/ppermute | solution.py:87
  22.6 0.0 collective-permute-done.3
  22.6 0.0 collective-permute-done.6
  22.6 0.0 copy-done.1
  22.6 0.1 convolution_bitcast_fusion.3
  22.8 1.9 %collective-permute-start.7 = (f32[32,32]{1,0:T(8,128)S(1)}, f32[32,32]{1,0:T(8,128)S(1)}, u32[]{:S(2)}, u32[]{:S(2)}) collective-permute-start(f32[32,32]{1,0:T(8,128)S(1)} %bitcast.92), channel_id=1, source_target_pairs={{0,12},{4,8},{8,4},{12,0},{1,13},{5,9},{9,5},{13,1},{2,14},{6,10},... | collective-permute-start | bytes 12296 | tf_op jit(solution)/shard_map/ppermute | solution.py:108
  24.7 0.5 %collective-permute-start.8 = (f32[32,32]{1,0:T(8,128)S(1)}, f32[32,32]{1,0:T(8,128)S(1)}, u32[]{:S(2)}, u32[]{:S(2)}) collective-permute-start(f32[32,32]{1,0:T(8,128)S(1)} %bitcast.91), channel_id=1, source_target_pairs={{0,4},{4,0},{8,12},{12,8},{1,5},{5,1},{9,13},{13,9},{2,6},{6,2},{1... | collective-permute-start | bytes 12296 | tf_op jit(solution)/shard_map/ppermute | solution.py:108
  25.2 0.0 collective-permute-done.2
  25.2 0.0 collective-permute-done.5
  25.2 0.1 fusion.16
  25.4 2.0 %collective-permute-start.9 = (f32[32,32]{1,0:T(8,128)S(1)}, f32[32,32]{1,0:T(8,128)S(1)}, u32[]{:S(2)}, u32[]{:S(2)}) collective-permute-start(f32[32,32]{1,0:T(8,128)S(1)} %bitcast.93), channel_id=1, source_target_pairs={{0,8},{4,12},{8,0},{12,4},{1,9},{5,13},{9,1},{13,5},{2,10},{6,14},... | collective-permute-start | bytes 12296 | tf_op jit(solution)/shard_map/ppermute | solution.py:109
  27.4 0.1 fusion.19
  27.6 0.9 %collective-permute-done.7 = f32[32,32]{1,0:T(8,128)S(1)} collective-permute-done((f32[32,32]{1,0:T(8,128)S(1)}, f32[32,32]{1,0:T(8,128)S(1)}, u32[]{:S(2)}, u32[]{:S(2)}) %collective-permute-start.7) | collective-permute-done | bytes 4128 | tf_op jit(solution)/shard_map/ppermute | solution.py:108
  28.5 0.0 collective-permute-done.8
  28.6 1.4 %collective-permute-done.9 = f32[32,32]{1,0:T(8,128)S(1)} collective-permute-done((f32[32,32]{1,0:T(8,128)S(1)}, f32[32,32]{1,0:T(8,128)S(1)}, u32[]{:S(2)}, u32[]{:S(2)}) %collective-permute-start.9) | collective-permute-done | bytes 4128 | tf_op jit(solution)/shard_map/ppermute | solution.py:109
  30.0 0.1 collective-permute-start.10
  30.1 0.7 %fusion.12 = bf16[1,1,4,32,448]{4,3,2,1,0:T(8,128)(2,1)} fusion(bf16[1,32,384]{2,1,0:T(8,128)(2,1)S(1)} %get-tuple-element.15, bf16[1,32,384]{2,1,0:T(8,128)(2,1)S(1)} %get-tuple-element.16, bf16[1,32,384]{2,1,0:T(8,128)(2,1)S(1)} %get-tuple-element.17, bf16[1,32,384]{2,1,0:T(8,128)(2,1)S(1)} %get-tuple-element.14), kind=kLoop, calls=%fused_computation.19 | loop fusion | flops 745472 | bytes 212992 | tf_op jit(solution)/shard_map/broadcast_in_dim | solution.py:117
  30.8 0.5 %collective-permute-done.10 = f32[16,32]{1,0:T(8,128)S(1)} collective-permute-done((f32[16,32]{1,0:T(8,128)S(1)}, f32[16,32]{1,0:T(8,128)S(1)}, u32[]{:S(2)}, u32[]{:S(2)}) %collective-permute-start.10) | collective-permute-done | bytes 2080 | tf_op jit(solution)/shard_map/ppermute | solution.py:111
  31.3 0.6 %broadcast_select_fusion = f32[16,2,1,32]{3,2,1,0:T(1,128)} fusion(pred[]{:T(512)S(6)} %eq.7, f32[16,1,1,32]{3,2,1,0:T(1,128)S(1)} %bitcast.94, f32[16,1,1,32]{3,2,1,0:T(1,128)S(1)} %bitcast.89), kind=kLoop, calls=%fused_computation.30 | loop fusion | flops 3072 | bytes 8193 | tf_op jit(solution)/shard_map/jit(_where)/select_n | solution.py:113
  (12 shorter events, 0.2 us)
Async XLA Ops:
  0.6 1.0 %copy-start = (bf16[1,1,64,2304]{3,2,1,0:T(8,128)(2,1)S(1)}, bf16[1,1,64,2304]{3,2,1,0:T(8,128)(2,1)}, u32[]{:S(2)}) copy-start(bf16[1,1,64,2304]{3,2,1,0:T(8,128)(2,1)} %param.6) | copy-start | bytes 884740
  1.6 10.4 %collective-permute-start.1 = (bf16[32,2304]{1,0:T(8,128)(2,1)S(1)}, bf16[32,2304]{1,0:T(8,128)(2,1)S(1)}, u32[]{:S(2)}, u32[]{:S(2)}) collective-permute-start(bf16[32,2304]{1,0:T(8,128)(2,1)S(1)} %dynamic-slice_bitcast_fusion.2), channel_id=1, source_target_pairs={{0,12},{4,8},{8,4},{12,0},{2,28},{6,24},{10,20},{14,16},{16,14},{2... | collective-permute-start | bytes 442376 | tf_op jit(solution)/shard_map/ppermute | solution.py:76
  6.7 8.0 %collective-permute-start = (bf16[32,2304]{1,0:T(8,128)(2,1)S(1)}, bf16[32,2304]{1,0:T(8,128)(2,1)S(1)}, u32[]{:S(2)}, u32[]{:S(2)}) collective-permute-start(bf16[32,2304]{1,0:T(8,128)(2,1)S(1)} %dynamic-slice_bitcast_fusion.2), channel_id=1, source_target_pairs={{0,4},{4,0},{8,12},{12,8},{2,20},{6,16},{10,28},{14,24},{16,6},{20... | collective-permute-start | bytes 442376 | tf_op jit(solution)/shard_map/ppermute | solution.py:77
  8.3 14.4 %collective-permute-start.6 = (bf16[16,384]{1,0:T(8,128)(2,1)}, bf16[16,384]{1,0:T(8,128)(2,1)S(1)}, u32[]{:S(2)}, u32[]{:S(2)}) collective-permute-start(bf16[16,384]{1,0:T(8,128)(2,1)} %get-tuple-element.11), channel_id=1, source_target_pairs={{0,1},{1,0},{2,3},{3,2},{4,5},{5,4},{6,7},{7,6},{8,9},{9,8},{10,11... | collective-permute-start | bytes 36872 | tf_op jit(solution)/shard_map/ppermute | solution.py:81
  12.0 6.9 %collective-permute-start.4 = (bf16[32,2304]{1,0:T(8,128)(2,1)S(1)}, bf16[32,2304]{1,0:T(8,128)(2,1)S(1)}, u32[]{:S(2)}, u32[]{:S(2)}) collective-permute-start(bf16[32,2304]{1,0:T(8,128)(2,1)S(1)} %collective-permute-done.1), channel_id=1, source_target_pairs={{0,4},{4,0},{8,12},{12,8},{1,5},{5,1},{9,13},{13,9},{2,6},{6,2},{1... | collective-permute-start | bytes 442376 | tf_op jit(solution)/shard_map/ppermute | solution.py:78
  14.7 8.0 %copy-start.1 = (bf16[16,384]{1,0:T(8,128)(2,1)S(1)}, bf16[16,384]{1,0:T(8,128)(2,1)}, u32[]{:S(2)}) copy-start(bf16[16,384]{1,0:T(8,128)(2,1)} %get-tuple-element.11) | copy-start | bytes 36868
  15.4 7.2 %collective-permute-start.3 = (f32[2,32,384]{2,1,0:T(8,128)S(1)}, f32[2,32,384]{2,1,0:T(8,128)S(1)}, u32[]{:S(2)}, u32[]{:S(2)}) collective-permute-start(f32[2,32,384]{2,1,0:T(8,128)S(1)} %pad_maximum_fusion), channel_id=1, source_target_pairs={{0,16},{16,0},{1,17},{17,1},{2,18},{18,2},{3,19},{19,3},{4,20},{20... | collective-permute-start | bytes 294920 | tf_op jit(solution)/shard_map/ppermute | solution.py:87
  18.8 6.4 %collective-permute-start.2 = (f32[1,32,384]{2,1,0:T(8,128)S(1)}, f32[1,32,384]{2,1,0:T(8,128)S(1)}, u32[]{:S(2)}, u32[]{:S(2)}) collective-permute-start(f32[1,32,384]{2,1,0:T(8,128)S(1)} %bitcast.88), channel_id=1, source_target_pairs={{0,2},{2,0},{1,3},{3,1},{4,6},{6,4},{5,7},{7,5},{8,10},{10,8},{9,1... | collective-permute-start | bytes 147464 | tf_op jit(solution)/shard_map/ppermute | solution.py:87
  19.5 5.7 %collective-permute-start.5 = (f32[1,32,384]{2,1,0:T(8,128)S(1)}, f32[1,32,384]{2,1,0:T(8,128)S(1)}, u32[]{:S(2)}, u32[]{:S(2)}) collective-permute-start(f32[1,32,384]{2,1,0:T(8,128)S(1)} %convolution_bitcast_fusion), channel_id=1, source_target_pairs={{0,16},{16,0},{1,17},{17,1},{2,18},{18,2},{3,19},{19,3},{4,20},{20... | collective-permute-start | bytes 147464 | tf_op jit(solution)/shard_map/ppermute | solution.py:87
  22.8 5.7 %collective-permute-start.7 = (f32[32,32]{1,0:T(8,128)S(1)}, f32[32,32]{1,0:T(8,128)S(1)}, u32[]{:S(2)}, u32[]{:S(2)}) collective-permute-start(f32[32,32]{1,0:T(8,128)S(1)} %bitcast.92), channel_id=1, source_target_pairs={{0,12},{4,8},{8,4},{12,0},{1,13},{5,9},{9,5},{13,1},{2,14},{6,10},... | collective-permute-start | bytes 12296 | tf_op jit(solution)/shard_map/ppermute | solution.py:108
  24.7 3.9 %collective-permute-start.8 = (f32[32,32]{1,0:T(8,128)S(1)}, f32[32,32]{1,0:T(8,128)S(1)}, u32[]{:S(2)}, u32[]{:S(2)}) collective-permute-start(f32[32,32]{1,0:T(8,128)S(1)} %bitcast.91), channel_id=1, source_target_pairs={{0,4},{4,0},{8,12},{12,8},{1,5},{5,1},{9,13},{13,9},{2,6},{6,2},{1... | collective-permute-start | bytes 12296 | tf_op jit(solution)/shard_map/ppermute | solution.py:108
  25.4 4.6 %collective-permute-start.9 = (f32[32,32]{1,0:T(8,128)S(1)}, f32[32,32]{1,0:T(8,128)S(1)}, u32[]{:S(2)}, u32[]{:S(2)}) collective-permute-start(f32[32,32]{1,0:T(8,128)S(1)} %bitcast.93), channel_id=1, source_target_pairs={{0,8},{4,12},{8,0},{12,4},{1,9},{5,13},{9,1},{13,5},{2,10},{6,14},... | collective-permute-start | bytes 12296 | tf_op jit(solution)/shard_map/ppermute | solution.py:109
  30.0 1.2 %collective-permute-start.10 = (f32[16,32]{1,0:T(8,128)S(1)}, f32[16,32]{1,0:T(8,128)S(1)}, u32[]{:S(2)}, u32[]{:S(2)}) collective-permute-start(f32[16,32]{1,0:T(8,128)S(1)} %get-tuple-element.25), channel_id=1, source_target_pairs={{0,1},{1,0},{2,3},{3,2},{4,5},{5,4},{6,7},{7,6},{8,9},{9,8},{10,11... | collective-permute-start | bytes 6152 | tf_op jit(solution)/shard_map/ppermute | solution.py:111

commit v8 on v7

--- a/solution.py
+++ b/solution.py
@@ -87,7 +87,7 @@
         sent = lax.ppermute(sent, axis, swap)
         if after is not None:
             sent, _ = lax.optimization_barrier((sent, after))
-        return jnp.where(live[0] > 0, part + sent, 0.0).astype(jnp.bfloat16)
+        return ((part + sent) * live[0]).astype(jnp.bfloat16)
 
     def terms(virtual):
         out = jnp.einsum("spr,kwr->kspw", weights, virtual, preferred_element_type=jnp.float32)
@@ -97,7 +97,7 @@
     own_slab = lax.optimization_barrier(lax.dynamic_slice(decoder[0, 0], (0, x * width), (rows, width)))
     halves = products(whole, own_slab)
     ours, theirs = jnp.where(x == 0, halves, halves[::-1])
-    early = jnp.concatenate([products(near[None], slab), products(far[None], slab)])
+    early = products(jnp.stack([near, far]), slab)
     ours, theirs, _ = lax.optimization_barrier((ours, theirs, early))
     own = swapped_sum(ours[None], theirs[None], "tgt")
     early = swapped_sum(early, early, "group", after=last)

time: 32.2 us -> 32.2 us (level)
  other arithmetic: 2.13 us -> 1.37 us
  local copies, waits for them, and re-layouts: 3.27 us -> 4 us
  matrix products: 2.88 us -> 2.33 us
  waiting for transfers between devices: 2.93 us -> 3.26 us
    gt x1 -> x0, other arithmetic: 0.73 us -> none  [swapped_sum(): return jnp.where(live[0] > 0, part + sent, 0.0).astype(jnp.bfloat16)]
    slice x0 -> x1, local copies, waits for them, and re-layouts: none -> 0.73 us  [swapped_sum(): return ((part + sent) * live[0]).astype(jnp.bfloat16)]
    dot_general x4 -> x3, matrix products: 2.5 us -> 1.95 us  [products(): jnp.einsum('kwd,rd->kwr', blocks, slab, preferred_element_type=jnp.float32)]
    ppermute x1, waiting for transfers between devices: 0.01 us -> 0.33 us  [square_mesh(): last = lax.ppermute(far, 'src', step(1))]
  transfers between devices with their start and end apart: 11 -> 11, of which waited for: 3 -> 4; matrix products, arithmetic and copies ran while one was open for 21% -> 19% of each run, Pallas kernels for 5% -> 5%
where the time goes in v8:
time: 32.2 us; the launch traced here: 31.9 us
  starting transfers between devices  18.6 us (58%)
  local copies, waits for them, and re-layouts  4 us (12%)
  waiting for transfers between devices  3.26 us (10%)
  matrix products  2.33 us (7%)
  Pallas kernels  1.52 us (5%)
  other arithmetic  1.37 us (4%)
  between operations  0.79 us (2%)
    ppermute x3, starting transfers between devices, swapped_sum(): sent = lax.ppermute(sent, axis, swap)  6.89 us
    ppermute x1, starting transfers between devices, square_mesh(): far = lax.ppermute(piece, AXES, swapped(step(3)))  5.11 us
    dynamic_slice x1, local copies, waits for them, and re-layouts, square_mesh(): lax.dynamic_slice(decoder[0, 0], (0, x * width), (rows, width))  2.24 us
    ppermute x1, starting transfers between devices, square_mesh(): last = lax.ppermute(far, 'src', step(1))  2.09 us
    ppermute x1, starting transfers between devices, square_mesh(): total = total + lax.ppermute(last_terms, 'src', step(2))  2.04 us
    dot_general x3, matrix products, products(): jnp.einsum('kwd,rd->kwr', blocks, slab, preferred_element_type=jnp.float32)  1.95 us
    ppermute x1, starting transfers between devices, square_mesh(): lax.ppermute(far_terms, 'src', step(3))  1.91 us
    pallas_call x1, Pallas kernels, masked(): pl.pallas_call(mask_kernel, out_shape=(jax.ShapeDtypeStruct((activations....  1.52 us
  transfers between devices with their start and end apart: 11, of which 4 were waited for; matrix products, arithmetic and copies ran while one was open for 19% of the time, Pallas kernels for 5%

profile of v8, /device:TPU:0, one launch (start us, length us, event | category | flops | bytes accessed | tf_op | source)
XLA Modules:
  0.0 31.9 jit_solution(14570738623144102297)
XLA Ops:
  0.6 0.0 copy-start
  0.7 0.9 %copy-done = bf16[1,1,64,2304]{3,2,1,0:T(8,128)(2,1)S(1)} copy-done((bf16[1,1,64,2304]{3,2,1,0:T(8,128)(2,1)S(1)}, bf16[1,1,64,2304]{3,2,1,0:T(8,128)(2,1)}, u32[]{:S(2)}) %copy-start) | copy-done | bytes 294936
  1.6 5.1 %collective-permute-start.1 = (bf16[32,2304]{1,0:T(8,128)(2,1)S(1)}, bf16[32,2304]{1,0:T(8,128)(2,1)S(1)}, u32[]{:S(2)}, u32[]{:S(2)}) collective-permute-start(bf16[32,2304]{1,0:T(8,128)(2,1)S(1)} %dynamic-slice_bitcast_fusion.2), channel_id=1, source_target_pairs={{0,12},{4,8},{8,4},{12,0},{2,28},{6,24},{10,20},{14,16},{16,14},{2... | collective-permute-start | bytes 442376 | tf_op jit(solution)/shard_map/ppermute | solution.py:76
  6.7 0.0 collective-permute-start
  6.7 1.5 %shard_map.68 = (bf16[16,384]{1,0:T(8,128)(2,1)}, f32[8,384]{1,0:T(8,128)}) custom-call(s32[4]{0:T(128)} %counts_ref.1, bf16[16,448]{1,0:T(8,128)(2,1)} %bitcast.89, s32[7,1,16]{2,1,0:T(1,128)} %bitcast.94), custom_call_target="tpu_custom_call" | custom-call | tf_op jit(solution)/shard_map/pallas_call | solution.py:32
  8.3 0.0 collective-permute-start.6
  8.3 2.2 %dynamic-slice_bitcast_fusion.1 = (bf16[384,2304]{1,0:T(8,128)(2,1)S(1)}, bf16[384,2304]{1,0:T(8,128)(2,1)S(1)}) fusion(bf16[1,1,448,4608]{3,2,1,0:T(8,128)(2,1)} %param.5, s32[]{:T(128)S(6)} %select_n.46, s32[]{:T(128)S(6)} %select_n.49), kind=kLoop, calls=%fused_computation.5 | loop fusion | bytes 7077896 | tf_op jit(solution)/shard_map/dynamic_slice | solution.py:97
  10.5 0.7 %fusion.4 = f32[2,32,384]{2,1,0:T(8,128)S(1)} fusion(bf16[2,32,2304]{2,1,0:T(8,128)(2,1)S(1)} %bitcast.78, bf16[384,2304]{1,0:T(8,128)(2,1)S(1)} %get-tuple-element.12), kind=kOutput, calls=%fused_computation.6 | convolution fusion | flops 113246208 | bytes 2162688 | tf_op jit(solution)/shard_map/kwd,rd->kwr/dot_general | solution.py:84
  11.2 0.7 %slice_reduce_fusion = f32[384]{0:T(512)S(1)} fusion(f32[8,384]{1,0:T(8,128)} %get-tuple-element.9), kind=kLoop, calls=%fused_computation.46 | loop fusion | bytes 3072 | tf_op jit(solution)/shard_map/slice | solution.py:90
  12.0 0.0 collective-permute-done.1
  12.0 2.1 %collective-permute-start.4 = (bf16[32,2304]{1,0:T(8,128)(2,1)S(1)}, bf16[32,2304]{1,0:T(8,128)(2,1)S(1)}, u32[]{:S(2)}, u32[]{:S(2)}) collective-permute-start(bf16[32,2304]{1,0:T(8,128)(2,1)S(1)} %collective-permute-done.1), channel_id=1, source_target_pairs={{0,4},{4,0},{8,12},{12,8},{1,5},{5,1},{9,13},{13,9},{2,6},{6,2},{1... | collective-permute-start | bytes 442376 | tf_op jit(solution)/shard_map/ppermute | solution.py:78
  14.1 0.0 collective-permute-done
  14.1 0.0 copy-start.1
  14.1 0.7 %fusion = f32[2,32,384]{2,1,0:T(8,128)S(1)} fusion(bf16[384,2304]{1,0:T(8,128)(2,1)S(1)} %get-tuple-element.13, bf16[1,32,2304]{2,1,0:T(8,128)(2,1)S(1)} %bitcast.79, bf16[1,32,2304]{2,1,0:T(8,128)(2,1)S(1)} %bitcast.80), kind=kOutput, calls=%fused_computation | convolution fusion | flops 113393664 | bytes 2162688 | tf_op jit(solution)/shard_map/kwd,rd->kwr/dot_general | solution.py:84
  14.7 3.5 %collective-permute-start.3 = (f32[2,32,384]{2,1,0:T(8,128)S(1)}, f32[2,32,384]{2,1,0:T(8,128)S(1)}, u32[]{:S(2)}, u32[]{:S(2)}) collective-permute-start(f32[2,32,384]{2,1,0:T(8,128)S(1)} %fusion), channel_id=1, source_target_pairs={{0,16},{16,0},{1,17},{17,1},{2,18},{18,2},{3,19},{19,3},{4,20},{20... | collective-permute-start | bytes 294920 | tf_op jit(solution)/shard_map/ppermute | solution.py:87
  18.2 0.1 collective-permute-start.2
  18.2 0.3 %collective-permute-done.4 = bf16[32,2304]{1,0:T(8,128)(2,1)S(1)} collective-permute-done((bf16[32,2304]{1,0:T(8,128)(2,1)S(1)}, bf16[32,2304]{1,0:T(8,128)(2,1)S(1)}, u32[]{:S(2)}, u32[]{:S(2)}) %collective-permute-start.4) | collective-permute-done | bytes 147488 | tf_op jit(solution)/shard_map/ppermute | solution.py:78
  18.6 0.6 %convolution_bitcast_fusion = f32[1,32,384]{2,1,0:T(8,128)S(1)} fusion(bf16[32,2304]{1,0:T(8,128)(2,1)S(1)} %collective-permute-done.4, bf16[384,2304]{1,0:T(8,128)(2,1)S(1)} %get-tuple-element.13), kind=kOutput, calls=%fused_computation.7 | convolution fusion | flops 56623104 | bytes 1966080 | tf_op jit(solution)/shard_map/kwd,rd->kwr/dot_general | solution.py:84
  19.2 3.4 %collective-permute-start.5 = (f32[1,32,384]{2,1,0:T(8,128)S(1)}, f32[1,32,384]{2,1,0:T(8,128)S(1)}, u32[]{:S(2)}, u32[]{:S(2)}) collective-permute-start(f32[1,32,384]{2,1,0:T(8,128)S(1)} %convolution_bitcast_fusion), channel_id=1, source_target_pairs={{0,16},{16,0},{1,17},{17,1},{2,18},{18,2},{3,19},{19,3},{4,20},{20... | collective-permute-start | bytes 147464 | tf_op jit(solution)/shard_map/ppermute | solution.py:87
  22.6 0.0 collective-permute-done.3
  22.6 0.0 collective-permute-done.6
  22.6 0.0 copy-done.1
  22.6 0.1 convolution_bitcast_fusion.1
  22.8 1.9 %collective-permute-start.7 = (f32[32,32]{1,0:T(8,128)S(1)}, f32[32,32]{1,0:T(8,128)S(1)}, u32[]{:S(2)}, u32[]{:S(2)}) collective-permute-start(f32[32,32]{1,0:T(8,128)S(1)} %bitcast.91), channel_id=1, source_target_pairs={{0,12},{4,8},{8,4},{12,0},{1,13},{5,9},{9,5},{13,1},{2,14},{6,10},... | collective-permute-start | bytes 12296 | tf_op jit(solution)/shard_map/ppermute | solution.py:108
  24.7 0.5 %collective-permute-start.8 = (f32[32,32]{1,0:T(8,128)S(1)}, f32[32,32]{1,0:T(8,128)S(1)}, u32[]{:S(2)}, u32[]{:S(2)}) collective-permute-start(f32[32,32]{1,0:T(8,128)S(1)} %bitcast.90), channel_id=1, source_target_pairs={{0,4},{4,0},{8,12},{12,8},{1,5},{5,1},{9,13},{13,9},{2,6},{6,2},{1... | collective-permute-start | bytes 12296 | tf_op jit(solution)/shard_map/ppermute | solution.py:108
  25.2 0.0 collective-permute-done.2
  25.2 0.0 collective-permute-done.5
  25.3 0.1 fusion.21
  25.4 2.0 %collective-permute-start.9 = (f32[32,32]{1,0:T(8,128)S(1)}, f32[32,32]{1,0:T(8,128)S(1)}, u32[]{:S(2)}, u32[]{:S(2)}) collective-permute-start(f32[32,32]{1,0:T(8,128)S(1)} %bitcast.92), channel_id=1, source_target_pairs={{0,8},{4,12},{8,0},{12,4},{1,9},{5,13},{9,1},{13,5},{2,10},{6,14},... | collective-permute-start | bytes 12296 | tf_op jit(solution)/shard_map/ppermute | solution.py:109
  27.4 0.1 fusion.24
  27.6 1.0 %collective-permute-done.7 = f32[32,32]{1,0:T(8,128)S(1)} collective-permute-done((f32[32,32]{1,0:T(8,128)S(1)}, f32[32,32]{1,0:T(8,128)S(1)}, u32[]{:S(2)}, u32[]{:S(2)}) %collective-permute-start.7) | collective-permute-done | bytes 4128 | tf_op jit(solution)/shard_map/ppermute | solution.py:108
  28.6 0.0 collective-permute-done.8
  28.6 1.4 %collective-permute-done.9 = f32[32,32]{1,0:T(8,128)S(1)} collective-permute-done((f32[32,32]{1,0:T(8,128)S(1)}, f32[32,32]{1,0:T(8,128)S(1)}, u32[]{:S(2)}, u32[]{:S(2)}) %collective-permute-start.9) | collective-permute-done | bytes 4128 | tf_op jit(solution)/shard_map/ppermute | solution.py:109
  30.0 0.1 collective-permute-start.10
  30.1 0.7 %fusion.17 = bf16[1,1,4,32,448]{4,3,2,1,0:T(8,128)(2,1)} fusion(bf16[1,32,384]{2,1,0:T(8,128)(2,1)S(1)} %get-tuple-element.15, bf16[1,32,384]{2,1,0:T(8,128)(2,1)S(1)} %get-tuple-element.16, bf16[1,32,384]{2,1,0:T(8,128)(2,1)S(1)} %get-tuple-element.17, bf16[1,32,384]{2,1,0:T(8,128)(2,1)S(1)} %get-tuple-element.14), kind=kLoop, calls=%fused_computation.22 | loop fusion | flops 745472 | bytes 212992 | tf_op jit(solution)/shard_map/broadcast_in_dim | solution.py:117
  30.8 0.5 %collective-permute-done.10 = f32[16,32]{1,0:T(8,128)S(1)} collective-permute-done((f32[16,32]{1,0:T(8,128)S(1)}, f32[16,32]{1,0:T(8,128)S(1)}, u32[]{:S(2)}, u32[]{:S(2)}) %collective-permute-start.10) | collective-permute-done | bytes 2080 | tf_op jit(solution)/shard_map/ppermute | solution.py:111
  31.3 0.6 %broadcast_select_fusion = f32[16,2,1,32]{3,2,1,0:T(1,128)} fusion(pred[]{:T(512)S(6)} %eq.7, f32[16,1,1,32]{3,2,1,0:T(1,128)S(1)} %bitcast.93, f32[16,1,1,32]{3,2,1,0:T(1,128)S(1)} %bitcast.88), kind=kLoop, calls=%fused_computation.32 | loop fusion | flops 3072 | bytes 8193 | tf_op jit(solution)/shard_map/jit(_where)/select_n | solution.py:113
  (11 shorter events, 0.1 us)
Async XLA Ops:
  0.6 1.0 %copy-start = (bf16[1,1,64,2304]{3,2,1,0:T(8,128)(2,1)S(1)}, bf16[1,1,64,2304]{3,2,1,0:T(8,128)(2,1)}, u32[]{:S(2)}) copy-start(bf16[1,1,64,2304]{3,2,1,0:T(8,128)(2,1)} %param.6) | copy-start | bytes 884740
  1.6 10.3 %collective-permute-start.1 = (bf16[32,2304]{1,0:T(8,128)(2,1)S(1)}, bf16[32,2304]{1,0:T(8,128)(2,1)S(1)}, u32[]{:S(2)}, u32[]{:S(2)}) collective-permute-start(bf16[32,2304]{1,0:T(8,128)(2,1)S(1)} %dynamic-slice_bitcast_fusion.2), channel_id=1, source_target_pairs={{0,12},{4,8},{8,4},{12,0},{2,28},{6,24},{10,20},{14,16},{16,14},{2... | collective-permute-start | bytes 442376 | tf_op jit(solution)/shard_map/ppermute | solution.py:76
  6.7 7.3 %collective-permute-start = (bf16[32,2304]{1,0:T(8,128)(2,1)S(1)}, bf16[32,2304]{1,0:T(8,128)(2,1)S(1)}, u32[]{:S(2)}, u32[]{:S(2)}) collective-permute-start(bf16[32,2304]{1,0:T(8,128)(2,1)S(1)} %dynamic-slice_bitcast_fusion.2), channel_id=1, source_target_pairs={{0,4},{4,0},{8,12},{12,8},{2,20},{6,16},{10,28},{14,24},{16,6},{20... | collective-permute-start | bytes 442376 | tf_op jit(solution)/shard_map/ppermute | solution.py:77
  8.3 14.4 %collective-permute-start.6 = (bf16[16,384]{1,0:T(8,128)(2,1)}, bf16[16,384]{1,0:T(8,128)(2,1)S(1)}, u32[]{:S(2)}, u32[]{:S(2)}) collective-permute-start(bf16[16,384]{1,0:T(8,128)(2,1)} %get-tuple-element.11), channel_id=1, source_target_pairs={{0,1},{1,0},{2,3},{3,2},{4,5},{5,4},{6,7},{7,6},{8,9},{9,8},{10,11... | collective-permute-start | bytes 36872 | tf_op jit(solution)/shard_map/ppermute | solution.py:81
  12.0 6.6 %collective-permute-start.4 = (bf16[32,2304]{1,0:T(8,128)(2,1)S(1)}, bf16[32,2304]{1,0:T(8,128)(2,1)S(1)}, u32[]{:S(2)}, u32[]{:S(2)}) collective-permute-start(bf16[32,2304]{1,0:T(8,128)(2,1)S(1)} %collective-permute-done.1), channel_id=1, source_target_pairs={{0,4},{4,0},{8,12},{12,8},{1,5},{5,1},{9,13},{13,9},{2,6},{6,2},{1... | collective-permute-start | bytes 442376 | tf_op jit(solution)/shard_map/ppermute | solution.py:78
  14.1 8.6 %copy-start.1 = (bf16[16,384]{1,0:T(8,128)(2,1)S(1)}, bf16[16,384]{1,0:T(8,128)(2,1)}, u32[]{:S(2)}) copy-start(bf16[16,384]{1,0:T(8,128)(2,1)} %get-tuple-element.11) | copy-start | bytes 36868
  14.7 7.8 %collective-permute-start.3 = (f32[2,32,384]{2,1,0:T(8,128)S(1)}, f32[2,32,384]{2,1,0:T(8,128)S(1)}, u32[]{:S(2)}, u32[]{:S(2)}) collective-permute-start(f32[2,32,384]{2,1,0:T(8,128)S(1)} %fusion), channel_id=1, source_target_pairs={{0,16},{16,0},{1,17},{17,1},{2,18},{18,2},{3,19},{19,3},{4,20},{20... | collective-permute-start | bytes 294920 | tf_op jit(solution)/shard_map/ppermute | solution.py:87
  18.2 7.0 %collective-permute-start.2 = (f32[1,32,384]{2,1,0:T(8,128)S(1)}, f32[1,32,384]{2,1,0:T(8,128)S(1)}, u32[]{:S(2)}, u32[]{:S(2)}) collective-permute-start(f32[1,32,384]{2,1,0:T(8,128)S(1)} %bitcast.87), channel_id=1, source_target_pairs={{0,2},{2,0},{1,3},{3,1},{4,6},{6,4},{5,7},{7,5},{8,10},{10,8},{9,1... | collective-permute-start | bytes 147464 | tf_op jit(solution)/shard_map/ppermute | solution.py:87
  19.2 6.0 %collective-permute-start.5 = (f32[1,32,384]{2,1,0:T(8,128)S(1)}, f32[1,32,384]{2,1,0:T(8,128)S(1)}, u32[]{:S(2)}, u32[]{:S(2)}) collective-permute-start(f32[1,32,384]{2,1,0:T(8,128)S(1)} %convolution_bitcast_fusion), channel_id=1, source_target_pairs={{0,16},{16,0},{1,17},{17,1},{2,18},{18,2},{3,19},{19,3},{4,20},{20... | collective-permute-start | bytes 147464 | tf_op jit(solution)/shard_map/ppermute | solution.py:87
  22.8 5.8 %collective-permute-start.7 = (f32[32,32]{1,0:T(8,128)S(1)}, f32[32,32]{1,0:T(8,128)S(1)}, u32[]{:S(2)}, u32[]{:S(2)}) collective-permute-start(f32[32,32]{1,0:T(8,128)S(1)} %bitcast.91), channel_id=1, source_target_pairs={{0,12},{4,8},{8,4},{12,0},{1,13},{5,9},{9,5},{13,1},{2,14},{6,10},... | collective-permute-start | bytes 12296 | tf_op jit(solution)/shard_map/ppermute | solution.py:108
  24.7 3.9 %collective-permute-start.8 = (f32[32,32]{1,0:T(8,128)S(1)}, f32[32,32]{1,0:T(8,128)S(1)}, u32[]{:S(2)}, u32[]{:S(2)}) collective-permute-start(f32[32,32]{1,0:T(8,128)S(1)} %bitcast.90), channel_id=1, source_target_pairs={{0,4},{4,0},{8,12},{12,8},{1,5},{5,1},{9,13},{13,9},{2,6},{6,2},{1... | collective-permute-start | bytes 12296 | tf_op jit(solution)/shard_map/ppermute | solution.py:108
  25.4 4.6 %collective-permute-start.9 = (f32[32,32]{1,0:T(8,128)S(1)}, f32[32,32]{1,0:T(8,128)S(1)}, u32[]{:S(2)}, u32[]{:S(2)}) collective-permute-start(f32[32,32]{1,0:T(8,128)S(1)} %bitcast.92), channel_id=1, source_target_pairs={{0,8},{4,12},{8,0},{12,4},{1,9},{5,13},{9,1},{13,5},{2,10},{6,14},... | collective-permute-start | bytes 12296 | tf_op jit(solution)/shard_map/ppermute | solution.py:109
  30.0 1.2 %collective-permute-start.10 = (f32[16,32]{1,0:T(8,128)S(1)}, f32[16,32]{1,0:T(8,128)S(1)}, u32[]{:S(2)}, u32[]{:S(2)}) collective-permute-start(f32[16,32]{1,0:T(8,128)S(1)} %get-tuple-element.25), channel_id=1, source_target_pairs={{0,1},{1,0},{2,3},{3,2},{4,5},{5,4},{6,7},{7,6},{8,9},{9,8},{10,11... | collective-permute-start | bytes 6152 | tf_op jit(solution)/shard_map/ppermute | solution.py:111

commit v9 on v8

--- a/solution.py
+++ b/solution.py
@@ -105,7 +105,7 @@
     late = products(last[None], slab)
     late = swapped_sum(late, late, "group")
     last_terms = terms(late)[0]
-    total = terms(own)[0] + lax.ppermute(far_terms, "src", step(3)) + lax.ppermute(near_terms, "src", step(1))
+    total = lax.ppermute(far_terms, "src", step(3)) + lax.ppermute(near_terms, "src", step(1)) + terms(own)[0]
     total = total + lax.ppermute(last_terms, "src", step(2))
     half = total.shape[0] // 2
     theirs = lax.ppermute(total[half:], "prompt", swap)

time: 32.2 us -> 32.2 us (level)
  no operation moved by 1% of the time
where the time goes in v9:
time: 32.2 us; the launch traced here: 31.9 us
  starting transfers between devices  18.6 us (58%)
  local copies, waits for them, and re-layouts  4 us (12%)
  waiting for transfers between devices  3.26 us (10%)
  matrix products  2.33 us (7%)
  Pallas kernels  1.52 us (5%)
  other arithmetic  1.37 us (4%)
  between operations  0.79 us (2%)
    ppermute x3, starting transfers between devices, swapped_sum(): sent = lax.ppermute(sent, axis, swap)  6.89 us
    ppermute x1, starting transfers between devices, square_mesh(): far = lax.ppermute(piece, AXES, swapped(step(3)))  5.11 us
    dynamic_slice x1, local copies, waits for them, and re-layouts, square_mesh(): lax.dynamic_slice(decoder[0, 0], (0, x * width), (rows, width))  2.24 us
    ppermute x1, starting transfers between devices, square_mesh(): last = lax.ppermute(far, 'src', step(1))  2.09 us
    ppermute x1, starting transfers between devices, square_mesh(): total = total + lax.ppermute(last_terms, 'src', step(2))  2.04 us
    dot_general x3, matrix products, products(): jnp.einsum('kwd,rd->kwr', blocks, slab, preferred_element_type=jnp.float32)  1.95 us
    ppermute x1, starting transfers between devices, square_mesh(): lax.ppermute(far_terms, 'src', step(3))  1.91 us
    pallas_call x1, Pallas kernels, masked(): pl.pallas_call(mask_kernel, out_shape=(jax.ShapeDtypeStruct((activations....  1.52 us
  transfers between devices with their start and end apart: 11, of which 4 were waited for; matrix products, arithmetic and copies ran while one was open for 19% of the time, Pallas kernels for 5%

profile of v9, /device:TPU:0, one launch (start us, length us, event | category | flops | bytes accessed | tf_op | source)
XLA Modules:
  0.0 31.9 jit_solution(13895883083015684391)
XLA Ops:
  0.6 0.0 copy-start
  0.7 0.9 %copy-done = bf16[1,1,64,2304]{3,2,1,0:T(8,128)(2,1)S(1)} copy-done((bf16[1,1,64,2304]{3,2,1,0:T(8,128)(2,1)S(1)}, bf16[1,1,64,2304]{3,2,1,0:T(8,128)(2,1)}, u32[]{:S(2)}) %copy-start) | copy-done | bytes 294936
  1.6 5.1 %collective-permute-start.1 = (bf16[32,2304]{1,0:T(8,128)(2,1)S(1)}, bf16[32,2304]{1,0:T(8,128)(2,1)S(1)}, u32[]{:S(2)}, u32[]{:S(2)}) collective-permute-start(bf16[32,2304]{1,0:T(8,128)(2,1)S(1)} %dynamic-slice_bitcast_fusion.2), channel_id=1, source_target_pairs={{0,12},{4,8},{8,4},{12,0},{2,28},{6,24},{10,20},{14,16},{16,14},{2... | collective-permute-start | bytes 442376 | tf_op jit(solution)/shard_map/ppermute | solution.py:76
  6.7 0.0 collective-permute-start
  6.7 1.5 %shard_map.68 = (bf16[16,384]{1,0:T(8,128)(2,1)}, f32[8,384]{1,0:T(8,128)}) custom-call(s32[4]{0:T(128)} %counts_ref.1, bf16[16,448]{1,0:T(8,128)(2,1)} %bitcast.87, s32[7,1,16]{2,1,0:T(1,128)} %bitcast.92), custom_call_target="tpu_custom_call" | custom-call | tf_op jit(solution)/shard_map/pallas_call | solution.py:32
  8.3 0.0 collective-permute-start.6
  8.3 2.2 %dynamic-slice_bitcast_fusion.1 = (bf16[384,2304]{1,0:T(8,128)(2,1)S(1)}, bf16[384,2304]{1,0:T(8,128)(2,1)S(1)}) fusion(bf16[1,1,448,4608]{3,2,1,0:T(8,128)(2,1)} %param.5, s32[]{:T(128)S(6)} %select_n.46, s32[]{:T(128)S(6)} %select_n.49), kind=kLoop, calls=%fused_computation.5 | loop fusion | bytes 7077896 | tf_op jit(solution)/shard_map/dynamic_slice | solution.py:97
  10.5 0.7 %fusion.4 = f32[2,32,384]{2,1,0:T(8,128)S(1)} fusion(bf16[2,32,2304]{2,1,0:T(8,128)(2,1)S(1)} %bitcast.76, bf16[384,2304]{1,0:T(8,128)(2,1)S(1)} %get-tuple-element.12), kind=kOutput, calls=%fused_computation.6 | convolution fusion | flops 113246208 | bytes 2162688 | tf_op jit(solution)/shard_map/kwd,rd->kwr/dot_general | solution.py:84
  11.2 0.7 %slice_reduce_fusion = f32[384]{0:T(512)S(1)} fusion(f32[8,384]{1,0:T(8,128)} %get-tuple-element.9), kind=kLoop, calls=%fused_computation.45 | loop fusion | bytes 3072 | tf_op jit(solution)/shard_map/slice | solution.py:90
  12.0 0.0 collective-permute-done.1
  12.0 2.1 %collective-permute-start.4 = (bf16[32,2304]{1,0:T(8,128)(2,1)S(1)}, bf16[32,2304]{1,0:T(8,128)(2,1)S(1)}, u32[]{:S(2)}, u32[]{:S(2)}) collective-permute-start(bf16[32,2304]{1,0:T(8,128)(2,1)S(1)} %collective-permute-done.1), channel_id=1, source_target_pairs={{0,4},{4,0},{8,12},{12,8},{1,5},{5,1},{9,13},{13,9},{2,6},{6,2},{1... | collective-permute-start | bytes 442376 | tf_op jit(solution)/shard_map/ppermute | solution.py:78
  14.1 0.0 collective-permute-done
  14.1 0.0 copy-start.1
  14.1 0.7 %fusion = f32[2,32,384]{2,1,0:T(8,128)S(1)} fusion(bf16[384,2304]{1,0:T(8,128)(2,1)S(1)} %get-tuple-element.13, bf16[1,32,2304]{2,1,0:T(8,128)(2,1)S(1)} %bitcast.77, bf16[1,32,2304]{2,1,0:T(8,128)(2,1)S(1)} %bitcast.78), kind=kOutput, calls=%fused_computation | convolution fusion | flops 113393664 | bytes 2162688 | tf_op jit(solution)/shard_map/kwd,rd->kwr/dot_general | solution.py:84
  14.7 3.5 %collective-permute-start.3 = (f32[2,32,384]{2,1,0:T(8,128)S(1)}, f32[2,32,384]{2,1,0:T(8,128)S(1)}, u32[]{:S(2)}, u32[]{:S(2)}) collective-permute-start(f32[2,32,384]{2,1,0:T(8,128)S(1)} %fusion), channel_id=1, source_target_pairs={{0,16},{16,0},{1,17},{17,1},{2,18},{18,2},{3,19},{19,3},{4,20},{20... | collective-permute-start | bytes 294920 | tf_op jit(solution)/shard_map/ppermute | solution.py:87
  18.2 0.1 collective-permute-start.2
  18.2 0.3 %collective-permute-done.4 = bf16[32,2304]{1,0:T(8,128)(2,1)S(1)} collective-permute-done((bf16[32,2304]{1,0:T(8,128)(2,1)S(1)}, bf16[32,2304]{1,0:T(8,128)(2,1)S(1)}, u32[]{:S(2)}, u32[]{:S(2)}) %collective-permute-start.4) | collective-permute-done | bytes 147488 | tf_op jit(solution)/shard_map/ppermute | solution.py:78
  18.6 0.6 %convolution_bitcast_fusion = f32[1,32,384]{2,1,0:T(8,128)S(1)} fusion(bf16[32,2304]{1,0:T(8,128)(2,1)S(1)} %collective-permute-done.4, bf16[384,2304]{1,0:T(8,128)(2,1)S(1)} %get-tuple-element.13), kind=kOutput, calls=%fused_computation.7 | convolution fusion | flops 56623104 | bytes 1966080 | tf_op jit(solution)/shard_map/kwd,rd->kwr/dot_general | solution.py:84
  19.2 3.4 %collective-permute-start.5 = (f32[1,32,384]{2,1,0:T(8,128)S(1)}, f32[1,32,384]{2,1,0:T(8,128)S(1)}, u32[]{:S(2)}, u32[]{:S(2)}) collective-permute-start(f32[1,32,384]{2,1,0:T(8,128)S(1)} %convolution_bitcast_fusion), channel_id=1, source_target_pairs={{0,16},{16,0},{1,17},{17,1},{2,18},{18,2},{3,19},{19,3},{4,20},{20... | collective-permute-start | bytes 147464 | tf_op jit(solution)/shard_map/ppermute | solution.py:87
  22.6 0.0 collective-permute-done.3
  22.6 0.0 collective-permute-done.6
  22.6 0.0 copy-done.1
  22.6 0.1 convolution_bitcast_fusion.1
  22.8 1.9 %collective-permute-start.7 = (f32[32,32]{1,0:T(8,128)S(1)}, f32[32,32]{1,0:T(8,128)S(1)}, u32[]{:S(2)}, u32[]{:S(2)}) collective-permute-start(f32[32,32]{1,0:T(8,128)S(1)} %bitcast.89), channel_id=1, source_target_pairs={{0,12},{4,8},{8,4},{12,0},{1,13},{5,9},{9,5},{13,1},{2,14},{6,10},... | collective-permute-start | bytes 12296 | tf_op jit(solution)/shard_map/ppermute | solution.py:108
  24.7 0.5 %collective-permute-start.8 = (f32[32,32]{1,0:T(8,128)S(1)}, f32[32,32]{1,0:T(8,128)S(1)}, u32[]{:S(2)}, u32[]{:S(2)}) collective-permute-start(f32[32,32]{1,0:T(8,128)S(1)} %bitcast.88), channel_id=1, source_target_pairs={{0,4},{4,0},{8,12},{12,8},{1,5},{5,1},{9,13},{13,9},{2,6},{6,2},{1... | collective-permute-start | bytes 12296 | tf_op jit(solution)/shard_map/ppermute | solution.py:108
  25.2 0.0 collective-permute-done.2
  25.2 0.0 collective-permute-done.5
  25.3 0.1 fusion.21
  25.4 2.0 %collective-permute-start.9 = (f32[32,32]{1,0:T(8,128)S(1)}, f32[32,32]{1,0:T(8,128)S(1)}, u32[]{:S(2)}, u32[]{:S(2)}) collective-permute-start(f32[32,32]{1,0:T(8,128)S(1)} %bitcast.90), channel_id=1, source_target_pairs={{0,8},{4,12},{8,0},{12,4},{1,9},{5,13},{9,1},{13,5},{2,10},{6,14},... | collective-permute-start | bytes 12296 | tf_op jit(solution)/shard_map/ppermute | solution.py:109
  27.4 0.1 fusion.23
  27.6 1.0 %collective-permute-done.7 = f32[32,32]{1,0:T(8,128)S(1)} collective-permute-done((f32[32,32]{1,0:T(8,128)S(1)}, f32[32,32]{1,0:T(8,128)S(1)}, u32[]{:S(2)}, u32[]{:S(2)}) %collective-permute-start.7) | collective-permute-done | bytes 4128 | tf_op jit(solution)/shard_map/ppermute | solution.py:108
  28.6 0.0 collective-permute-done.8
  28.6 1.4 %collective-permute-done.9 = f32[32,32]{1,0:T(8,128)S(1)} collective-permute-done((f32[32,32]{1,0:T(8,128)S(1)}, f32[32,32]{1,0:T(8,128)S(1)}, u32[]{:S(2)}, u32[]{:S(2)}) %collective-permute-start.9) | collective-permute-done | bytes 4128 | tf_op jit(solution)/shard_map/ppermute | solution.py:109
  30.0 0.1 collective-permute-start.10
  30.1 0.7 %fusion.17 = bf16[1,1,4,32,448]{4,3,2,1,0:T(8,128)(2,1)} fusion(bf16[1,32,384]{2,1,0:T(8,128)(2,1)S(1)} %get-tuple-element.15, bf16[1,32,384]{2,1,0:T(8,128)(2,1)S(1)} %get-tuple-element.16, bf16[1,32,384]{2,1,0:T(8,128)(2,1)S(1)} %get-tuple-element.17, bf16[1,32,384]{2,1,0:T(8,128)(2,1)S(1)} %get-tuple-element.14), kind=kLoop, calls=%fused_computation.22 | loop fusion | flops 745472 | bytes 212992 | tf_op jit(solution)/shard_map/broadcast_in_dim | solution.py:117
  30.8 0.5 %collective-permute-done.10 = f32[16,32]{1,0:T(8,128)S(1)} collective-permute-done((f32[16,32]{1,0:T(8,128)S(1)}, f32[16,32]{1,0:T(8,128)S(1)}, u32[]{:S(2)}, u32[]{:S(2)}) %collective-permute-start.10) | collective-permute-done | bytes 2080 | tf_op jit(solution)/shard_map/ppermute | solution.py:111
  31.3 0.6 %broadcast_select_fusion = f32[16,2,1,32]{3,2,1,0:T(1,128)} fusion(pred[]{:T(512)S(6)} %eq.7, f32[16,1,1,32]{3,2,1,0:T(1,128)S(1)} %bitcast.91, f32[16,1,1,32]{3,2,1,0:T(1,128)S(1)} %bitcast.86), kind=kLoop, calls=%fused_computation.32 | loop fusion | flops 3072 | bytes 8193 | tf_op jit(solution)/shard_map/jit(_where)/select_n | solution.py:113
  (11 shorter events, 0.2 us)
Async XLA Ops:
  0.6 1.0 %copy-start = (bf16[1,1,64,2304]{3,2,1,0:T(8,128)(2,1)S(1)}, bf16[1,1,64,2304]{3,2,1,0:T(8,128)(2,1)}, u32[]{:S(2)}) copy-start(bf16[1,1,64,2304]{3,2,1,0:T(8,128)(2,1)} %param.6) | copy-start | bytes 884740
  1.6 10.3 %collective-permute-start.1 = (bf16[32,2304]{1,0:T(8,128)(2,1)S(1)}, bf16[32,2304]{1,0:T(8,128)(2,1)S(1)}, u32[]{:S(2)}, u32[]{:S(2)}) collective-permute-start(bf16[32,2304]{1,0:T(8,128)(2,1)S(1)} %dynamic-slice_bitcast_fusion.2), channel_id=1, source_target_pairs={{0,12},{4,8},{8,4},{12,0},{2,28},{6,24},{10,20},{14,16},{16,14},{2... | collective-permute-start | bytes 442376 | tf_op jit(solution)/shard_map/ppermute | solution.py:76
  6.7 7.3 %collective-permute-start = (bf16[32,2304]{1,0:T(8,128)(2,1)S(1)}, bf16[32,2304]{1,0:T(8,128)(2,1)S(1)}, u32[]{:S(2)}, u32[]{:S(2)}) collective-permute-start(bf16[32,2304]{1,0:T(8,128)(2,1)S(1)} %dynamic-slice_bitcast_fusion.2), channel_id=1, source_target_pairs={{0,4},{4,0},{8,12},{12,8},{2,20},{6,16},{10,28},{14,24},{16,6},{20... | collective-permute-start | bytes 442376 | tf_op jit(solution)/shard_map/ppermute | solution.py:77
  8.3 14.4 %collective-permute-start.6 = (bf16[16,384]{1,0:T(8,128)(2,1)}, bf16[16,384]{1,0:T(8,128)(2,1)S(1)}, u32[]{:S(2)}, u32[]{:S(2)}) collective-permute-start(bf16[16,384]{1,0:T(8,128)(2,1)} %get-tuple-element.11), channel_id=1, source_target_pairs={{0,1},{1,0},{2,3},{3,2},{4,5},{5,4},{6,7},{7,6},{8,9},{9,8},{10,11... | collective-permute-start | bytes 36872 | tf_op jit(solution)/shard_map/ppermute | solution.py:81
  12.0 6.6 %collective-permute-start.4 = (bf16[32,2304]{1,0:T(8,128)(2,1)S(1)}, bf16[32,2304]{1,0:T(8,128)(2,1)S(1)}, u32[]{:S(2)}, u32[]{:S(2)}) collective-permute-start(bf16[32,2304]{1,0:T(8,128)(2,1)S(1)} %collective-permute-done.1), channel_id=1, source_target_pairs={{0,4},{4,0},{8,12},{12,8},{1,5},{5,1},{9,13},{13,9},{2,6},{6,2},{1... | collective-permute-start | bytes 442376 | tf_op jit(solution)/shard_map/ppermute | solution.py:78
  14.1 8.6 %copy-start.1 = (bf16[16,384]{1,0:T(8,128)(2,1)S(1)}, bf16[16,384]{1,0:T(8,128)(2,1)}, u32[]{:S(2)}) copy-start(bf16[16,384]{1,0:T(8,128)(2,1)} %get-tuple-element.11) | copy-start | bytes 36868
  14.7 7.8 %collective-permute-start.3 = (f32[2,32,384]{2,1,0:T(8,128)S(1)}, f32[2,32,384]{2,1,0:T(8,128)S(1)}, u32[]{:S(2)}, u32[]{:S(2)}) collective-permute-start(f32[2,32,384]{2,1,0:T(8,128)S(1)} %fusion), channel_id=1, source_target_pairs={{0,16},{16,0},{1,17},{17,1},{2,18},{18,2},{3,19},{19,3},{4,20},{20... | collective-permute-start | bytes 294920 | tf_op jit(solution)/shard_map/ppermute | solution.py:87
  18.2 7.0 %collective-permute-start.2 = (f32[1,32,384]{2,1,0:T(8,128)S(1)}, f32[1,32,384]{2,1,0:T(8,128)S(1)}, u32[]{:S(2)}, u32[]{:S(2)}) collective-permute-start(f32[1,32,384]{2,1,0:T(8,128)S(1)} %bitcast.85), channel_id=1, source_target_pairs={{0,2},{2,0},{1,3},{3,1},{4,6},{6,4},{5,7},{7,5},{8,10},{10,8},{9,1... | collective-permute-start | bytes 147464 | tf_op jit(solution)/shard_map/ppermute | solution.py:87
  19.2 6.0 %collective-permute-start.5 = (f32[1,32,384]{2,1,0:T(8,128)S(1)}, f32[1,32,384]{2,1,0:T(8,128)S(1)}, u32[]{:S(2)}, u32[]{:S(2)}) collective-permute-start(f32[1,32,384]{2,1,0:T(8,128)S(1)} %convolution_bitcast_fusion), channel_id=1, source_target_pairs={{0,16},{16,0},{1,17},{17,1},{2,18},{18,2},{3,19},{19,3},{4,20},{20... | collective-permute-start | bytes 147464 | tf_op jit(solution)/shard_map/ppermute | solution.py:87
  22.8 5.8 %collective-permute-start.7 = (f32[32,32]{1,0:T(8,128)S(1)}, f32[32,32]{1,0:T(8,128)S(1)}, u32[]{:S(2)}, u32[]{:S(2)}) collective-permute-start(f32[32,32]{1,0:T(8,128)S(1)} %bitcast.89), channel_id=1, source_target_pairs={{0,12},{4,8},{8,4},{12,0},{1,13},{5,9},{9,5},{13,1},{2,14},{6,10},... | collective-permute-start | bytes 12296 | tf_op jit(solution)/shard_map/ppermute | solution.py:108
  24.7 3.9 %collective-permute-start.8 = (f32[32,32]{1,0:T(8,128)S(1)}, f32[32,32]{1,0:T(8,128)S(1)}, u32[]{:S(2)}, u32[]{:S(2)}) collective-permute-start(f32[32,32]{1,0:T(8,128)S(1)} %bitcast.88), channel_id=1, source_target_pairs={{0,4},{4,0},{8,12},{12,8},{1,5},{5,1},{9,13},{13,9},{2,6},{6,2},{1... | collective-permute-start | bytes 12296 | tf_op jit(solution)/shard_map/ppermute | solution.py:108
  25.4 4.6 %collective-permute-start.9 = (f32[32,32]{1,0:T(8,128)S(1)}, f32[32,32]{1,0:T(8,128)S(1)}, u32[]{:S(2)}, u32[]{:S(2)}) collective-permute-start(f32[32,32]{1,0:T(8,128)S(1)} %bitcast.90), channel_id=1, source_target_pairs={{0,8},{4,12},{8,0},{12,4},{1,9},{5,13},{9,1},{13,5},{2,10},{6,14},... | collective-permute-start | bytes 12296 | tf_op jit(solution)/shard_map/ppermute | solution.py:109
  30.0 1.2 %collective-permute-start.10 = (f32[16,32]{1,0:T(8,128)S(1)}, f32[16,32]{1,0:T(8,128)S(1)}, u32[]{:S(2)}, u32[]{:S(2)}) collective-permute-start(f32[16,32]{1,0:T(8,128)S(1)} %get-tuple-element.25), channel_id=1, source_target_pairs={{0,1},{1,0},{2,3},{3,2},{4,5},{5,4},{6,7},{7,6},{8,9},{9,8},{10,11... | collective-permute-start | bytes 6152 | tf_op jit(solution)/shard_map/ppermute | solution.py:111
